TPU v7x, 512 devices: a whole 4x8x8 slice. The times are simulated.
512 devices in a mesh: ctx: 64 (over y, z_lo, x), ch: 8 (over z_hi, core).
Axes of the slice: x: 4, y: 8, z: 8 (z_hi: 4, z_lo: 2; z = z_hi * 2 + z_lo), core: 2. Of those that a mesh axis runs over, the one named last changes fastest.
Arguments:
- layer_input: bfloat16 [1280, 32768], P('ch', 'ctx'), may hold values from -6 to 6
- w_block: bfloat16 [512, 512], replicated, may hold values from -0.25 to 0.25
- w_cross: bfloat16 [64, 64], replicated, may hold values from -0.75 to 0.75
- ch_first: bfloat16 [8, 160, 160], P('ch'), may hold values from -0.5 to 0.5
- ch_second: bfloat16 [160, 8, 8], P('ch'), may hold values from -2 to 2
- gate_gain: float32 [1280], P('ch'), may hold values from 0.5 to 2
- gate_bias: float32 [1280], P('ch'), may hold values from -3 to 3
- cotangent: bfloat16 [1280, 32768], P('ch', 'ctx'), may hold values from -6 to 6
Outputs:
- output: bfloat16 [1280, 32768], P('ch', 'ctx')
- grad_input: bfloat16 [1280, 32768], P('ch', 'ctx')
- grad_block: float32 [512, 512], replicated
- grad_cross: float32 [64, 64], replicated
- grad_first: float32 [8, 160, 160], P('ch')
- grad_second: float32 [160, 8, 8], P('ch')
- grad_gain: float32 [1280], P('ch')
- grad_bias: float32 [1280], P('ch')
All inputs are finite; a program needn't handle non-finite values.
Results may differ from a plain program's by a relative error of at most 0.007.
Values may be sent and summed in bfloat16 or wider, within the bound.
No kernel may reach another device: no remote copies, remote signals or barrier semaphores. Data moves between devices by JAX's collectives and lax.ppermute only.
A program may use at most 64 MiB of HBM per device.

v0:
```python
import jax
import jax.numpy as jnp
from jax import lax
from jax.sharding import PartitionSpec as P


def on_device(layer_input, w_block, w_cross, ch_first, ch_second, gate_gain, gate_bias, cotangent):
    chan_rows, tokens_here = layer_input.shape
    tile_arrangement = w_block.shape[0]
    local_blocks = tokens_here // tile_arrangement
    groups = ch_first.shape[0]
    group_width = ch_first.shape[1]
    ctx_count = lax.axis_size("ctx")
    col_width = tile_arrangement // ctx_count
    transverse_arrangement = local_blocks * ctx_count
    input_blocks = layer_input.reshape(chan_rows, local_blocks, tile_arrangement)
    first_rows = jnp.einsum(
        "cij,jk->cik", input_blocks, w_block, preferred_element_type=jnp.float32
    ).astype(jnp.bfloat16)
    first_sent = lax.all_to_all(
        first_rows.reshape(chan_rows, local_blocks, ctx_count, col_width),
        "ctx",
        split_axis=2,
        concat_axis=1,
        tiled=True,
    )
    first_cols = first_sent.reshape(chan_rows, transverse_arrangement, col_width)
    mixed_cols = jnp.einsum(
        "cij,il->clj", first_cols, w_cross, preferred_element_type=jnp.float32
    ).astype(jnp.bfloat16)
    returned_output = lax.all_to_all(
        mixed_cols.reshape(chan_rows, ctx_count, local_blocks, col_width),
        "ctx",
        split_axis=1,
        concat_axis=3,
        tiled=True,
    )
    mixed_seq = returned_output.reshape(chan_rows, tokens_here)
    input_full = layer_input.astype(jnp.float32)
    gate_value = jax.nn.sigmoid(input_full * gate_gain[:, None] + gate_bias[:, None])
    hidden = (input_full + gate_value * mixed_seq.astype(jnp.float32)).astype(jnp.bfloat16)
    hidden_grouped = hidden.reshape(groups, group_width, tokens_here)
    pre_act = jnp.einsum(
        "gkm,gmn->gkn", ch_first, hidden_grouped, preferred_element_type=jnp.float32
    )
    activated = jax.nn.gelu(pre_act).astype(jnp.bfloat16)
    cot_grouped = cotangent.reshape(groups, group_width, tokens_here)
    act_cols = lax.all_to_all(activated, "ch", split_axis=1, concat_axis=0, tiled=True)
    branch_cols = jnp.einsum(
        "kgh,hkn->gkn", ch_second, act_cols, preferred_element_type=jnp.float32
    ).astype(jnp.bfloat16)
    path_choice_flag = lax.all_to_all(branch_cols, "ch", split_axis=0, concat_axis=1, tiled=True)
    cot_cols = lax.all_to_all(cot_grouped, "ch", split_axis=1, concat_axis=0, tiled=True)
    nonlinear_column_derivs = jnp.einsum(
        "kgh,gkn->hkn", ch_second, cot_cols, preferred_element_type=jnp.float32
    ).astype(jnp.bfloat16)
    grad_second_part = jnp.einsum(
        "gkn,hkn->kgh", cot_cols, act_cols, preferred_element_type=jnp.float32
    )
    d_act = lax.all_to_all(nonlinear_column_derivs, "ch", split_axis=0, concat_axis=1, tiled=True)
    output = (
        (hidden_grouped.astype(jnp.float32) + path_choice_flag.astype(jnp.float32))
        .astype(jnp.bfloat16)
        .reshape(chan_rows, tokens_here)
    )
    gelu_pull = jax.vjp(jax.nn.gelu, pre_act)[1]
    d_pre = gelu_pull(d_act.astype(jnp.float32))[0].astype(jnp.bfloat16)
    grad_first_part = jnp.einsum(
        "gkn,gmn->gkm", d_pre, hidden_grouped, preferred_element_type=jnp.float32
    )
    d_hidden = cot_grouped.astype(jnp.float32) + jnp.einsum(
        "gkm,gkn->gmn", ch_first, d_pre, preferred_element_type=jnp.float32
    )
    d_hidden = d_hidden.reshape(chan_rows, tokens_here)
    d_mixed = (d_hidden * gate_value).astype(jnp.bfloat16)
    d_gate = d_hidden * mixed_seq.astype(jnp.float32) * gate_value * (1.0 - gate_value)
    gain_part = jnp.sum(d_gate * input_full, axis=1)
    bias_part = jnp.sum(d_gate, axis=1)
    d_mixed_sent = lax.all_to_all(
        d_mixed.reshape(chan_rows, local_blocks, ctx_count, col_width),
        "ctx",
        split_axis=2,
        concat_axis=1,
        tiled=True,
    )
    d_mixed_cols = d_mixed_sent.reshape(chan_rows, transverse_arrangement, col_width)
    d_first_cols = jnp.einsum(
        "clj,il->cij", d_mixed_cols, w_cross, preferred_element_type=jnp.float32
    ).astype(jnp.bfloat16)
    transverse_share = jnp.einsum(
        "cij,clj->il", first_cols, d_mixed_cols, preferred_element_type=jnp.float32
    )
    d_first_back = lax.all_to_all(
        d_first_cols.reshape(chan_rows, ctx_count, local_blocks, col_width),
        "ctx",
        split_axis=1,
        concat_axis=3,
        tiled=True,
    )
    leading_matrix_deriv = d_first_back.reshape(chan_rows, local_blocks, tile_arrangement)
    block_part = jnp.einsum(
        "cij,cik->jk", input_blocks, leading_matrix_deriv, preferred_element_type=jnp.float32
    )
    d_input = jnp.einsum(
        "cik,jk->cij", leading_matrix_deriv, w_block, preferred_element_type=jnp.float32
    )
    grad_input = (
        d_hidden + d_gate * gate_gain[:, None] + d_input.reshape(chan_rows, tokens_here)
    ).astype(jnp.bfloat16)
    grad_first, grad_second, grad_gain, grad_bias = lax.psum(
        (grad_first_part, grad_second_part, gain_part, bias_part), "ctx"
    )
    grad_block, grad_cross = lax.psum((block_part, transverse_share), ("ctx", "ch"))
    return (
        output,
        grad_input,
        grad_block,
        grad_cross,
        grad_first,
        grad_second,
        grad_gain,
        grad_bias,
    )


def solution(mesh):
    in_specs = (
        P("ch", "ctx"),
        P(),
        P(),
        P("ch", None, None),
        P("ch", None, None),
        P("ch"),
        P("ch"),
        P("ch", "ctx"),
    )
    out_specs = (
        P("ch", "ctx"),
        P("ch", "ctx"),
        P(),
        P(),
        P("ch", None, None),
        P("ch", None, None),
        P("ch"),
        P("ch"),
    )
    return jax.shard_map(
        on_device, mesh=mesh, in_specs=in_specs, out_specs=out_specs, check_vma=False
    )
```

profile of v0, /device:TPU:22, one launch (start us, length us, event | category | flops | bytes accessed | tf_op | source)
XLA Modules:
  0.0 944.6 jit_solution(6243286589830568353)
XLA Ops:
  7.2 1.2 copy.121
  8.9 1.6 reduce.4
  10.5 0.7 reshape.163
  11.3 10.4 %all-to-all-start.4 = ((bf16[8,2,5120]{2,1,0:T(2,128)(2,1)}), bf16[8,2,5120]{2,1,0:T(2,128)(2,1)S(1)}, u32[]{:S(2)}, u32[]{:S(2)}) async-start(bf16[8,2,5120]{2,1,0:T(2,128)(2,1)} %reshape.163), calls=%async_computation.4 | async-start | bytes 327680 | tf_op jit(solution)/shard_map/all_to_all | solution.py:53
  22.1 0.8 copy.68
  23.0 9.4 all-to-all-done.4
  32.4 10.6 %all-to-all-start = ((bf16[160,1,64,8]{0,3,1,2:T(8,128)(2,1)}), bf16[160,1,64,8]{0,3,1,2:T(8,128)(2,1)S(1)}, u32[]{:S(2)}, u32[]{:S(2)}) async-start(bf16[160,1,64,8]{0,3,1,2:T(8,128)(2,1)} %bitcast.1), calls=%async_computation | async-start | bytes 524288 | tf_op jit(solution)/shard_map/all_to_all | solution.py:20
  43.1 0.9 bitcast_reduce_fusion
  45.0 7.8 all-to-all-done
  52.8 3.4 all-to-all-start.5
  56.5 0.9 copy.72
  57.3 9.9 %all-to-all-done.5 = bf16[8,20,512]{2,1,0:T(8,128)(2,1)S(1)} async-done(((bf16[8,20,512]{2,1,0:T(8,128)(2,1)}), bf16[8,20,512]{2,1,0:T(8,128)(2,1)S(1)}, u32[]{:S(2)}, u32[]{:S(2)}) %all-to-all-start.5) | async-done | bytes 163872 | tf_op jit(solution)/shard_map/all_to_all | solution.py:60
  67.2 8.0 all-to-all-start.1
  75.3 8.8 all-to-all-done.1
  87.3 16.8 %all_to_all.38 = bf16[160,1,64,8]{0,3,1,2:T(8,128)(2,1)S(1)} all-to-all(bf16[160,1,64,8]{0,3,1,2:T(8,128)(2,1)S(1)} %bitcast.92), channel_id=1, replica_groups=mesh['ctx'=64,'ch'=8] {'ctx'}, dimensions={2} | all-to-all | bytes 327680 | tf_op jit(solution)/shard_map/all_to_all | solution.py:79
  104.4 16.0 %all_to_all.39 = bf16[160,64,1,8]{0,3,2,1:T(8,128)(2,1)S(1)} all-to-all(bf16[160,64,1,8]{0,3,2,1:T(8,128)(2,1)S(1)} %copy.86), channel_id=1, replica_groups=mesh['ctx'=64,'ch'=8] {'ctx'}, dimensions={1} | all-to-all | bytes 327680 | tf_op jit(solution)/shard_map/all_to_all | solution.py:93
  120.4 1.2 convolution_bitcast_fusion
  121.9 1.6 reduce.5
  123.5 0.7 reshape.161
  124.3 4.1 all-to-all-start.2
  128.6 0.9 convolution_bitcast_fusion.3
  129.5 9.5 %all-to-all-done.2 = bf16[8,2,5120]{2,1,0:T(2,128)(2,1)S(1)} async-done(((bf16[8,2,5120]{2,1,0:T(2,128)(2,1)}), bf16[8,2,5120]{2,1,0:T(2,128)(2,1)S(1)}, u32[]{:S(2)}, u32[]{:S(2)}) %all-to-all-start.2) | async-done | bytes 163872 | tf_op jit(solution)/shard_map/all_to_all | solution.py:48
  139.1 0.9 bitcast_reduce_fusion.1
  140.3 0.7 copy.77
  141.0 3.4 all-to-all-start.3
  144.7 280.4 %all-reduce = (f32[20,8,8]{1,2,0:T(8,128)S(1)}, f32[160]{0:T(256)}, f32[160]{0:T(256)}) all-reduce(f32[20,8,8]{1,2,0:T(8,128)S(1)} %convolution_bitcast_fusion.4, f32[160]{0:T(256)S(1)} %get-tuple-element.41, f32[160]{0:T(256)S(1)} %get-tuple-element.40), channel_id=1, replica_groups=mesh['ctx'=64,'ch'=8] {'ctx'}, use_global_device_ids=true, to_apply=%region_3.0 | all-reduce | flops 1600 | bytes 12800 | tf_op jit(solution)/shard_map/psum | solution.py:110
  425.0 0.7 copy.90
  426.0 120.0 %psum.43 = f32[64,64]{1,0:T(8,128)} all-reduce(f32[64,64]{1,0:T(8,128)S(1)} %convolution_bitcast_fusion.5), channel_id=1, replica_groups=mesh['ctx'=64,'ch'=8] {'ctx','ch'}, use_global_device_ids=true, to_apply=%region_1.0 | all-reduce | flops 4096 | bytes 32768 | tf_op jit(solution)/shard_map/psum | solution.py:113
  546.8 1.0 fusion.3
  547.8 2.5 copy.89
  550.3 385.9 %all-reduce.6.cloned.1.call-done = f32[1,160,160]{2,1,0:T(8,128)} async-done(((f32[1,160,160]{2,1,0:T(8,128)}), f32[1,160,160]{2,1,0:T(8,128)}) %all-reduce.6.cloned.1.call-update) | async-done | bytes 102416 | tf_op jit(solution)/shard_map/psum | solution.py:110
  936.2 1.6 copy.125
  (47 shorter events, 7.9 us)
Async XLA Ops:
  7.2 14.7 %copy-start = (bf16[512,512]{1,0:T(8,128)(2,1)S(1)}, bf16[512,512]{1,0:T(8,128)(2,1)}, u32[]{:S(2)}) copy-start(bf16[512,512]{1,0:T(8,128)(2,1)} %param.9) | copy-start | bytes 1572868
  11.3 10.4 %copy-start.4 = (bf16[20,8,8]{0,2,1:T(8,128)(2,1)S(1)}, bf16[20,8,8]{0,2,1:T(8,128)(2,1)}, u32[]{:S(2)}) copy-start(bf16[20,8,8]{0,2,1:T(8,128)(2,1)} %param.12) | copy-start | bytes 7684
  11.3 10.6 %copy-start.1 = (bf16[160,512]{1,0:T(8,128)(2,1)S(1)}, bf16[160,512]{1,0:T(8,128)(2,1)}, u32[]{:S(2)}) copy-start(bf16[160,512]{1,0:T(8,128)(2,1)} %param.8) | copy-start | bytes 491524
  11.3 21.1 %all-to-all-start.4 = ((bf16[8,2,5120]{2,1,0:T(2,128)(2,1)}), bf16[8,2,5120]{2,1,0:T(2,128)(2,1)S(1)}, u32[]{:S(2)}, u32[]{:S(2)}) async-start(bf16[8,2,5120]{2,1,0:T(2,128)(2,1)} %reshape.163), calls=%async_computation.4 | async-start | bytes 327680 | tf_op jit(solution)/shard_map/all_to_all | solution.py:53
  32.4 20.4 %all-to-all-start = ((bf16[160,1,64,8]{0,3,1,2:T(8,128)(2,1)}), bf16[160,1,64,8]{0,3,1,2:T(8,128)(2,1)S(1)}, u32[]{:S(2)}, u32[]{:S(2)}) async-start(bf16[160,1,64,8]{0,3,1,2:T(8,128)(2,1)} %bitcast.1), calls=%async_computation | async-start | bytes 524288 | tf_op jit(solution)/shard_map/all_to_all | solution.py:20
  45.0 11.2 %copy-start.3 = (bf16[64,64]{1,0:T(8,128)(2,1)S(1)}, bf16[64,64]{1,0:T(8,128)(2,1)}, u32[]{:S(2)}) copy-start(bf16[64,64]{1,0:T(8,128)(2,1)} %param.10) | copy-start | bytes 24580
  52.8 14.4 %all-to-all-start.5 = ((bf16[8,20,512]{2,1,0:T(8,128)(2,1)}), bf16[8,20,512]{2,1,0:T(8,128)(2,1)S(1)}, u32[]{:S(2)}, u32[]{:S(2)}) async-start(bf16[8,20,512]{2,1,0:T(8,128)(2,1)} %copy.81), calls=%async_computation.5 | async-start | bytes 393216 | tf_op jit(solution)/shard_map/all_to_all | solution.py:60
  67.2 16.9 %all-to-all-start.1 = ((bf16[160,64,1,8]{0,3,2,1:T(8,128)(2,1)}), bf16[160,64,1,8]{0,3,2,1:T(8,128)(2,1)S(1)}, u32[]{:S(2)}, u32[]{:S(2)}) async-start(bf16[160,64,1,8]{0,3,2,1:T(8,128)(2,1)} %copy.72), calls=%async_computation.1 | async-start | bytes 524288 | tf_op jit(solution)/shard_map/all_to_all | solution.py:31
  75.2 472.6 %all-reduce.4.cloned.1.call-start = ((), (), s32[]{:S(2)}) async-start(), calls=%async_computation.8 | async-start | bytes 2097152 | tf_op jit(solution)/shard_map/psum | solution.py:113
  84.1 0.7 copy-start.5
  84.2 0.7 copy-start.6
  84.8 0.9 copy-start.7
  85.7 0.9 copy-start.2
  124.3 14.7 %all-to-all-start.2 = ((bf16[8,2,5120]{2,1,0:T(2,128)(2,1)}), bf16[8,2,5120]{2,1,0:T(2,128)(2,1)S(1)}, u32[]{:S(2)}, u32[]{:S(2)}) async-start(bf16[8,2,5120]{2,1,0:T(2,128)(2,1)} %reshape.161), calls=%async_computation.2 | async-start | bytes 327680 | tf_op jit(solution)/shard_map/all_to_all | solution.py:48
  128.3 807.9 %all-reduce.6.cloned.1.call-start = ((), (), s32[]{:S(2)}) async-start(), calls=%async_computation.9 | async-start | bytes 327680 | tf_op jit(solution)/shard_map/psum | solution.py:110
  141.0 405.0 %all-to-all-start.3 = ((bf16[8,20,512]{2,1,0:T(8,128)(2,1)}), bf16[8,20,512]{2,1,0:T(8,128)(2,1)S(1)}, u32[]{:S(2)}, u32[]{:S(2)}) async-start(bf16[8,20,512]{2,1,0:T(8,128)(2,1)} %copy.77), calls=%async_computation.3 | async-start | bytes 393216 | tf_op jit(solution)/shard_map/all_to_all | solution.py:52
Sparse Core Ops, SparseCore 0:
  121.8 270.5 all-reduce.3
  395.5 540.6 all-reduce.5
where the time goes:
time: 946 us; the launch traced here: 945 us
  blocking collectives  433 us (46%)
  waiting for transfers between devices  431 us (46%)
  starting transfers between devices  40.2 us (4%)
  local copies, waits for them, and re-layouts  16 us (2%)
  between operations  14.3 us (2%)
    psum x1, waiting for transfers between devices, on_device(): lax.psum((grad_first_part, grad_second_part, gain_part, bias_part), 'ctx')  386 us
    psum x1, blocking collectives, on_device(): lax.psum((grad_first_part, grad_second_part, gain_part, bias_part), 'ctx')  280 us
    psum x1, blocking collectives, on_device(): lax.psum((block_part, transverse_share), ('ctx', 'ch'))  120 us
  transfers between devices with their start and end apart: 8, of which 6 were waited for; matrix products, arithmetic and copies ran while one was open for 2% of the time, Pallas kernels for 0%

commit v1 on v0

v1 whole, which is shorter than its diff:
```python
import functools

import jax
import jax.numpy as jnp
from jax import lax
from jax.experimental import pallas as pl
from jax.experimental.pallas import tpu as pltpu
from jax.sharding import PartitionSpec as P

BF = jnp.bfloat16
F32 = jnp.float32
NB = 64
BLK = 512
CB = 8
CS = 160
KCH = 20
W = 256
HALF = 128
TOK = 64


def dot(a, b, dims=((1,), (0,))):
    return lax.dot_general(a, b, (dims, ((), ())), preferred_element_type=F32)


NN = ((1,), (0,))
NT = ((1,), (1,))
TN = ((0,), (0,))


def iota(shape, axis):
    return lax.broadcasted_iota(jnp.int32, shape, axis)


def ones_where(cond):
    return jnp.where(cond, 1.0, 0.0).astype(BF)


def lanes_of(x):
    groups = x.shape[0] // 8
    left = x[:, :HALF].reshape(groups, 8, HALF)
    right = x[:, HALF:].reshape(groups, 8, HALF)
    return left, right


def call(body, out_shapes, *args, scratch=(), smem=()):
    specs = [
        pl.BlockSpec(memory_space=pltpu.SMEM if at in smem else pltpu.VMEM)
        for at in range(len(args))
    ]
    return pl.pallas_call(
        body,
        out_shape=[jax.ShapeDtypeStruct(s, d) for s, d in out_shapes],
        in_specs=specs,
        out_specs=[pl.BlockSpec(memory_space=pltpu.VMEM) for _ in out_shapes],
        scratch_shapes=list(scratch),
        compiler_params=pltpu.CompilerParams(vmem_limit_bytes=48 * 1024 * 1024),
    )(*args)


def prepare(x_ref, cot_ref, second_ref, first_ref, gain_ref, bias_ref, cross_ref,
            xt_ref, cott_ref, weight_ref, scale_ref, kron_ref, kront_ref, pad_ref):
    zeros = jnp.zeros((W - CS, BLK), F32)
    xt = jnp.concatenate([x_ref[...].astype(F32), zeros], axis=0).T
    xt_ref[...] = xt.reshape(NB, 8, W).astype(BF)
    cott = jnp.concatenate([cot_ref[...].astype(F32), zeros], axis=0).T
    place = ones_where(iota((KCH, W), 1) == iota((KCH, W), 0) + CS)
    factor = dot(second_ref[...], place, TN)
    cott_ref[...] = (cott.reshape(CB, TOK, W) + factor[None]).astype(BF)
    pad_ref[...] = jnp.zeros((W, W), F32)
    pad_ref[:CS, :CS] = first_ref[0].astype(F32)
    weight_ref[...] = pad_ref[...].astype(BF)
    scale_ref[...] = jnp.zeros((8, W), F32)
    scale_ref[0:1, :CS] = gain_ref[...]
    scale_ref[1:2, :CS] = bias_ref[...]
    spread = ones_where(iota((BLK, NB), 0) // 8 == iota((BLK, NB), 1))
    same = iota((BLK, BLK), 0) % 8 == iota((BLK, BLK), 1) % 8
    half = dot(spread, cross_ref[...], NN).astype(BF)
    kron_ref[...] = jnp.where(same, dot(half, spread, NT), 0.0).astype(BF)
    half = dot(spread, cross_ref[...], NT).astype(BF)
    kront_ref[...] = jnp.where(same, dot(half, spread, NT), 0.0).astype(BF)


def cross_forward(kront_ref, cols_ref, out_ref):
    cols = cols_ref[...].astype(F32).reshape(BLK, W).astype(BF)
    out_ref[...] = dot(kront_ref[...], cols).reshape(NB, 8, W).astype(BF)


def channel_forward(u_ref, block_ref, xt_ref, scale_ref, weight_ref, cot_ref,
                    send_ref, mixed_ref, gate_ref, hidden_ref, slope_ref, second_ref):
    u = u_ref[...].astype(F32).reshape(BLK, W).astype(BF)
    mixed = dot(block_ref[...], u, TN).astype(BF)
    mixed_ref[...] = mixed
    xt = xt_ref[...].astype(F32).reshape(BLK, W)
    gate = jax.nn.sigmoid(xt * scale_ref[0:1, :] + scale_ref[1:2, :])
    gate_ref[...] = gate
    hidden = (xt + gate * mixed.astype(F32)).astype(BF)
    hidden_ref[...] = hidden
    pre = dot(hidden, weight_ref[...], NT)
    root = 0.7978845608028654
    square = pre * pre
    curve = jnp.tanh(root * (pre + 0.044715 * (square * pre)))
    act = pre * (0.5 * (1.0 + curve))
    slope_ref[...] = 0.5 * (1.0 + curve) + pre * (0.5 * (1.0 - curve * curve)) * (
        root * (1.0 + (3 * 0.044715) * square)
    )
    send_ref[:, :TOK, :] = act.astype(BF).reshape(CB, TOK, W)
    second = jnp.zeros((TOK, W), F32)
    for g in range(CB):
        pick = (iota((W, W), 0) >= CS) & (iota((W, W), 1) == iota((W, W), 0) - CS + KCH * g)
        pick = pick & (iota((W, W), 0) < CS + KCH)
        second = second + dot(cot_ref[g], ones_where(pick))
    second_ref[...] = second
    inside = iota((TOK, W), 1) < CS
    for g2 in range(CB):
        total = jnp.zeros((TOK, W), F32)
        for g in range(CB):
            total = total + second[g * CB + g2][None, :] * cot_ref[g].astype(F32)
        send_ref[g2, TOK:, :] = jnp.where(inside, total, 0.0).astype(BF)


def channel_backward(recv_ref, cot_ref, cott_ref, second_ref, mixed_ref, gate_ref, hidden_ref,
                     slope_ref, weight_ref, xt_ref, scale_ref, block_ref, u_ref,
                     send_ref, branch_ref, rest_ref, misc_ref):
    second = second_ref[...]
    for g in range(CB):
        total = jnp.zeros((TOK, W), F32)
        for g2 in range(CB):
            total = total + second[g * CB + g2][None, :] * recv_ref[g2, :TOK, :].astype(F32)
        branch_ref[g] = total.astype(BF)
    misc_ref[...] = jnp.zeros(misc_ref.shape, F32)
    for g in range(CB):
        cot = cot_ref[g].astype(F32)
        for g2 in range(CB):
            row = 320 + g * CB + g2
            misc_ref[row:row + 1, :] = jnp.sum(
                cot * recv_ref[g2, :TOK, :].astype(F32), axis=0, keepdims=True
            )
    d_act = recv_ref[:, TOK:, :].reshape(BLK, W).astype(F32)
    d_pre = (d_act * slope_ref[...]).astype(BF)
    hidden = hidden_ref[...]
    grad_first = dot(d_pre, hidden, TN)
    misc_ref[0:CS, :] = grad_first[:CS]
    inside = iota((BLK, W), 1) < CS
    cot = jnp.where(inside, cott_ref[...].reshape(BLK, W).astype(F32), 0.0)
    d_hidden = cot + dot(d_pre, weight_ref[...], NN)
    gate = gate_ref[...]
    d_mixed = (d_hidden * gate).astype(BF)
    d_gate = d_hidden * mixed_ref[...].astype(F32) * gate * (1.0 - gate)
    xt = xt_ref[...].astype(F32).reshape(BLK, W)
    misc_ref[448:449, :] = jnp.sum(d_gate * xt, axis=0, keepdims=True)
    misc_ref[449:450, :] = jnp.sum(d_gate, axis=0, keepdims=True)
    rest_ref[...] = d_hidden + d_gate * scale_ref[0:1, :]
    v = dot(block_ref[...], d_mixed, NN)
    u = u_ref[...].astype(F32).reshape(BLK, W).astype(BF)
    at = iota((CS, HALF), 1)

    def packed(x):
        keep = at[: x.shape[0]]
        left, right = x[:, :HALF], x[:, HALF:]
        first = jnp.where(keep >= 32, left, 0.0)
        moved = jnp.where(keep < 64, pltpu.roll(left, 32, 1), pltpu.roll(right, 64, 1))
        second = jnp.where((keep >= 32) & (keep < 96), moved, 0.0)
        return first, second

    first_a, first_b = packed(misc_ref[0:CS, :])
    second_a, second_b = packed(misc_ref[320:384, :])
    scale_a, scale_b = packed(misc_ref[448:456, :])
    misc = jnp.concatenate(
        [first_a, first_b, second_a, second_b, scale_a, scale_b, jnp.zeros((48, HALF), F32)], axis=0
    )
    left = v[:, :HALF].reshape(NB, 8, HALF)
    right = (jnp.where(iota((BLK, HALF), 1) < 32, v[:, HALF:], misc)).reshape(NB, 8, HALF)
    send_ref[:, 0:16, :] = jnp.concatenate([left, right], axis=1).astype(BF)
    d_block = dot(u, d_mixed, NT)
    parts = [d_block[:, HALF * s:HALF * (s + 1)].reshape(NB, 8, HALF) for s in range(4)]
    send_ref[:, 16:48, :] = jnp.concatenate(parts, axis=1).astype(BF)


def cross_backward(recv_ref, x_ref, kron_ref, branch_ref, send_ref, d_input_ref, misc_ref):
    head = recv_ref[:, 0:16, :].astype(F32)
    low = iota((NB, 8, HALF), 2) < 32
    left, right = head[:, 0:8, :], head[:, 8:16, :]
    v = jnp.concatenate(
        [left.reshape(BLK, HALF), jnp.where(low, right, 0.0).reshape(BLK, HALF)], axis=1
    ).astype(BF)
    misc_ref[...] = jnp.sum(right, axis=0)
    d_input_ref[...] = dot(kron_ref[...], v).astype(BF)
    x = x_ref[...].astype(F32).reshape(BLK, W).astype(BF)
    pairs = dot(x, v, NT)
    same = iota((BLK, BLK), 0) % 8 == iota((BLK, BLK), 1) % 8
    rows = jnp.sum(jnp.where(same, pairs, 0.0).reshape(NB, 8, BLK), axis=1)
    gather = ones_where(iota((BLK, HALF), 0) // 8 == iota((BLK, HALF), 1) - 64)
    high = rows.astype(BF)
    cross = dot(high, gather) + dot((rows - high.astype(F32)).astype(BF), gather)
    tail = jnp.sum(recv_ref[:, 16:48, :].astype(F32), axis=0)
    extra = jnp.concatenate([tail, misc_ref[...], jnp.zeros((8, HALF), F32)], axis=0).astype(BF)
    lane = iota((TOK, HALF), 1)
    for g in range(CB):
        branch = branch_ref[g].astype(F32)
        send_ref[g, 0:64, :] = branch[:, :HALF].astype(BF)
        send_ref[g, 64:128, :] = jnp.where(lane < 32, branch[:, HALF:], cross).astype(BF)
        send_ref[g, 128:176, :] = extra


def finish_output(recv_ref, hidden_ref, d_input_ref, misc_ref, flag_ref, out_ref, send_ref):
    low = iota((CB, TOK, HALF), 2) < 32
    right = recv_ref[:, 64:128, :].astype(F32)
    left = recv_ref[:, 0:64, :].astype(F32)
    branch = jnp.concatenate(
        [left.reshape(BLK, HALF), jnp.where(low, right, 0.0).reshape(BLK, HALF)], axis=1
    )
    total = hidden_ref[...].astype(F32) + branch
    out_ref[...] = total.T[:CS].astype(BF)
    cross = jnp.sum(right, axis=0)
    lane = iota((32, HALF), 1)
    cross = jnp.where(lane < 64, pltpu.roll(cross[0:32], 64, 1), cross[32:64])
    block = jnp.sum(recv_ref[:, 128:160, :].astype(F32), axis=0)
    summed = jnp.sum(recv_ref[:, 160:176, :].astype(F32), axis=0)[0:8]
    misc = jnp.where(flag_ref[0] > 0, summed, misc_ref[...])
    d_input = d_input_ref[...].astype(F32)
    left = d_input[:, :HALF].reshape(NB, 8, HALF)
    right = jnp.where(
        iota((NB, 8, HALF), 2) < 32, d_input[:, HALF:].reshape(NB, 8, HALF), misc[None]
    )
    send_ref[:, 0:16, :] = jnp.concatenate([left, right], axis=1).astype(BF)
    tail = jnp.concatenate([block, cross], axis=0).astype(BF)
    send_ref[:, 16:80, :] = jnp.broadcast_to(tail[None], (NB, 64, HALF))


def finish(recv_ref, rest_ref, flag_ref, grad_ref, block_ref, cross_ref, first_ref, second_ref,
           gain_ref, bias_ref):
    head = recv_ref[:, 0:16, :].astype(F32)
    left, right = head[:, 0:8, :], head[:, 8:16, :].reshape(BLK, HALF)
    low = iota((BLK, HALF), 1) < 32
    d_input = jnp.concatenate([left.reshape(BLK, HALF), jnp.where(low, right, 0.0)], axis=1)
    grad_ref[...] = (rest_ref[...] + d_input).T[:CS].astype(BF)
    block = recv_ref[:, 16:48, :].astype(F32)
    for s in range(4):
        block_ref[:, HALF * s:HALF * (s + 1)] = block[:, 8 * s:8 * s + 8, :].reshape(BLK, HALF)
    cross = jnp.sum(recv_ref[:, 48:80, :].astype(F32), axis=0)
    cross_ref[0:32, :] = cross[:, 0:64]
    cross_ref[32:64, :] = pltpu.roll(cross, 64, 1)[:, 0:64]
    misc = right

    def unpacked(start, rows):
        a, b = misc[start:start + rows], misc[start + rows:start + 2 * rows]
        keep = iota((rows, HALF), 1)
        left = jnp.where(keep >= 32, a, pltpu.roll(b, 96, 1))
        return left, pltpu.roll(b, 64, 1)

    left, right = unpacked(0, CS)
    first_ref[0, :, 0:HALF] = left
    first_ref[0, :, HALF:CS] = right[:, 0:32]
    left, right = unpacked(320, 64)
    own = flag_ref[1] * KCH
    pick_left = ones_where(iota((KCH, HALF), 1) == iota((KCH, HALF), 0) + own)
    pick_right = ones_where(iota((KCH, HALF), 1) + HALF == iota((KCH, HALF), 0) + own)
    pick_right = jnp.where(iota((KCH, HALF), 1) < 32, pick_right, 0.0).astype(BF)
    second_ref[...] = dot(pick_left, left.astype(BF), NT) + dot(pick_right, right.astype(BF), NT)
    left, right = unpacked(448, 8)
    gain_ref[:, 0:HALF] = left[0:1]
    gain_ref[:, HALF:CS] = right[0:1, 0:32]
    bias_ref[:, 0:HALF] = left[1:2]
    bias_ref[:, HALF:CS] = right[1:2, 0:32]


def on_device(layer_input, w_block, w_cross, ch_first, ch_second, gate_gain, gate_bias, cotangent):
    swap = functools.partial(lax.all_to_all, split_axis=0, concat_axis=0, tiled=True)
    ctx, ch = lax.axis_index("ctx"), lax.axis_index("ch")
    flag = jnp.stack([((ctx >= 40) & (ctx < 56)).astype(jnp.int32), ch.astype(jnp.int32)])
    xt, cott, weight, scale, kron, kront = call(
        prepare,
        [((NB, 8, W), BF), ((CB, TOK, W), BF), ((W, W), BF), ((8, W), F32),
         ((BLK, BLK), BF), ((BLK, BLK), BF)],
        layer_input, cotangent, ch_second.reshape(KCH, CB * CB), ch_first,
        gate_gain.reshape(1, CS), gate_bias.reshape(1, CS), w_cross,
        scratch=[pltpu.VMEM((W, W), F32)],
    )
    x_cols = swap(xt, "ctx")
    cot_cols = swap(cott, "ch")
    (u_cols,) = call(cross_forward, [((NB, 8, W), BF)], kront, x_cols)
    u = swap(u_cols, "ctx")
    send, mixed, gate, hidden, slope, second = call(
        channel_forward,
        [((CB, 2 * TOK, W), BF), ((BLK, W), BF), ((BLK, W), F32), ((BLK, W), BF), ((BLK, W), F32),
         ((TOK, W), F32)],
        u, w_block, xt, scale, weight, cot_cols,
    )
    recv = swap(send, "ch")
    send, branch, rest = call(
        channel_backward,
        [((NB, 48, HALF), BF), ((CB, TOK, W), BF), ((BLK, W), F32)],
        recv, cot_cols, cott, second, mixed, gate, hidden, slope, weight, xt, scale, w_block, u,
        scratch=[pltpu.VMEM((456, W), F32)],
    )
    recv = swap(send, "ctx")
    send, d_input, misc = call(
        cross_backward,
        [((CB, 176, HALF), BF), ((BLK, W), BF), ((8, HALF), F32)],
        recv, x_cols, kron, branch,
    )
    recv = swap(send, "ch")
    output, send = call(
        finish_output,
        [((CS, BLK), BF), ((NB, 80, HALF), BF)],
        recv, hidden, d_input, misc, flag,
        smem=(4,),
    )
    recv = swap(send, "ctx")
    grad_input, grad_block, grad_cross, grad_first, grad_second, grad_gain, grad_bias = call(
        finish,
        [((CS, BLK), BF), ((BLK, BLK), F32), ((NB, NB), F32), ((1, CS, CS), F32),
         ((KCH, CB * CB), F32), ((1, CS), F32), ((1, CS), F32)],
        recv, rest, flag,
        smem=(2,),
    )
    return (
        output,
        grad_input,
        grad_block,
        grad_cross,
        grad_first,
        grad_second.reshape(KCH, CB, CB),
        grad_gain.reshape(CS),
        grad_bias.reshape(CS),
    )


def solution(mesh):
    in_specs = (
        P("ch", "ctx"),
        P(),
        P(),
        P("ch", None, None),
        P("ch", None, None),
        P("ch"),
        P("ch"),
        P("ch", "ctx"),
    )
    out_specs = (
        P("ch", "ctx"),
        P("ch", "ctx"),
        P(),
        P(),
        P("ch", None, None),
        P("ch", None, None),
        P("ch"),
        P("ch"),
    )
    return jax.shard_map(
        on_device, mesh=mesh, in_specs=in_specs, out_specs=out_specs, check_vma=False
    )
```

time: 946 us -> 186 us (0.20)
  the two profiles are of different devices: /device:TPU:22 before, /device:TPU:1 now
where the time goes in v1:
time: 186 us; the launch traced here: 183 us
  blocking collectives  126 us (68%)
  waiting for transfers between devices  21 us (11%)
  starting transfers between devices  18.8 us (10%)
  Pallas kernels  9.85 us (5%)
  local copies, waits for them, and re-layouts  6.31 us (3%)
    all_to_all x2, blocking collectives, on_device(): recv = swap(send, 'ctx')  65.9 us
    all_to_all x1, blocking collectives, on_device(): x_cols = swap(xt, 'ctx')  24 us
    all_to_all x1, blocking collectives, on_device(): recv = swap(send, 'ch')  20.4 us
    all_to_all x1, blocking collectives, on_device(): u = swap(u_cols, 'ctx')  15.8 us
    all_to_all x1, starting transfers between devices, on_device(): cot_cols = swap(cott, 'ch')  12.4 us
    all_to_all x1, waiting for transfers between devices, on_device(): recv = swap(send, 'ch')  11.3 us
    pallas_call x7, Pallas kernels, call(): pl.pallas_call(body, out_shape=[jax.ShapeDtypeStruct(s, d) for s, d in ou...  9.85 us
    all_to_all x1, waiting for transfers between devices, on_device(): cot_cols = swap(cott, 'ch')  9.73 us
  transfers between devices with their start and end apart: 2, of which 2 were waited for; matrix products, arithmetic and copies ran while one was open for 0% of the time, Pallas kernels for 0%

profile of v1, /device:TPU:1, one launch (start us, length us, event | category | flops | bytes accessed | tf_op | source)
XLA Modules:
  0.0 182.8 jit_solution(7780529657031503812)
XLA Ops:
  0.6 0.8 copy.18.second_ref
  1.4 0.0 copy-start.1
  1.4 0.9 copy-done.1
  2.4 0.0 copy-start.2
  2.4 0.9 copy-done.2
  3.3 0.0 copy-start.3
  3.3 0.9 copy-done.3
  4.2 0.0 copy-start.4
  4.2 0.7 copy-done.4
  4.9 0.0 copy-start.5
  4.9 0.7 copy-done.5
  5.6 0.0 copy-start.6
  5.6 0.7 copy-done.6
  6.2 1.0 shard_map.143
  7.2 24.0 %all_to_all.35.cols_ref.x_ref = bf16[64,8,256]{2,1,0:T(8,128)(2,1)S(1)} all-to-all(bf16[64,8,256]{2,1,0:T(8,128)(2,1)S(1)} %get-tuple-element.36.xt_ref), channel_id=1, replica_groups=mesh['ctx'=64,'ch'=8] {'ctx'}, dimensions={0} | all-to-all | bytes 524288 | tf_op jit(solution)/shard_map/all_to_all | solution.py:280
  31.2 12.4 %all-to-all-start.2 = ((bf16[8,64,256]{2,1,0:T(8,128)(2,1)}), bf16[8,64,256]{2,1,0:T(8,128)(2,1)S(1)}, u32[]{:S(2)}, u32[]{:S(2)}) async-start(bf16[8,64,256]{2,1,0:T(8,128)(2,1)} %get-tuple-element.39.cott_ref), calls=%async_computation.2 | async-start | bytes 524288 | tf_op jit(solution)/shard_map/all_to_all | solution.py:281
  43.6 0.3 shard_map.144
  43.9 9.7 %all-to-all-done.2.cot_ref = bf16[8,64,256]{2,1,0:T(8,128)(2,1)S(1)} async-done(((bf16[8,64,256]{2,1,0:T(8,128)(2,1)}), bf16[8,64,256]{2,1,0:T(8,128)(2,1)S(1)}, u32[]{:S(2)}, u32[]{:S(2)}) %all-to-all-start.2) | async-done | bytes 262176 | tf_op jit(solution)/shard_map/all_to_all | solution.py:281
  53.6 15.8 %all_to_all.36.u_ref = bf16[64,8,256]{2,1,0:T(8,128)(2,1)S(1)} all-to-all(bf16[64,8,256]{2,1,0:T(8,128)(2,1)S(1)} %shard_map.144), channel_id=1, replica_groups=mesh['ctx'=64,'ch'=8] {'ctx'}, dimensions={0} | all-to-all | bytes 524288 | tf_op jit(solution)/shard_map/all_to_all | solution.py:283
  69.4 0.0 copy-done
  69.4 1.3 shard_map.145
  70.7 20.4 %all_to_all.37.recv_ref = bf16[8,128,256]{2,1,0:T(8,128)(2,1)S(1)} all-to-all(bf16[8,128,256]{2,1,0:T(8,128)(2,1)S(1)} %get-tuple-element.40), channel_id=1, replica_groups=mesh['ctx'=64,'ch'=8] {'ch'}, dimensions={0} | all-to-all | bytes 1048576 | tf_op jit(solution)/shard_map/all_to_all | solution.py:290
  91.2 2.3 %shard_map.146 = (bf16[64,48,128]{2,1,0:T(8,128)(2,1)S(1)}, bf16[8,64,256]{2,1,0:T(8,128)(2,1)S(1)}, f32[512,256]{1,0:T(8,128)S(1)}) custom-call(bf16[8,128,256]{2,1,0:T(8,128)(2,1)S(1)} %all_to_all.37.recv_ref, bf16[8,64,256]{2,1,0:T(8,128)(2,1)S(1)} %all-to-all-done.2.cot_ref, bf16[8,64,256]{2,1,0:T(8,128)(2,1)} %get-tuple-element.39.cott_ref, ...), custom_call_target="tpu_custom_call" | custom-call | tf_op jit(solution)/shard_map/pallas_call | solution.py:51
  93.5 28.5 %all_to_all.38.recv_ref = bf16[64,48,128]{2,1,0:T(8,128)(2,1)S(1)} all-to-all(bf16[64,48,128]{2,1,0:T(8,128)(2,1)S(1)} %get-tuple-element.46), channel_id=1, replica_groups=mesh['ctx'=64,'ch'=8] {'ctx'}, dimensions={0} | all-to-all | bytes 1572864 | tf_op jit(solution)/shard_map/all_to_all | solution.py:297
  122.0 1.8 shard_map.147
  123.8 6.4 %all-to-all-start.5 = ((bf16[8,176,128]{2,1,0:T(8,128)(2,1)}), bf16[8,176,128]{2,1,0:T(8,128)(2,1)S(1)}, u32[]{:S(2)}, u32[]{:S(2)}) async-start(bf16[8,176,128]{2,1,0:T(8,128)(2,1)} %get-tuple-element.49), calls=%async_computation.5 | async-start | bytes 720896 | tf_op jit(solution)/shard_map/all_to_all | solution.py:303
  130.1 0.1 pad_add_fusion.flag_ref
  130.2 11.3 %all-to-all-done.5.recv_ref = bf16[8,176,128]{2,1,0:T(8,128)(2,1)S(1)} async-done(((bf16[8,176,128]{2,1,0:T(8,128)(2,1)}), bf16[8,176,128]{2,1,0:T(8,128)(2,1)S(1)}, u32[]{:S(2)}, u32[]{:S(2)}) %all-to-all-start.5) | async-done | bytes 360480 | tf_op jit(solution)/shard_map/all_to_all | solution.py:303
  141.5 1.4 shard_map.148
  142.8 37.4 %all_to_all.39.recv_ref = bf16[64,80,128]{2,1,0:T(8,128)(2,1)S(1)} all-to-all(bf16[64,80,128]{2,1,0:T(8,128)(2,1)S(1)} %get-tuple-element.53), channel_id=1, replica_groups=mesh['ctx'=64,'ch'=8] {'ctx'}, dimensions={0} | all-to-all | bytes 2621440 | tf_op jit(solution)/shard_map/all_to_all | solution.py:310
  180.2 1.8 %shard_map.149 = (bf16[160,512]{1,0:T(8,128)(2,1)}, f32[512,512]{1,0:T(8,128)}, f32[64,64]{1,0:T(8,128)}, f32[1,160,160]{2,1,0:T(8,128)}, f32[20,64]{1,0:T(8,128...) custom-call(bf16[64,80,128]{2,1,0:T(8,128)(2,1)S(1)} %all_to_all.39.recv_ref, f32[512,256]{1,0:T(8,128)S(1)} %get-tuple-element.54.rest_ref, ...), custom_call_target="tpu_custom_call" | custom-call | tf_op jit(solution)/shard_map/pallas_call | solution.py:51
  182.1 0.7 copy.19
  (1 shorter events, 0.0 us)
Async XLA Ops:
  1.4 0.9 copy-start.1
  2.4 0.9 copy-start.2
  3.3 0.9 copy-start.3
  4.2 0.7 copy-start.4
  4.9 0.7 copy-start.5
  5.6 0.7 copy-start.6
  7.2 62.2 %copy-start = (bf16[512,512]{1,0:T(8,128)(2,1)S(1)}, bf16[512,512]{1,0:T(8,128)(2,1)}, u32[]{:S(2)}) copy-start(bf16[512,512]{1,0:T(8,128)(2,1)} %block_ref.3) | copy-start | bytes 1572868
  31.2 22.4 %all-to-all-start.2 = ((bf16[8,64,256]{2,1,0:T(8,128)(2,1)}), bf16[8,64,256]{2,1,0:T(8,128)(2,1)S(1)}, u32[]{:S(2)}, u32[]{:S(2)}) async-start(bf16[8,64,256]{2,1,0:T(8,128)(2,1)} %get-tuple-element.39.cott_ref), calls=%async_computation.2 | async-start | bytes 524288 | tf_op jit(solution)/shard_map/all_to_all | solution.py:281
  123.8 17.7 %all-to-all-start.5 = ((bf16[8,176,128]{2,1,0:T(8,128)(2,1)}), bf16[8,176,128]{2,1,0:T(8,128)(2,1)S(1)}, u32[]{:S(2)}, u32[]{:S(2)}) async-start(bf16[8,176,128]{2,1,0:T(8,128)(2,1)} %get-tuple-element.49), calls=%async_computation.5 | async-start | bytes 720896 | tf_op jit(solution)/shard_map/all_to_all | solution.py:303

commit v2 on v0

v2 whole, which is shorter than its diff:
```python
import functools

import jax
import jax.numpy as jnp
from jax import lax
from jax.experimental import pallas as pl
from jax.experimental.pallas import tpu as pltpu
from jax.sharding import PartitionSpec as P

BF = jnp.bfloat16
F32 = jnp.float32
NB = 64
BLK = 512
CB = 8
CS = 160
KCH = 20
W = 256
HALF = 128


def dot(a, b, dims=((1,), (0,))):
    return lax.dot_general(a, b, (dims, ((), ())), preferred_element_type=F32)


NN = ((1,), (0,))
NT = ((1,), (1,))
TN = ((0,), (0,))


def iota(shape, axis):
    return lax.broadcasted_iota(jnp.int32, shape, axis)


def ones_where(cond):
    return jnp.where(cond, 1.0, 0.0).astype(BF)


def call(body, out_shapes, *args, scratch=(), smem=(), after=()):
    specs = [
        pl.BlockSpec(memory_space=pltpu.SMEM if at in smem else pltpu.VMEM)
        for at in range(len(args))
    ]
    specs += [pl.BlockSpec(memory_space=pl.ANY) for _ in after]
    used, held = len(args), len(args) + len(after)

    def run(*refs):
        body(*refs[:used], *refs[held:])

    return pl.pallas_call(
        run,
        out_shape=[jax.ShapeDtypeStruct(s, d) for s, d in out_shapes],
        in_specs=specs,
        out_specs=[pl.BlockSpec(memory_space=pltpu.VMEM) for _ in out_shapes],
        scratch_shapes=list(scratch),
        compiler_params=pltpu.CompilerParams(vmem_limit_bytes=48 * 1024 * 1024),
    )(*args, *after)


def group_of(rank, flag_ref):
    return ((flag_ref[1] - rank % 4) & 3) * 2 + ((rank // 4) ^ flag_ref[2])


def transpose_input(x_ref, xt_ref):
    zeros = jnp.zeros((W - CS, BLK), F32)
    xt = jnp.concatenate([x_ref[...].astype(F32), zeros], axis=0).T
    xt_ref[...] = xt.reshape(NB, 8, W).astype(BF)


def pack_cotangent(cot_ref, second_ref, out_ref, pad_ref):
    out_ref[0:CS, :] = cot_ref[...]
    pad_ref[...] = jnp.zeros(pad_ref.shape, F32)
    pad_ref[0:KCH, 0:64] = second_ref[...].astype(F32)
    more = jnp.concatenate([pltpu.roll(pad_ref[16:24, :], 64, 1), jnp.zeros((8, HALF), F32)], axis=0)
    tile = (pad_ref[0:16, :] + more).astype(BF)
    out_ref[CS:CS + 16, :] = jnp.concatenate([tile] * 4, axis=1)


def prepare(gain_ref, bias_ref, cross_ref, gain_out_ref, bias_out_ref, kron_ref, kront_ref, pad_ref):
    for row, out_ref in ((gain_ref, gain_out_ref), (bias_ref, bias_out_ref)):
        pad_ref[...] = jnp.zeros(pad_ref.shape, F32)
        pad_ref[:, 0:CS] = jnp.broadcast_to(row[...], (HALF, CS))
        out_ref[...] = pad_ref[...].T[:CS]
    spread = ones_where(iota((BLK, NB), 0) // 8 == iota((BLK, NB), 1))
    same = iota((BLK, BLK), 0) % 8 == iota((BLK, BLK), 1) % 8
    half = dot(spread, cross_ref[...], NN).astype(BF)
    kron_ref[...] = jnp.where(same, dot(half, spread, NT), 0.0).astype(BF)
    half = dot(spread, cross_ref[...], NT).astype(BF)
    kront_ref[...] = jnp.where(same, dot(half, spread, NT), 0.0).astype(BF)


def cross_forward(kront_ref, cols_ref, out_ref):
    cols = cols_ref[...].astype(F32).reshape(BLK, W).astype(BF)
    out_ref[...] = dot(kront_ref[...], cols).reshape(NB, 8, W).astype(BF)


def channel(u_ref, block_ref, x_ref, gain_ref, bias_ref, weight_ref, side_ref, other_ref,
            flag_ref, send_ref, act_ref, hidden_ref, rest_ref, factor_ref):
    cots = [ref.at[s] for ref in (side_ref, other_ref) for s in range(4)]
    q = flag_ref[0]
    u = u_ref[...].astype(F32).reshape(BLK, W).astype(BF)
    mixed = dot(u, block_ref[...], TN)[:CS].astype(BF).astype(F32)
    x = x_ref[...].astype(F32)
    gain = jnp.concatenate([gain_ref[...]] * 4, axis=1)
    bias = jnp.concatenate([bias_ref[...]] * 4, axis=1)
    gate = jax.nn.sigmoid(x * gain + bias)
    hidden = (x + gate * mixed).astype(BF)
    hidden_ref[...] = hidden
    weight = weight_ref[0]
    pre = dot(weight, hidden)
    root = 0.7978845608028654
    square = pre * pre
    curve = jnp.tanh(root * (pre + 0.044715 * (square * pre)))
    act = (pre * (0.5 * (1.0 + curve))).astype(BF)
    act_ref[...] = act
    act = act.astype(F32)
    slope = 0.5 * (1.0 + curve) + pre * (0.5 * (1.0 - curve * curve)) * (
        root * (1.0 + (3 * 0.044715) * square)
    )
    tiles = jnp.concatenate([cot[CS:CS + 16, 0:HALF].astype(F32) for cot in cots], axis=0).astype(BF)
    k, m = iota((CS, HALF), 0), iota((CS, HALF), 1)
    start = KCH * group_of(m // 16, flag_ref)
    low = dot(ones_where(k == start + m % 16), tiles)
    high = dot(ones_where((k == start + 16 + m % 16) & (m % 16 < 4)), tiles)
    second = jnp.where(m < 64, low + pltpu.roll(high, 64, 1), 0.0).astype(BF)
    pair, rank = iota((HALF, HALF), 0), iota((HALF, HALF), 1)
    group = group_of(rank, flag_ref)
    factor_ref[...] = dot(second, ones_where((pair == q * CB + group) & (rank < CB)))
    back = dot(second, ones_where((pair == group * CB + q) & (rank < CB)))
    d_act = jnp.zeros((CS, BLK), F32)
    grad_second = jnp.zeros((CS, HALF), F32)
    for r in range(CB):
        cot = cots[r][0:CS, :].astype(F32)
        d_act = d_act + back[:, r:r + 1] * cot
        column = jnp.sum(cot * act, axis=1, keepdims=True)
        grad_second = jnp.where(m == 32 + CB * group_of(r, flag_ref) + q, column, grad_second)
    d_pre = (d_act.astype(BF).astype(F32) * slope).astype(BF)
    zeros = jnp.zeros((W - CS, BLK), F32)
    tall = jnp.concatenate([hidden.astype(F32), zeros], axis=0).astype(BF)
    grad_first = dot(d_pre, tall, NT)
    d_hidden = side_ref[0, 0:CS, :].astype(F32) + dot(weight, d_pre, TN)
    d_mixed = jnp.concatenate([d_hidden * gate, zeros], axis=0).astype(BF)
    d_gate = d_hidden * mixed * gate * (1.0 - gate)
    grad_gain = jnp.sum(d_gate * x, axis=1, keepdims=True)
    grad_bias = jnp.sum(d_gate, axis=1, keepdims=True)
    rest_ref[...] = d_hidden + d_gate * gain
    v = dot(block_ref[...], d_mixed, NT)
    left, right = grad_first[:, :HALF], grad_first[:, HALF:]
    misc_b = jnp.where(m < 64, pltpu.roll(left, 32, 1), pltpu.roll(right, 64, 1))
    misc_b = jnp.where(m == 96, grad_gain, jnp.where(m == 97, grad_bias, misc_b))
    misc = jnp.concatenate([left, misc_b, grad_second, jnp.zeros((32, HALF), F32)], axis=0)
    right = jnp.where(iota((BLK, HALF), 1) < 32, v[:, HALF:], misc).reshape(NB, 8, HALF)
    left = v[:, :HALF].reshape(NB, 8, HALF)
    send_ref[:, 0:16, :] = jnp.concatenate([left, right], axis=1).astype(BF)
    d_block = dot(u, d_mixed, NN)
    parts = [d_block[:, HALF * s:HALF * (s + 1)].reshape(NB, 8, HALF) for s in range(4)]
    send_ref[:, 16:48, :] = jnp.concatenate(parts, axis=1).astype(BF)


def cross_backward(recv_ref, x_ref, kron_ref, part_ref, d_input_ref):
    head = recv_ref[:, 0:16, :].astype(F32)
    low = iota((NB, 8, HALF), 2) < 32
    left, right = head[:, 0:8, :], head[:, 8:16, :]
    v = jnp.concatenate(
        [left.reshape(BLK, HALF), jnp.where(low, right, 0.0).reshape(BLK, HALF)], axis=1
    ).astype(BF)
    part_ref[64:72, :] = jnp.sum(right, axis=0)
    d_input_ref[...] = dot(kron_ref[...], v).astype(BF)
    x = x_ref[...].astype(F32).reshape(BLK, W).astype(BF)
    pairs = dot(x, v, NT)
    same = iota((BLK, BLK), 0) % 8 == iota((BLK, BLK), 1) % 8
    rows = jnp.sum(jnp.where(same, pairs, 0.0).reshape(NB, 8, BLK), axis=1)
    high = rows.astype(BF)
    rest = (rows - high.astype(F32)).astype(BF)
    at, lane = iota((BLK, HALF), 0) // 8, iota((BLK, HALF), 1)
    cross = jnp.zeros((32, HALF), F32)
    for s in range(2):
        gather = ones_where(at == lane - 64 * s)
        cross = cross + dot(high[32 * s:32 * s + 32], gather) + dot(rest[32 * s:32 * s + 32], gather)
    part_ref[32:64, :] = cross
    part_ref[0:32, :] = jnp.sum(recv_ref[:, 16:48, :].astype(F32), axis=0)


def add_parts(a_ref, b_ref, out_ref):
    out_ref[...] = a_ref[...] + b_ref[...]


def pack_last(a_ref, b_ref, c_ref, d_ref, own_ref, d_input_ref, flag_ref, send_ref):
    even = a_ref[...] + c_ref[...]
    odd = b_ref[...] + d_ref[...]
    total = even + odd
    misc = jnp.where(flag_ref[3] > 0, total[64:72], own_ref[64:72, :])
    d_input = d_input_ref[...].astype(F32)
    left = d_input[:, :HALF].reshape(NB, 8, HALF)
    right = jnp.where(
        iota((NB, 8, HALF), 2) < 32, d_input[:, HALF:].reshape(NB, 8, HALF), misc[None]
    )
    send_ref[:, 0:16, :] = jnp.concatenate([left, right], axis=1).astype(BF)
    first = flag_ref[2] == 0
    block = jnp.where(first, total[0:16], total[16:32])
    cross = jnp.where(first, total[32:48], total[48:64])
    tail = jnp.concatenate([block, cross], axis=0).astype(BF)
    send_ref[:, 16:48, :] = jnp.broadcast_to(tail[None], (NB, 32, HALF))


def finish_output(hidden_ref, factor_ref, side_ref, other_ref, out_ref):
    acts = [ref.at[s] for ref in (side_ref, other_ref) for s in range(4)]
    factor = factor_ref[...]
    branch = jnp.zeros((CS, BLK), F32)
    for r in range(CB):
        branch = branch + factor[:, r:r + 1] * acts[r][...].astype(F32)
    out_ref[...] = (hidden_ref[...].astype(F32) + branch.astype(BF).astype(F32)).astype(BF)


def finish_input(recv_ref, rest_ref, flag_ref, grad_ref, first_ref, second_ref, gain_ref, bias_ref):
    head = recv_ref[:, 0:16, :].astype(F32)
    left, misc = head[:, 0:8, :], head[:, 8:16, :].reshape(BLK, HALF)
    low = iota((BLK, HALF), 1) < 32
    d_input = jnp.concatenate([left.reshape(BLK, HALF), jnp.where(low, misc, 0.0)], axis=1)
    grad_ref[...] = (rest_ref[...] + d_input.T[:CS]).astype(BF)
    a, b = misc[0:CS], misc[CS:2 * CS]
    first_ref[0, :, 0:HALF] = jnp.where(iota((CS, HALF), 1) >= 32, a, pltpu.roll(b, 96, 1))
    first_ref[0, :, HALF:CS] = pltpu.roll(b, 64, 1)[:, 0:32]
    rows = misc[CS:CS + W].T
    gain_ref[...] = rows[96:97, 0:CS]
    bias_ref[...] = rows[97:98, 0:CS]
    pick = ones_where(iota((KCH, CS), 1) == iota((KCH, CS), 0) + KCH * flag_ref[0])
    second = dot(pick, misc[2 * CS:3 * CS].astype(BF))
    second_ref[...] = pltpu.roll(second, 96, 1)[:, 0:64]


def finish_sums(recv_ref, swap_ref, flag_ref, block_ref, cross_ref):
    first = flag_ref[2] == 0
    recv, swap = recv_ref[:, 16:48, :].astype(F32), swap_ref[:, 16:48, :].astype(F32)
    low, high = jnp.where(first, recv, swap), jnp.where(first, swap, recv)
    for s, half in enumerate((low, high)):
        for t in range(2):
            at = HALF * (2 * s + t)
            block_ref[:, at:at + HALF] = half[:, 8 * t:8 * t + 8, :].reshape(BLK, HALF)
    cross = jnp.concatenate(
        [jnp.sum(low[:, 16:32, :], axis=0), jnp.sum(high[:, 16:32, :], axis=0)], axis=0
    )
    cross_ref[0:32, :] = cross[:, 0:64]
    cross_ref[32:64, :] = pltpu.roll(cross, 64, 1)[:, 0:64]


PAIR = [(i, i ^ 1) for i in range(CB)]


def shift(s):
    return [(i, (i + 2 * s) % CB) for i in range(CB)]


def along(x):
    return [lax.ppermute(x, "ch", shift(s)) for s in (1, 2, 3)]


def across(x, arrived):
    side = jnp.stack([x] + arrived)
    return side, lax.ppermute(side, "ch", PAIR)


def on_device(layer_input, w_block, w_cross, ch_first, ch_second, gate_gain, gate_bias, cotangent):
    swap = functools.partial(
        lax.all_to_all, axis_name="ctx", split_axis=0, concat_axis=0, tiled=True
    )
    ctx, ch = lax.axis_index("ctx"), lax.axis_index("ch")
    second_sum = (ctx >= 40) & (ctx < 60)
    flag = jnp.stack([ch, ch // 2, ch % 2, second_sum.astype(jnp.int32)]).astype(jnp.int32)
    (xt,) = call(transpose_input, [((NB, 8, W), BF)], layer_input)
    (packed,) = call(
        pack_cotangent, [((CS + 16, BLK), BF)], cotangent, ch_second.reshape(KCH, CB * CB),
        scratch=[pltpu.VMEM((24, HALF), F32)],
    )
    x_cols = swap(xt)
    arrived = along(packed)
    gain, bias, kron, kront = call(
        prepare,
        [((CS, HALF), F32), ((CS, HALF), F32), ((BLK, BLK), BF), ((BLK, BLK), BF)],
        gate_gain.reshape(1, CS), gate_bias.reshape(1, CS), w_cross,
        scratch=[pltpu.VMEM((HALF, W), F32)],
    )
    (u_cols,) = call(cross_forward, [((NB, 8, W), BF)], kront, x_cols, after=arrived)
    u = swap(u_cols)
    cots = across(packed, arrived)
    send, act, hidden, rest, factor = call(
        channel,
        [((NB, 48, HALF), BF), ((CS, BLK), BF), ((CS, BLK), BF), ((CS, BLK), F32), ((CS, HALF), F32)],
        u, w_block, layer_input, gain, bias, ch_first, *cots, flag,
        smem=(8,),
    )
    recv = swap(send)
    arrived = along(act)
    part, d_input = call(
        cross_backward, [((72, HALF), F32), ((BLK, W), BF)], recv, x_cols, kron, after=arrived
    )
    (total,) = call(add_parts, [((72, HALF), F32)], part, lax.ppermute(part, "ch", PAIR))
    (send,) = call(
        pack_last, [((NB, 48, HALF), BF)], total, *along(total), part, d_input, flag, smem=(6,)
    )
    recv = swap(send)
    acts = across(act, arrived)
    (output,) = call(finish_output, [((CS, BLK), BF)], hidden, factor, *acts)
    swapped = lax.ppermute(recv, "ch", PAIR)
    grad_input, grad_first, grad_second, grad_gain, grad_bias = call(
        finish_input,
        [((CS, BLK), BF), ((1, CS, CS), F32), ((KCH, CB * CB), F32), ((1, CS), F32), ((1, CS), F32)],
        recv, rest, flag,
        smem=(2,),
    )
    grad_block, grad_cross = call(
        finish_sums, [((BLK, BLK), F32), ((NB, NB), F32)], recv, swapped, flag, smem=(2,)
    )
    return (
        output,
        grad_input,
        grad_block,
        grad_cross,
        grad_first,
        grad_second.reshape(KCH, CB, CB),
        grad_gain.reshape(CS),
        grad_bias.reshape(CS),
    )


def solution(mesh):
    in_specs = (
        P("ch", "ctx"),
        P(),
        P(),
        P("ch", None, None),
        P("ch", None, None),
        P("ch"),
        P("ch"),
        P("ch", "ctx"),
    )
    out_specs = (
        P("ch", "ctx"),
        P("ch", "ctx"),
        P(),
        P(),
        P("ch", None, None),
        P("ch", None, None),
        P("ch"),
        P("ch"),
    )
    return jax.shard_map(
        on_device, mesh=mesh, in_specs=in_specs, out_specs=out_specs, check_vma=False
    )
```

time: 946 us -> 183 us (0.19)
  the two profiles are of different devices: /device:TPU:22 before, /device:TPU:1 now
where the time goes in v2:
time: 183 us; the launch traced here: 182 us
  starting transfers between devices  88 us (48%)
  waiting for transfers between devices  44.6 us (24%)
  blocking collectives  29.2 us (16%)
  Pallas kernels  11.8 us (6%)
  local copies, waits for them, and re-layouts  6.86 us (4%)
    ppermute x9, starting transfers between devices, along(): return [lax.ppermute(x, 'ch', shift(s)) for s in (1, 2, 3)]  38.2 us
    ppermute x9, waiting for transfers between devices, along(): return [lax.ppermute(x, 'ch', shift(s)) for s in (1, 2, 3)]  29.6 us
    all_to_all x1, blocking collectives, on_device(): recv = swap(send)  29.2 us
    all_to_all x1, starting transfers between devices, on_device(): u = swap(u_cols)  13.7 us
    all_to_all x1, starting transfers between devices, on_device(): x_cols = swap(xt)  13.1 us
    all_to_all x1, waiting for transfers between devices, on_device(): u = swap(u_cols)  12.1 us
    pallas_call x11, Pallas kernels, call(): pl.pallas_call(run, out_shape=[jax.ShapeDtypeStruct(s, d) for s, d in out...  11.8 us
    ppermute x1, starting transfers between devices, on_device(): swapped = lax.ppermute(recv, 'ch', PAIR)  7.62 us
  transfers between devices with their start and end apart: 16, of which 9 were waited for; matrix products, arithmetic and copies ran while one was open for 1% of the time, Pallas kernels for 2%

profile of v2, /device:TPU:1, one launch (start us, length us, event | category | flops | bytes accessed | tf_op | source)
XLA Modules:
  0.0 181.7 jit_solution(17367149723262518458)
XLA Ops:
  0.6 0.9 copy-done
  2.4 13.1 %all-to-all-start = ((bf16[64,8,256]{2,1,0:T(8,128)(2,1)}), bf16[64,8,256]{2,1,0:T(8,128)(2,1)S(1)}, u32[]{:S(2)}, u32[]{:S(2)}) async-start(bf16[64,8,256]{2,1,0:T(8,128)(2,1)} %shard_map.144), calls=%async_computation | async-start | bytes 524288 | tf_op jit(solution)/shard_map/all_to_all | solution.py:274
  15.7 9.8 %collective-permute-start.2 = (bf16[176,512]{1,0:T(8,128)(2,1)S(1)}, bf16[176,512]{1,0:T(8,128)(2,1)S(1)}, u32[]{:S(2)}, u32[]{:S(2)}) collective-permute-start(bf16[176,512]{1,0:T(8,128)(2,1)S(1)} %shard_map.145), channel_id=1, source_target_pairs={{0,6},{1,7},{2,0},{3,1},{4,2},{5,3},{6,4},{7,5},{8,14},{9,15},{10,... | collective-permute-start | bytes 540680 | tf_op jit(solution)/shard_map/ppermute | solution.py:254
  25.4 1.9 %collective-permute-start.1 = (bf16[176,512]{1,0:T(8,128)(2,1)S(1)}, bf16[176,512]{1,0:T(8,128)(2,1)S(1)}, u32[]{:S(2)}, u32[]{:S(2)}) collective-permute-start(bf16[176,512]{1,0:T(8,128)(2,1)S(1)} %shard_map.145), channel_id=1, source_target_pairs={{0,4},{1,5},{2,6},{3,7},{4,0},{5,1},{6,2},{7,3},{8,12},{9,13},{10,... | collective-permute-start | bytes 540680 | tf_op jit(solution)/shard_map/ppermute | solution.py:254
  27.3 4.2 %collective-permute-start = (bf16[176,512]{1,0:T(8,128)(2,1)S(1)}, bf16[176,512]{1,0:T(8,128)(2,1)S(1)}, u32[]{:S(2)}, u32[]{:S(2)}) collective-permute-start(bf16[176,512]{1,0:T(8,128)(2,1)S(1)} %shard_map.145), channel_id=1, source_target_pairs={{0,2},{1,3},{2,4},{3,5},{4,6},{5,7},{6,0},{7,1},{8,10},{9,11},{10,... | collective-permute-start | bytes 540680 | tf_op jit(solution)/shard_map/ppermute | solution.py:254
  31.6 8.2 %collective-permute-done.2.refs_4_ = bf16[176,512]{1,0:T(8,128)(2,1)S(1)} collective-permute-done((bf16[176,512]{1,0:T(8,128)(2,1)S(1)}, bf16[176,512]{1,0:T(8,128)(2,1)S(1)}, u32[]{:S(2)}, u32[]{:S(2)}) %collective-permute-start.2) | collective-permute-done | bytes 180256 | tf_op jit(solution)/shard_map/ppermute | solution.py:254
  40.7 4.4 %collective-permute-start.3 = (bf16[4,176,512]{2,1,0:T(8,128)(2,1)S(1)}, bf16[4,176,512]{2,1,0:T(8,128)(2,1)S(1)}, u32[]{:S(2)}, u32[]{:S(2)}) collective-permute-start(bf16[4,176,512]{2,1,0:T(8,128)(2,1)S(1)} %pad_maximum_fusion.refs_6_), channel_id=1, source_target_pairs={{0,1},{1,0},{2,3},{3,2},{4,5},{5,4},{6,7},{7,6},{8,9},{9,8},{10,11... | collective-permute-start | bytes 2162696 | tf_op jit(solution)/shard_map/ppermute | solution.py:259
  48.6 1.0 shard_map.146
  49.6 13.7 %all-to-all-start.1 = ((bf16[64,8,256]{2,1,0:T(8,128)(2,1)}), bf16[64,8,256]{2,1,0:T(8,128)(2,1)S(1)}, u32[]{:S(2)}, u32[]{:S(2)}) async-start(bf16[64,8,256]{2,1,0:T(8,128)(2,1)} %shard_map.146), calls=%async_computation.1 | async-start | bytes 524288 | tf_op jit(solution)/shard_map/all_to_all | solution.py:283
  63.3 12.1 %all-to-all-done.1.refs_0_ = bf16[64,8,256]{2,1,0:T(8,128)(2,1)S(1)} async-done(((bf16[64,8,256]{2,1,0:T(8,128)(2,1)}), bf16[64,8,256]{2,1,0:T(8,128)(2,1)S(1)}, u32[]{:S(2)}, u32[]{:S(2)}) %all-to-all-start.1) | async-done | bytes 262176 | tf_op jit(solution)/shard_map/all_to_all | solution.py:283
  76.3 0.9 copy-done.10
  77.2 3.4 %shard_map.147 = (bf16[64,48,128]{2,1,0:T(8,128)(2,1)}, bf16[160,512]{1,0:T(8,128)(2,1)S(1)}, bf16[160,512]{1,0:T(8,128)(2,1)S(1)}, f32[160,512]{1,0:T(8,128)S(1)}, f32[160,128]{1,0:T(8,128)S(1)}) custom-call(bf16[64,8,256]{2,1,0:T(8,128)(2,1)S(1)} %all-to-all-done.1.refs_0_, bf16[512,512]{1,0:T(8,128)(2,1)S(1)} %copy-done.2, ...), custom_call_target="tpu_custom_call" | custom-call | tf_op jit(solution)/shard_map/pallas_call | solution.py:49
  81.2 5.5 %all-to-all-start.2 = ((bf16[64,48,128]{2,1,0:T(8,128)(2,1)}), bf16[64,48,128]{2,1,0:T(8,128)(2,1)S(1)}, u32[]{:S(2)}, u32[]{:S(2)}) async-start(bf16[64,48,128]{2,1,0:T(8,128)(2,1)} %get-tuple-element.32), calls=%async_computation.2 | async-start | bytes 1572864 | tf_op jit(solution)/shard_map/all_to_all | solution.py:291
  86.7 6.0 %collective-permute-start.6 = (bf16[160,512]{1,0:T(8,128)(2,1)S(1)}, bf16[160,512]{1,0:T(8,128)(2,1)S(1)}, u32[]{:S(2)}, u32[]{:S(2)}) collective-permute-start(bf16[160,512]{1,0:T(8,128)(2,1)S(1)} %get-tuple-element.31), channel_id=1, source_target_pairs={{0,6},{1,7},{2,0},{3,1},{4,2},{5,3},{6,4},{7,5},{8,14},{9,15},{10,... | collective-permute-start | bytes 491528 | tf_op jit(solution)/shard_map/ppermute | solution.py:254
  92.7 2.0 %collective-permute-start.5 = (bf16[160,512]{1,0:T(8,128)(2,1)S(1)}, bf16[160,512]{1,0:T(8,128)(2,1)S(1)}, u32[]{:S(2)}, u32[]{:S(2)}) collective-permute-start(bf16[160,512]{1,0:T(8,128)(2,1)S(1)} %get-tuple-element.31), channel_id=1, source_target_pairs={{0,4},{1,5},{2,6},{3,7},{4,0},{5,1},{6,2},{7,3},{8,12},{9,13},{10,... | collective-permute-start | bytes 491528 | tf_op jit(solution)/shard_map/ppermute | solution.py:254
  94.7 4.2 %collective-permute-start.4 = (bf16[160,512]{1,0:T(8,128)(2,1)S(1)}, bf16[160,512]{1,0:T(8,128)(2,1)S(1)}, u32[]{:S(2)}, u32[]{:S(2)}) collective-permute-start(bf16[160,512]{1,0:T(8,128)(2,1)S(1)} %get-tuple-element.31), channel_id=1, source_target_pairs={{0,2},{1,3},{2,4},{3,5},{4,6},{5,7},{6,0},{7,1},{8,10},{9,11},{10,... | collective-permute-start | bytes 491528 | tf_op jit(solution)/shard_map/ppermute | solution.py:254
  98.9 15.4 %collective-permute-done.5.refs_4_ = bf16[160,512]{1,0:T(8,128)(2,1)S(1)} collective-permute-done((bf16[160,512]{1,0:T(8,128)(2,1)S(1)}, bf16[160,512]{1,0:T(8,128)(2,1)S(1)}, u32[]{:S(2)}, u32[]{:S(2)}) %collective-permute-start.5) | collective-permute-done | bytes 163872 | tf_op jit(solution)/shard_map/ppermute | solution.py:254
  114.3 1.4 collective-permute-done.4.refs_3_
  115.7 1.0 shard_map.149
  116.7 3.7 %collective-permute-start.8 = (f32[72,128]{1,0:T(8,128)S(1)}, f32[72,128]{1,0:T(8,128)S(1)}, u32[]{:S(2)}, u32[]{:S(2)}) collective-permute-start(f32[72,128]{1,0:T(8,128)S(1)} %get-tuple-element.34.refs_0_.refs_4_), channel_id=1, source_target_pairs={{0,1},{1,0},{2,3},{3,2},{4,5},{5,4},{6,7},{7,6},{8,9},{9,8},{10,11... | collective-permute-start | bytes 110600 | tf_op jit(solution)/shard_map/ppermute | solution.py:296
  121.2 4.2 %collective-permute-start.11 = (f32[72,128]{1,0:T(8,128)S(1)}, f32[72,128]{1,0:T(8,128)S(1)}, u32[]{:S(2)}, u32[]{:S(2)}) collective-permute-start(f32[72,128]{1,0:T(8,128)S(1)} %shard_map.150.refs_0_), channel_id=1, source_target_pairs={{0,6},{1,7},{2,0},{3,1},{4,2},{5,3},{6,4},{7,5},{8,14},{9,15},{10,... | collective-permute-start | bytes 110600 | tf_op jit(solution)/shard_map/ppermute | solution.py:254
  125.4 2.6 %collective-permute-start.10 = (f32[72,128]{1,0:T(8,128)S(1)}, f32[72,128]{1,0:T(8,128)S(1)}, u32[]{:S(2)}, u32[]{:S(2)}) collective-permute-start(f32[72,128]{1,0:T(8,128)S(1)} %shard_map.150.refs_0_), channel_id=1, source_target_pairs={{0,4},{1,5},{2,6},{3,7},{4,0},{5,1},{6,2},{7,3},{8,12},{9,13},{10,... | collective-permute-start | bytes 110600 | tf_op jit(solution)/shard_map/ppermute | solution.py:254
  128.0 3.4 %collective-permute-start.9 = (f32[72,128]{1,0:T(8,128)S(1)}, f32[72,128]{1,0:T(8,128)S(1)}, u32[]{:S(2)}, u32[]{:S(2)}) collective-permute-start(f32[72,128]{1,0:T(8,128)S(1)} %shard_map.150.refs_0_), channel_id=1, source_target_pairs={{0,2},{1,3},{2,4},{3,5},{4,6},{5,7},{6,0},{7,1},{8,10},{9,11},{10,... | collective-permute-start | bytes 110600 | tf_op jit(solution)/shard_map/ppermute | solution.py:254
  131.4 2.8 %collective-permute-done.10.refs_2_ = f32[72,128]{1,0:T(8,128)S(1)} collective-permute-done((f32[72,128]{1,0:T(8,128)S(1)}, f32[72,128]{1,0:T(8,128)S(1)}, u32[]{:S(2)}, u32[]{:S(2)}) %collective-permute-start.10) | collective-permute-done | bytes 36896 | tf_op jit(solution)/shard_map/ppermute | solution.py:254
  134.3 1.0 collective-permute-done.9.refs_1_
  135.9 29.2 %all_to_all.20.refs_0_ = bf16[64,48,128]{2,1,0:T(8,128)(2,1)S(1)} all-to-all(bf16[64,48,128]{2,1,0:T(8,128)(2,1)S(1)} %shard_map.151), channel_id=1, replica_groups=mesh['ctx'=64,'ch'=8] {'ctx'}, dimensions={0} | all-to-all | bytes 1572864 | tf_op jit(solution)/shard_map/all_to_all | solution.py:300
  165.0 7.6 %collective-permute-start.12 = (bf16[64,48,128]{2,1,0:T(8,128)(2,1)S(1)}, bf16[64,48,128]{2,1,0:T(8,128)(2,1)S(1)}, u32[]{:S(2)}, u32[]{:S(2)}) collective-permute-start(bf16[64,48,128]{2,1,0:T(8,128)(2,1)S(1)} %all_to_all.20.refs_0_), channel_id=1, source_target_pairs={{0,1},{1,0},{2,3},{3,2},{4,5},{5,4},{6,7},{7,6},{8,9},{9,8},{10,11... | collective-permute-start | bytes 2359304 | tf_op jit(solution)/shard_map/ppermute | solution.py:303
  172.8 1.9 %collective-permute-start.7 = (bf16[4,160,512]{2,1,0:T(8,128)(2,1)S(1)}, bf16[4,160,512]{2,1,0:T(8,128)(2,1)S(1)}, u32[]{:S(2)}, u32[]{:S(2)}) collective-permute-start(bf16[4,160,512]{2,1,0:T(8,128)(2,1)S(1)} %pad_maximum_fusion.1.refs_2_), channel_id=1, source_target_pairs={{0,1},{1,0},{2,3},{3,2},{4,5},{5,4},{6,7},{7,6},{8,9},{9,8},{10,11... | collective-permute-start | bytes 1966088 | tf_op jit(solution)/shard_map/ppermute | solution.py:259
  174.7 2.1 %collective-permute-done.7.refs_3_ = bf16[4,160,512]{2,1,0:T(8,128)(2,1)S(1)} collective-permute-done((bf16[4,160,512]{2,1,0:T(8,128)(2,1)S(1)}, bf16[4,160,512]{2,1,0:T(8,128)(2,1)S(1)}, u32[]{:S(2)}, u32[]{:S(2)}) %collective-permute-start.7) | collective-permute-done | bytes 655392 | tf_op jit(solution)/shard_map/ppermute | solution.py:259
  176.8 1.0 shard_map.148
  177.8 1.4 shard_map.152
  179.9 1.8 shard_map.153
  (51 shorter events, 9.2 us)
Async XLA Ops:
  0.6 0.9 copy-start
  2.4 13.1 %copy-start.16 = (bf16[20,8,8]{0,2,1:T(8,128)(2,1)S(1)}, bf16[20,8,8]{0,2,1:T(8,128)(2,1)}, u32[]{:S(2)}) copy-start(bf16[20,8,8]{0,2,1:T(8,128)(2,1)} %param.12) | copy-start | bytes 7684
  2.4 13.2 %copy-start.5 = (bf16[160,512]{1,0:T(8,128)(2,1)S(1)}, bf16[160,512]{1,0:T(8,128)(2,1)}, u32[]{:S(2)}) copy-start(bf16[160,512]{1,0:T(8,128)(2,1)} %refs_0_.3) | copy-start | bytes 491524
  2.4 46.2 %all-to-all-start = ((bf16[64,8,256]{2,1,0:T(8,128)(2,1)}), bf16[64,8,256]{2,1,0:T(8,128)(2,1)S(1)}, u32[]{:S(2)}, u32[]{:S(2)}) async-start(bf16[64,8,256]{2,1,0:T(8,128)(2,1)} %shard_map.144), calls=%async_computation | async-start | bytes 524288 | tf_op jit(solution)/shard_map/all_to_all | solution.py:274
  15.7 24.1 %collective-permute-start.2 = (bf16[176,512]{1,0:T(8,128)(2,1)S(1)}, bf16[176,512]{1,0:T(8,128)(2,1)S(1)}, u32[]{:S(2)}, u32[]{:S(2)}) collective-permute-start(bf16[176,512]{1,0:T(8,128)(2,1)S(1)} %shard_map.145), channel_id=1, source_target_pairs={{0,6},{1,7},{2,0},{3,1},{4,2},{5,3},{6,4},{7,5},{8,14},{9,15},{10,... | collective-permute-start | bytes 540680 | tf_op jit(solution)/shard_map/ppermute | solution.py:254
  25.4 15.2 %collective-permute-start.1 = (bf16[176,512]{1,0:T(8,128)(2,1)S(1)}, bf16[176,512]{1,0:T(8,128)(2,1)S(1)}, u32[]{:S(2)}, u32[]{:S(2)}) collective-permute-start(bf16[176,512]{1,0:T(8,128)(2,1)S(1)} %shard_map.145), channel_id=1, source_target_pairs={{0,4},{1,5},{2,6},{3,7},{4,0},{5,1},{6,2},{7,3},{8,12},{9,13},{10,... | collective-permute-start | bytes 540680 | tf_op jit(solution)/shard_map/ppermute | solution.py:254
  27.3 13.3 %collective-permute-start = (bf16[176,512]{1,0:T(8,128)(2,1)S(1)}, bf16[176,512]{1,0:T(8,128)(2,1)S(1)}, u32[]{:S(2)}, u32[]{:S(2)}) collective-permute-start(bf16[176,512]{1,0:T(8,128)(2,1)S(1)} %shard_map.145), channel_id=1, source_target_pairs={{0,2},{1,3},{2,4},{3,5},{4,6},{5,7},{6,0},{7,1},{8,10},{9,11},{10,... | collective-permute-start | bytes 540680 | tf_op jit(solution)/shard_map/ppermute | solution.py:254
  40.6 4.5 %copy-start.13 = (bf16[64,64]{1,0:T(8,128)(2,1)S(1)}, bf16[64,64]{1,0:T(8,128)(2,1)}, u32[]{:S(2)}) copy-start(bf16[64,64]{1,0:T(8,128)(2,1)} %refs_2_.2) | copy-start | bytes 24580
  40.6 4.5 %copy-start.15 = (f32[160]{0:T(256)S(1)}, f32[160]{0:T(256)}, u32[]{:S(2)}) copy-start(f32[160]{0:T(256)} %param.14) | copy-start | bytes 1924
  40.7 22.6 %collective-permute-start.3 = (bf16[4,176,512]{2,1,0:T(8,128)(2,1)S(1)}, bf16[4,176,512]{2,1,0:T(8,128)(2,1)S(1)}, u32[]{:S(2)}, u32[]{:S(2)}) collective-permute-start(bf16[4,176,512]{2,1,0:T(8,128)(2,1)S(1)} %pad_maximum_fusion.refs_6_), channel_id=1, source_target_pairs={{0,1},{1,0},{2,3},{3,2},{4,5},{5,4},{6,7},{7,6},{8,9},{9,8},{10,11... | collective-permute-start | bytes 2162696 | tf_op jit(solution)/shard_map/ppermute | solution.py:259
  45.1 0.7 copy-start.14
  46.5 0.8 copy-start.3
  47.3 0.6 copy-start.7
  47.9 0.6 copy-start.9
  48.6 26.9 %copy-start.2 = (bf16[512,512]{1,0:T(8,128)(2,1)S(1)}, bf16[512,512]{1,0:T(8,128)(2,1)}, u32[]{:S(2)}) copy-start(bf16[512,512]{1,0:T(8,128)(2,1)} %refs_1_.1) | copy-start | bytes 1572868
  49.6 25.9 %copy-start.1 = (bf16[160,512]{1,0:T(8,128)(2,1)S(1)}, bf16[160,512]{1,0:T(8,128)(2,1)}, u32[]{:S(2)}) copy-start(bf16[160,512]{1,0:T(8,128)(2,1)} %refs_2_.3) | copy-start | bytes 491524
  49.6 25.9 %copy-start.6 = (bf16[1,160,160]{2,1,0:T(8,128)(2,1)S(1)}, bf16[1,160,160]{2,1,0:T(8,128)(2,1)}, u32[]{:S(2)}) copy-start(bf16[1,160,160]{2,1,0:T(8,128)(2,1)} %refs_5_.1) | copy-start | bytes 153604
  49.6 25.9 %all-to-all-start.1 = ((bf16[64,8,256]{2,1,0:T(8,128)(2,1)}), bf16[64,8,256]{2,1,0:T(8,128)(2,1)S(1)}, u32[]{:S(2)}, u32[]{:S(2)}) async-start(bf16[64,8,256]{2,1,0:T(8,128)(2,1)} %shard_map.146), calls=%async_computation.1 | async-start | bytes 524288 | tf_op jit(solution)/shard_map/all_to_all | solution.py:283
  75.5 0.9 copy-start.8
  76.3 0.9 copy-start.10
  81.2 34.5 %copy-start.4 = (bf16[512,512]{1,0:T(8,128)(2,1)S(1)}, bf16[512,512]{1,0:T(8,128)(2,1)}, u32[]{:S(2)}) copy-start(bf16[512,512]{1,0:T(8,128)(2,1)} %copy-done.3) | copy-start | bytes 1572868
  81.2 34.5 %all-to-all-start.2 = ((bf16[64,48,128]{2,1,0:T(8,128)(2,1)}), bf16[64,48,128]{2,1,0:T(8,128)(2,1)S(1)}, u32[]{:S(2)}, u32[]{:S(2)}) async-start(bf16[64,48,128]{2,1,0:T(8,128)(2,1)} %get-tuple-element.32), calls=%async_computation.2 | async-start | bytes 1572864 | tf_op jit(solution)/shard_map/all_to_all | solution.py:291
  86.7 12.2 %collective-permute-start.6 = (bf16[160,512]{1,0:T(8,128)(2,1)S(1)}, bf16[160,512]{1,0:T(8,128)(2,1)S(1)}, u32[]{:S(2)}, u32[]{:S(2)}) collective-permute-start(bf16[160,512]{1,0:T(8,128)(2,1)S(1)} %get-tuple-element.31), channel_id=1, source_target_pairs={{0,6},{1,7},{2,0},{3,1},{4,2},{5,3},{6,4},{7,5},{8,14},{9,15},{10,... | collective-permute-start | bytes 491528 | tf_op jit(solution)/shard_map/ppermute | solution.py:254
  92.7 21.6 %collective-permute-start.5 = (bf16[160,512]{1,0:T(8,128)(2,1)S(1)}, bf16[160,512]{1,0:T(8,128)(2,1)S(1)}, u32[]{:S(2)}, u32[]{:S(2)}) collective-permute-start(bf16[160,512]{1,0:T(8,128)(2,1)S(1)} %get-tuple-element.31), channel_id=1, source_target_pairs={{0,4},{1,5},{2,6},{3,7},{4,0},{5,1},{6,2},{7,3},{8,12},{9,13},{10,... | collective-permute-start | bytes 491528 | tf_op jit(solution)/shard_map/ppermute | solution.py:254
  94.7 21.0 %collective-permute-start.4 = (bf16[160,512]{1,0:T(8,128)(2,1)S(1)}, bf16[160,512]{1,0:T(8,128)(2,1)S(1)}, u32[]{:S(2)}, u32[]{:S(2)}) collective-permute-start(bf16[160,512]{1,0:T(8,128)(2,1)S(1)} %get-tuple-element.31), channel_id=1, source_target_pairs={{0,2},{1,3},{2,4},{3,5},{4,6},{5,7},{6,0},{7,1},{8,10},{9,11},{10,... | collective-permute-start | bytes 491528 | tf_op jit(solution)/shard_map/ppermute | solution.py:254
  116.7 4.5 %collective-permute-start.8 = (f32[72,128]{1,0:T(8,128)S(1)}, f32[72,128]{1,0:T(8,128)S(1)}, u32[]{:S(2)}, u32[]{:S(2)}) collective-permute-start(f32[72,128]{1,0:T(8,128)S(1)} %get-tuple-element.34.refs_0_.refs_4_), channel_id=1, source_target_pairs={{0,1},{1,0},{2,3},{3,2},{4,5},{5,4},{6,7},{7,6},{8,9},{9,8},{10,11... | collective-permute-start | bytes 110600 | tf_op jit(solution)/shard_map/ppermute | solution.py:296
  121.2 10.2 %collective-permute-start.11 = (f32[72,128]{1,0:T(8,128)S(1)}, f32[72,128]{1,0:T(8,128)S(1)}, u32[]{:S(2)}, u32[]{:S(2)}) collective-permute-start(f32[72,128]{1,0:T(8,128)S(1)} %shard_map.150.refs_0_), channel_id=1, source_target_pairs={{0,6},{1,7},{2,0},{3,1},{4,2},{5,3},{6,4},{7,5},{8,14},{9,15},{10,... | collective-permute-start | bytes 110600 | tf_op jit(solution)/shard_map/ppermute | solution.py:254
  125.4 8.9 %collective-permute-start.10 = (f32[72,128]{1,0:T(8,128)S(1)}, f32[72,128]{1,0:T(8,128)S(1)}, u32[]{:S(2)}, u32[]{:S(2)}) collective-permute-start(f32[72,128]{1,0:T(8,128)S(1)} %shard_map.150.refs_0_), channel_id=1, source_target_pairs={{0,4},{1,5},{2,6},{3,7},{4,0},{5,1},{6,2},{7,3},{8,12},{9,13},{10,... | collective-permute-start | bytes 110600 | tf_op jit(solution)/shard_map/ppermute | solution.py:254
  128.0 7.2 %collective-permute-start.9 = (f32[72,128]{1,0:T(8,128)S(1)}, f32[72,128]{1,0:T(8,128)S(1)}, u32[]{:S(2)}, u32[]{:S(2)}) collective-permute-start(f32[72,128]{1,0:T(8,128)S(1)} %shard_map.150.refs_0_), channel_id=1, source_target_pairs={{0,2},{1,3},{2,4},{3,5},{4,6},{5,7},{6,0},{7,1},{8,10},{9,11},{10,... | collective-permute-start | bytes 110600 | tf_op jit(solution)/shard_map/ppermute | solution.py:254
  165.0 14.9 %collective-permute-start.12 = (bf16[64,48,128]{2,1,0:T(8,128)(2,1)S(1)}, bf16[64,48,128]{2,1,0:T(8,128)(2,1)S(1)}, u32[]{:S(2)}, u32[]{:S(2)}) collective-permute-start(bf16[64,48,128]{2,1,0:T(8,128)(2,1)S(1)} %all_to_all.20.refs_0_), channel_id=1, source_target_pairs={{0,1},{1,0},{2,3},{3,2},{4,5},{5,4},{6,7},{7,6},{8,9},{9,8},{10,11... | collective-permute-start | bytes 2359304 | tf_op jit(solution)/shard_map/ppermute | solution.py:303
  172.7 4.1 %copy-start.12 = (f32[160,128]{1,0:T(8,128)S(1)}, f32[160,128]{1,0:T(8,128)}, u32[]{:S(2)}) copy-start(f32[160,128]{1,0:T(8,128)} %copy-done.11) | copy-start | bytes 245764
  172.8 4.0 %collective-permute-start.7 = (bf16[4,160,512]{2,1,0:T(8,128)(2,1)S(1)}, bf16[4,160,512]{2,1,0:T(8,128)(2,1)S(1)}, u32[]{:S(2)}, u32[]{:S(2)}) collective-permute-start(bf16[4,160,512]{2,1,0:T(8,128)(2,1)S(1)} %pad_maximum_fusion.1.refs_2_), channel_id=1, source_target_pairs={{0,1},{1,0},{2,3},{3,2},{4,5},{5,4},{6,7},{7,6},{8,9},{9,8},{10,11... | collective-permute-start | bytes 1966088 | tf_op jit(solution)/shard_map/ppermute | solution.py:259
  (1 other events, 0.6 us)

commit v3 on v2

--- a/solution.py
+++ b/solution.py
@@ -54,10 +54,6 @@
         scratch_shapes=list(scratch),
         compiler_params=pltpu.CompilerParams(vmem_limit_bytes=48 * 1024 * 1024),
     )(*args, *after)
-
-
-def group_of(rank, flag_ref):
-    return ((flag_ref[1] - rank % 4) & 3) * 2 + ((rank // 4) ^ flag_ref[2])
 
 
 def transpose_input(x_ref, xt_ref):
@@ -93,9 +89,9 @@
     out_ref[...] = dot(kront_ref[...], cols).reshape(NB, 8, W).astype(BF)
 
 
-def channel(u_ref, block_ref, x_ref, gain_ref, bias_ref, weight_ref, side_ref, other_ref,
-            flag_ref, send_ref, act_ref, hidden_ref, rest_ref, factor_ref):
-    cots = [ref.at[s] for ref in (side_ref, other_ref) for s in range(4)]
+def channel(u_ref, block_ref, x_ref, gain_ref, bias_ref, weight_ref, cot_ref,
+            cots_ref, flag_ref, send_ref, act_ref, hidden_ref, rest_ref, factor_ref):
+    cots = [cots_ref.at[g] for g in range(CB)]
     q = flag_ref[0]
     u = u_ref[...].astype(F32).reshape(BLK, W).astype(BF)
     mixed = dot(u, block_ref[...], TN)[:CS].astype(BF).astype(F32)
@@ -118,26 +114,25 @@
     )
     tiles = jnp.concatenate([cot[CS:CS + 16, 0:HALF].astype(F32) for cot in cots], axis=0).astype(BF)
     k, m = iota((CS, HALF), 0), iota((CS, HALF), 1)
-    start = KCH * group_of(m // 16, flag_ref)
+    start = KCH * (m // 16)
     low = dot(ones_where(k == start + m % 16), tiles)
     high = dot(ones_where((k == start + 16 + m % 16) & (m % 16 < 4)), tiles)
     second = jnp.where(m < 64, low + pltpu.roll(high, 64, 1), 0.0).astype(BF)
-    pair, rank = iota((HALF, HALF), 0), iota((HALF, HALF), 1)
-    group = group_of(rank, flag_ref)
-    factor_ref[...] = dot(second, ones_where((pair == q * CB + group) & (rank < CB)))
-    back = dot(second, ones_where((pair == group * CB + q) & (rank < CB)))
+    pair, group = iota((HALF, HALF), 0), iota((HALF, HALF), 1)
+    factor_ref[...] = dot(second, ones_where((pair == q * CB + group) & (group < CB)))
+    back = dot(second, ones_where((pair == group * CB + q) & (group < CB)))
     d_act = jnp.zeros((CS, BLK), F32)
     grad_second = jnp.zeros((CS, HALF), F32)
-    for r in range(CB):
-        cot = cots[r][0:CS, :].astype(F32)
-        d_act = d_act + back[:, r:r + 1] * cot
+    for g in range(CB):
+        cot = cots[g][0:CS, :].astype(F32)
+        d_act = d_act + back[:, g:g + 1] * cot
         column = jnp.sum(cot * act, axis=1, keepdims=True)
-        grad_second = jnp.where(m == 32 + CB * group_of(r, flag_ref) + q, column, grad_second)
+        grad_second = jnp.where(m == 32 + CB * g + q, column, grad_second)
     d_pre = (d_act.astype(BF).astype(F32) * slope).astype(BF)
     zeros = jnp.zeros((W - CS, BLK), F32)
     tall = jnp.concatenate([hidden.astype(F32), zeros], axis=0).astype(BF)
     grad_first = dot(d_pre, tall, NT)
-    d_hidden = side_ref[0, 0:CS, :].astype(F32) + dot(weight, d_pre, TN)
+    d_hidden = cot_ref[...].astype(F32) + dot(weight, d_pre, TN)
     d_mixed = jnp.concatenate([d_hidden * gate, zeros], axis=0).astype(BF)
     d_gate = d_hidden * mixed * gate * (1.0 - gate)
     grad_gain = jnp.sum(d_gate * x, axis=1, keepdims=True)
@@ -156,14 +151,15 @@
     send_ref[:, 16:48, :] = jnp.concatenate(parts, axis=1).astype(BF)
 
 
-def cross_backward(recv_ref, x_ref, kron_ref, part_ref, d_input_ref):
+def cross_backward(recv_ref, x_ref, kron_ref, send_ref, d_input_ref, misc_ref):
     head = recv_ref[:, 0:16, :].astype(F32)
     low = iota((NB, 8, HALF), 2) < 32
     left, right = head[:, 0:8, :], head[:, 8:16, :]
     v = jnp.concatenate(
         [left.reshape(BLK, HALF), jnp.where(low, right, 0.0).reshape(BLK, HALF)], axis=1
     ).astype(BF)
-    part_ref[64:72, :] = jnp.sum(right, axis=0)
+    misc = jnp.sum(right, axis=0)
+    misc_ref[...] = misc
     d_input_ref[...] = dot(kron_ref[...], v).astype(BF)
     x = x_ref[...].astype(F32).reshape(BLK, W).astype(BF)
     pairs = dot(x, v, NT)
@@ -176,19 +172,13 @@
     for s in range(2):
         gather = ones_where(at == lane - 64 * s)
         cross = cross + dot(high[32 * s:32 * s + 32], gather) + dot(rest[32 * s:32 * s + 32], gather)
-    part_ref[32:64, :] = cross
-    part_ref[0:32, :] = jnp.sum(recv_ref[:, 16:48, :].astype(F32), axis=0)
-
-
-def add_parts(a_ref, b_ref, out_ref):
-    out_ref[...] = a_ref[...] + b_ref[...]
-
-
-def pack_last(a_ref, b_ref, c_ref, d_ref, own_ref, d_input_ref, flag_ref, send_ref):
-    even = a_ref[...] + c_ref[...]
-    odd = b_ref[...] + d_ref[...]
-    total = even + odd
-    misc = jnp.where(flag_ref[3] > 0, total[64:72], own_ref[64:72, :])
+    tail = jnp.sum(recv_ref[:, 16:48, :].astype(F32), axis=0)
+    send_ref[...] = jnp.concatenate([tail, cross, misc], axis=0)
+
+
+def pack_last(recv_ref, own_ref, d_input_ref, flag_ref, send_ref):
+    total = jnp.sum(recv_ref[...], axis=0)
+    misc = jnp.where(flag_ref[3] > 0, total[64:72], own_ref[...])
     d_input = d_input_ref[...].astype(F32)
     left = d_input[:, :HALF].reshape(NB, 8, HALF)
     right = jnp.where(
@@ -202,12 +192,20 @@
     send_ref[:, 16:48, :] = jnp.broadcast_to(tail[None], (NB, 32, HALF))
 
 
-def finish_output(hidden_ref, factor_ref, side_ref, other_ref, out_ref):
-    acts = [ref.at[s] for ref in (side_ref, other_ref) for s in range(4)]
+def split_last(recv_ref, out_ref):
+    recv = recv_ref[:, 16:32, :].astype(F32)
+    left = recv[:, 0:8, :].reshape(BLK, HALF)
+    right = recv[:, 8:16, :].reshape(BLK, HALF)
+    out_ref[0:BLK, :] = jnp.concatenate([left, right], axis=1).astype(BF)
+    cross = jnp.sum(recv_ref[:, 32:48, :].astype(F32), axis=0)
+    out_ref[BLK:BLK + 16, :] = jnp.concatenate([cross, cross], axis=1).astype(BF)
+
+
+def finish_output(hidden_ref, factor_ref, acts_ref, out_ref):
     factor = factor_ref[...]
     branch = jnp.zeros((CS, BLK), F32)
-    for r in range(CB):
-        branch = branch + factor[:, r:r + 1] * acts[r][...].astype(F32)
+    for g in range(CB):
+        branch = branch + factor[:, g:g + 1] * acts_ref[g].astype(F32)
     out_ref[...] = (hidden_ref[...].astype(F32) + branch.astype(BF).astype(F32)).astype(BF)
 
 
@@ -228,17 +226,13 @@
     second_ref[...] = pltpu.roll(second, 96, 1)[:, 0:64]
 
 
-def finish_sums(recv_ref, swap_ref, flag_ref, block_ref, cross_ref):
+def finish_sums(own_ref, swap_ref, flag_ref, block_ref, cross_ref):
     first = flag_ref[2] == 0
-    recv, swap = recv_ref[:, 16:48, :].astype(F32), swap_ref[:, 16:48, :].astype(F32)
-    low, high = jnp.where(first, recv, swap), jnp.where(first, swap, recv)
-    for s, half in enumerate((low, high)):
-        for t in range(2):
-            at = HALF * (2 * s + t)
-            block_ref[:, at:at + HALF] = half[:, 8 * t:8 * t + 8, :].reshape(BLK, HALF)
-    cross = jnp.concatenate(
-        [jnp.sum(low[:, 16:32, :], axis=0), jnp.sum(high[:, 16:32, :], axis=0)], axis=0
-    )
+    own, swap = own_ref[...].astype(F32), swap_ref[...].astype(F32)
+    low, high = jnp.where(first, own, swap), jnp.where(first, swap, own)
+    block_ref[:, 0:W] = low[0:BLK]
+    block_ref[:, W:BLK] = high[0:BLK]
+    cross = jnp.concatenate([low[BLK:, 0:HALF], high[BLK:, 0:HALF]], axis=0)
     cross_ref[0:32, :] = cross[:, 0:64]
     cross_ref[32:64, :] = pltpu.roll(cross, 64, 1)[:, 0:64]
 
@@ -246,23 +240,8 @@
 PAIR = [(i, i ^ 1) for i in range(CB)]
 
 
-def shift(s):
-    return [(i, (i + 2 * s) % CB) for i in range(CB)]
-
-
-def along(x):
-    return [lax.ppermute(x, "ch", shift(s)) for s in (1, 2, 3)]
-
-
-def across(x, arrived):
-    side = jnp.stack([x] + arrived)
-    return side, lax.ppermute(side, "ch", PAIR)
-
-
 def on_device(layer_input, w_block, w_cross, ch_first, ch_second, gate_gain, gate_bias, cotangent):
-    swap = functools.partial(
-        lax.all_to_all, axis_name="ctx", split_axis=0, concat_axis=0, tiled=True
-    )
+    swap = functools.partial(lax.all_to_all, split_axis=0, concat_axis=0, tiled=True)
     ctx, ch = lax.axis_index("ctx"), lax.axis_index("ch")
     second_sum = (ctx >= 40) & (ctx < 60)
     flag = jnp.stack([ch, ch // 2, ch % 2, second_sum.astype(jnp.int32)]).astype(jnp.int32)
@@ -271,36 +250,34 @@
         pack_cotangent, [((CS + 16, BLK), BF)], cotangent, ch_second.reshape(KCH, CB * CB),
         scratch=[pltpu.VMEM((24, HALF), F32)],
     )
-    x_cols = swap(xt)
-    arrived = along(packed)
+    x_cols = swap(xt, "ctx")
+    cots = lax.all_gather(packed, "ch")
     gain, bias, kron, kront = call(
         prepare,
         [((CS, HALF), F32), ((CS, HALF), F32), ((BLK, BLK), BF), ((BLK, BLK), BF)],
         gate_gain.reshape(1, CS), gate_bias.reshape(1, CS), w_cross,
         scratch=[pltpu.VMEM((HALF, W), F32)],
     )
-    (u_cols,) = call(cross_forward, [((NB, 8, W), BF)], kront, x_cols, after=arrived)
-    u = swap(u_cols)
-    cots = across(packed, arrived)
+    (u_cols,) = call(cross_forward, [((NB, 8, W), BF)], kront, x_cols)
+    u = swap(u_cols, "ctx")
     send, act, hidden, rest, factor = call(
         channel,
         [((NB, 48, HALF), BF), ((CS, BLK), BF), ((CS, BLK), BF), ((CS, BLK), F32), ((CS, HALF), F32)],
-        u, w_block, layer_input, gain, bias, ch_first, *cots, flag,
+        u, w_block, layer_input, gain, bias, ch_first, cotangent, cots, flag,
         smem=(8,),
     )
-    recv = swap(send)
-    arrived = along(act)
-    part, d_input = call(
-        cross_backward, [((72, HALF), F32), ((BLK, W), BF)], recv, x_cols, kron, after=arrived
-    )
-    (total,) = call(add_parts, [((72, HALF), F32)], part, lax.ppermute(part, "ch", PAIR))
+    recv = swap(send, "ctx")
+    acts = lax.all_gather(act, "ch")
+    send, d_input, misc = call(
+        cross_backward, [((72, HALF), F32), ((BLK, W), BF), ((8, HALF), F32)], recv, x_cols, kron,
+    )
     (send,) = call(
-        pack_last, [((NB, 48, HALF), BF)], total, *along(total), part, d_input, flag, smem=(6,)
-    )
-    recv = swap(send)
-    acts = across(act, arrived)
-    (output,) = call(finish_output, [((CS, BLK), BF)], hidden, factor, *acts)
-    swapped = lax.ppermute(recv, "ch", PAIR)
+        pack_last, [((NB, 48, HALF), BF)], lax.all_gather(send, "ch"), misc, d_input, flag, smem=(3,)
+    )
+    recv = swap(send, "ctx")
+    (output,) = call(finish_output, [((CS, BLK), BF)], hidden, factor, acts)
+    (half,) = call(split_last, [((BLK + 16, W), BF)], recv, after=[output])
+    swapped = lax.ppermute(half, "ch", PAIR)
     grad_input, grad_first, grad_second, grad_gain, grad_bias = call(
         finish_input,
         [((CS, BLK), BF), ((1, CS, CS), F32), ((KCH, CB * CB), F32), ((1, CS), F32), ((1, CS), F32)],
@@ -308,7 +285,7 @@
         smem=(2,),
     )
     grad_block, grad_cross = call(
-        finish_sums, [((BLK, BLK), F32), ((NB, NB), F32)], recv, swapped, flag, smem=(2,)
+        finish_sums, [((BLK, BLK), F32), ((NB, NB), F32)], half, swapped, flag, smem=(2,)
     )
     return (
         output,

time: 183 us -> 159 us (0.87)
  starting transfers between devices: 88 us -> 43.6 us
  waiting for transfers between devices: 44.6 us -> 60.9 us
  between operations: 0.93 us -> 14.2 us
  blocking collectives: 29.2 us -> 18.8 us
    ppermute x13 -> x1, starting transfers between devices: 55.8 us -> 4.78 us  [on_device(): swapped = lax.ppermute(half, 'ch', PAIR)]
    all_to_all x3 -> x4, waiting for transfers between devices: 12.1 us -> 60 us  [the longest x2 39.1 us: on_device(): recv = swap(send, 'ctx')]
    ppermute x13 -> x1, waiting for transfers between devices: 32.5 us -> 0.01 us  [on_device(): swapped = lax.ppermute(half, 'ch', PAIR)]
    all_to_all x1 -> x0, blocking collectives: 29.2 us -> none  [on_device(): recv = swap(send)]
    all_gather x0 -> x1, blocking collectives: none -> 18.8 us  [on_device(): lax.all_gather(send, 'ch')]
    all_to_all x3 -> x4, starting transfers between devices: 32.2 us -> 38.8 us  [the longest x2 19.7 us: on_device(): recv = swap(send, 'ctx')]
    unnamed x34 -> x24, local copies, waits for them, and re-layouts: 6.06 us -> 5.49 us
  transfers between devices with their start and end apart: 16 -> 7, of which waited for: 9 -> 5; matrix products, arithmetic and copies ran while one was open for 1% -> 0% of each run, Pallas kernels for 2% -> 5%
where the time goes in v3:
time: 159 us; the launch traced here: 158 us
  waiting for transfers between devices  60.9 us (38%)
  starting transfers between devices  43.6 us (27%)
  blocking collectives  18.8 us (12%)
  between operations  14.2 us (9%)
  Pallas kernels  13.3 us (8%)
  local copies, waits for them, and re-layouts  6.99 us (4%)
    all_to_all x2, waiting for transfers between devices, on_device(): recv = swap(send, 'ctx')  39.1 us
    all_to_all x2, starting transfers between devices, on_device(): recv = swap(send, 'ctx')  19.7 us
    all_gather x1, blocking collectives, on_device(): lax.all_gather(send, 'ch')  18.8 us
    pallas_call x11, Pallas kernels, call(): pl.pallas_call(run, out_shape=[jax.ShapeDtypeStruct(s, d) for s, d in out...  13.3 us
    all_to_all x1, starting transfers between devices, on_device(): x_cols = swap(xt, 'ctx')  12.9 us
    all_to_all x1, waiting for transfers between devices, on_device(): u = swap(u_cols, 'ctx')  10.5 us
    all_to_all x1, waiting for transfers between devices, on_device(): x_cols = swap(xt, 'ctx')  10.4 us
    all_to_all x1, starting transfers between devices, on_device(): u = swap(u_cols, 'ctx')  6.19 us
  transfers between devices with their start and end apart: 7, of which 5 were waited for; matrix products, arithmetic and copies ran while one was open for 0% of the time, Pallas kernels for 5%

profile of v3, /device:TPU:1, one launch (start us, length us, event | category | flops | bytes accessed | tf_op | source)
XLA Modules:
  0.0 157.9 jit_solution(7102499868429242788)
XLA Ops:
  7.2 0.8 copy.18.refs_1_
  8.0 0.9 copy-done.4
  9.0 0.7 shard_map.146
  9.7 1.0 copy-done.2
  10.7 0.8 shard_map.144
  11.5 12.9 %all-to-all-start = ((bf16[64,8,256]{2,1,0:T(8,128)(2,1)}), bf16[64,8,256]{2,1,0:T(8,128)(2,1)S(1)}, u32[]{:S(2)}, u32[]{:S(2)}) async-start(bf16[64,8,256]{2,1,0:T(8,128)(2,1)} %shard_map.144), calls=%async_computation | async-start | bytes 524288 | tf_op jit(solution)/shard_map/all_to_all | solution.py:253
  24.5 0.7 shard_map.143
  25.2 10.4 %all-to-all-done.refs_1_ = bf16[64,8,256]{2,1,0:T(8,128)(2,1)S(1)} async-done(((bf16[64,8,256]{2,1,0:T(8,128)(2,1)}), bf16[64,8,256]{2,1,0:T(8,128)(2,1)S(1)}, u32[]{:S(2)}, u32[]{:S(2)}) %all-to-all-start) | async-done | bytes 262176 | tf_op jit(solution)/shard_map/all_to_all | solution.py:253
  35.6 1.0 shard_map.145
  36.6 6.2 %all-to-all-start.1 = ((bf16[64,8,256]{2,1,0:T(8,128)(2,1)}), bf16[64,8,256]{2,1,0:T(8,128)(2,1)S(1)}, u32[]{:S(2)}, u32[]{:S(2)}) async-start(bf16[64,8,256]{2,1,0:T(8,128)(2,1)} %shard_map.145), calls=%async_computation.1 | async-start | bytes 524288 | tf_op jit(solution)/shard_map/all_to_all | solution.py:262
  42.9 0.1 pad_add_fusion.refs_8_.refs_3_.refs_2_
  42.9 10.5 %all-to-all-done.1.refs_0_ = bf16[64,8,256]{2,1,0:T(8,128)(2,1)S(1)} async-done(((bf16[64,8,256]{2,1,0:T(8,128)(2,1)}), bf16[64,8,256]{2,1,0:T(8,128)(2,1)S(1)}, u32[]{:S(2)}, u32[]{:S(2)}) %all-to-all-start.1) | async-done | bytes 262176 | tf_op jit(solution)/shard_map/all_to_all | solution.py:262
  53.4 0.1 all-gather.6.cloned.1.call-done
  53.6 1.4 copy-done
  54.9 3.4 %shard_map.147 = (bf16[64,48,128]{2,1,0:T(8,128)(2,1)}, bf16[160,512]{1,0:T(8,128)(2,1)}, bf16[160,512]{1,0:T(8,128)(2,1)S(1)}, f32[160,512]{1,0:T(8,128)S(1)}, f32[160,128]{1,0:T(8,128)S(1)}) custom-call(bf16[64,8,256]{2,1,0:T(8,128)(2,1)S(1)} %all-to-all-done.1.refs_0_, bf16[512,512]{1,0:T(8,128)(2,1)S(1)} %copy-done.7, bf16[160,512]{1,0:T(8,128)(2,1)S(1)} %copy-done.3, ...), custom_call_target="tpu_custom_call" | custom-call | tf_op jit(solution)/shard_map/pallas_call | solution.py:49
  58.3 11.9 %all-to-all-start.2 = ((bf16[64,48,128]{2,1,0:T(8,128)(2,1)}), bf16[64,48,128]{2,1,0:T(8,128)(2,1)S(1)}, u32[]{:S(2)}, u32[]{:S(2)}) async-start(bf16[64,48,128]{2,1,0:T(8,128)(2,1)} %get-tuple-element.33), calls=%async_computation.2 | async-start | bytes 1572864 | tf_op jit(solution)/shard_map/all_to_all | solution.py:269
  70.2 0.0 all-gather.8.cloned.1.call-start
  70.3 0.7 all-gather.8.cloned.1.call-update
  71.0 20.4 %all-to-all-done.2.refs_0_ = bf16[64,48,128]{2,1,0:T(8,128)(2,1)S(1)} async-done(((bf16[64,48,128]{2,1,0:T(8,128)(2,1)}), bf16[64,48,128]{2,1,0:T(8,128)(2,1)S(1)}, u32[]{:S(2)}, u32[]{:S(2)}) %all-to-all-start.2) | async-done | bytes 786464 | tf_op jit(solution)/shard_map/all_to_all | solution.py:269
  91.4 1.0 shard_map.149
  92.3 18.8 %all-gather.2 = f32[576,128]{1,0:T(8,128)S(1)} all-gather(f32[72,128]{1,0:T(8,128)S(1)} %get-tuple-element.35), channel_id=4, replica_groups=mesh['ctx'=64,'ch'=8] {'ch'}, dimensions={0}, use_global_device_ids=true | all-gather | bytes 331776 | tf_op jit(solution)/shard_map/all_gather | solution.py:275
  111.1 1.5 shard_map.150
  112.6 7.7 %all-to-all-start.3 = ((bf16[64,48,128]{2,1,0:T(8,128)(2,1)}), bf16[64,48,128]{2,1,0:T(8,128)(2,1)S(1)}, u32[]{:S(2)}, u32[]{:S(2)}) async-start(bf16[64,48,128]{2,1,0:T(8,128)(2,1)} %shard_map.150), calls=%async_computation.3 | async-start | bytes 1572864 | tf_op jit(solution)/shard_map/all_to_all | solution.py:277
  120.4 1.3 copy-done.1
  121.7 1.0 shard_map.148.refs_1_
  122.7 18.7 %all-to-all-done.3.refs_0_ = bf16[64,48,128]{2,1,0:T(8,128)(2,1)S(1)} async-done(((bf16[64,48,128]{2,1,0:T(8,128)(2,1)}), bf16[64,48,128]{2,1,0:T(8,128)(2,1)S(1)}, u32[]{:S(2)}, u32[]{:S(2)}) %all-to-all-start.3) | async-done | bytes 786464 | tf_op jit(solution)/shard_map/all_to_all | solution.py:277
  141.5 0.9 copy-done.6
  142.4 0.1 shard_map.152.refs_0_
  142.5 4.8 %collective-permute-start = (bf16[528,256]{1,0:T(8,128)(2,1)S(1)}, bf16[528,256]{1,0:T(8,128)(2,1)S(1)}, u32[]{:S(2)}, u32[]{:S(2)}) collective-permute-start(bf16[528,256]{1,0:T(8,128)(2,1)S(1)} %shard_map.152.refs_0_), channel_id=1, source_target_pairs={{0,1},{1,0},{2,3},{3,2},{4,5},{5,4},{6,7},{7,6},{8,9},{9,8},{10,11... | collective-permute-start | bytes 811016 | tf_op jit(solution)/shard_map/ppermute | solution.py:280
  147.3 1.4 shard_map.151
  148.7 0.7 copy.19
  149.4 1.6 %shard_map.153 = (f32[512,512]{1,0:T(8,128)}, f32[64,64]{1,0:T(8,128)}) custom-call(bf16[528,256]{1,0:T(8,128)(2,1)S(1)} %shard_map.152.refs_0_, bf16[528,256]{1,0:T(8,128)(2,1)S(1)} %collective-permute-done.refs_1_, s32[4]{0:T(128)S(1)} %pad_add_fusion.refs_8_.refs_3_.refs_2_), custom_call_target="tpu_custom_call" | custom-call | tf_op jit(solution)/shard_map/pallas_call | solution.py:49
  (23 shorter events, 0.1 us)
Async XLA Ops:
  7.2 17.3 %copy-start.11 = (f32[160]{0:T(256)S(1)}, f32[160]{0:T(256)}, u32[]{:S(2)}) copy-start(f32[160]{0:T(256)} %param.14) | copy-start | bytes 1924
  7.2 17.3 %copy-start.10 = (f32[160]{0:T(256)S(1)}, f32[160]{0:T(256)}, u32[]{:S(2)}) copy-start(f32[160]{0:T(256)} %param.13) | copy-start | bytes 1924
  7.2 17.3 %copy-start.9 = (bf16[64,64]{1,0:T(8,128)(2,1)S(1)}, bf16[64,64]{1,0:T(8,128)(2,1)}, u32[]{:S(2)}) copy-start(bf16[64,64]{1,0:T(8,128)(2,1)} %refs_2_.2) | copy-start | bytes 24580
  7.2 46.4 %all-gather.6.cloned.1.call-start = ((), (), s32[]{:S(2)}) async-start(), calls=%async_computation.4 | async-start | bytes 1622016 | tf_op jit(solution)/shard_map/all_gather | solution.py:254
  8.0 0.9 copy-start.4
  9.0 44.6 %copy-start.5 = (bf16[160,512]{1,0:T(8,128)(2,1)S(1)}, bf16[160,512]{1,0:T(8,128)(2,1)}, u32[]{:S(2)}) copy-start(bf16[160,512]{1,0:T(8,128)(2,1)} %refs_6_.1) | copy-start | bytes 491524
  9.0 44.6 %copy-start.8 = (bf16[1,160,160]{2,1,0:T(8,128)(2,1)S(1)}, bf16[1,160,160]{2,1,0:T(8,128)(2,1)}, u32[]{:S(2)}) copy-start(bf16[1,160,160]{2,1,0:T(8,128)(2,1)} %refs_5_.1) | copy-start | bytes 153604
  9.7 43.8 %copy-start.3 = (bf16[160,512]{1,0:T(8,128)(2,1)S(1)}, bf16[160,512]{1,0:T(8,128)(2,1)}, u32[]{:S(2)}) copy-start(bf16[160,512]{1,0:T(8,128)(2,1)} %refs_2_.3) | copy-start | bytes 491524
  9.7 1.0 copy-start.2
  10.7 42.9 %copy-start.7 = (bf16[512,512]{1,0:T(8,128)(2,1)S(1)}, bf16[512,512]{1,0:T(8,128)(2,1)}, u32[]{:S(2)}) copy-start(bf16[512,512]{1,0:T(8,128)(2,1)} %refs_1_.1) | copy-start | bytes 1572868
  11.5 24.1 %all-to-all-start = ((bf16[64,8,256]{2,1,0:T(8,128)(2,1)}), bf16[64,8,256]{2,1,0:T(8,128)(2,1)S(1)}, u32[]{:S(2)}, u32[]{:S(2)}) async-start(bf16[64,8,256]{2,1,0:T(8,128)(2,1)} %shard_map.144), calls=%async_computation | async-start | bytes 524288 | tf_op jit(solution)/shard_map/all_to_all | solution.py:253
  36.6 16.8 %all-to-all-start.1 = ((bf16[64,8,256]{2,1,0:T(8,128)(2,1)}), bf16[64,8,256]{2,1,0:T(8,128)(2,1)S(1)}, u32[]{:S(2)}, u32[]{:S(2)}) async-start(bf16[64,8,256]{2,1,0:T(8,128)(2,1)} %shard_map.145), calls=%async_computation.1 | async-start | bytes 524288 | tf_op jit(solution)/shard_map/all_to_all | solution.py:262
  53.6 1.4 copy-start
  58.3 33.1 %all-to-all-start.2 = ((bf16[64,48,128]{2,1,0:T(8,128)(2,1)}), bf16[64,48,128]{2,1,0:T(8,128)(2,1)S(1)}, u32[]{:S(2)}, u32[]{:S(2)}) async-start(bf16[64,48,128]{2,1,0:T(8,128)(2,1)} %get-tuple-element.33), calls=%async_computation.2 | async-start | bytes 1572864 | tf_op jit(solution)/shard_map/all_to_all | solution.py:269
  70.2 50.1 %all-gather.8.cloned.1.call-start = ((), (), s32[]{:S(2)}) async-start(), calls=%async_computation.5 | async-start | bytes 1474560 | tf_op jit(solution)/shard_map/all_gather | solution.py:270
  112.6 28.9 %all-to-all-start.3 = ((bf16[64,48,128]{2,1,0:T(8,128)(2,1)}), bf16[64,48,128]{2,1,0:T(8,128)(2,1)S(1)}, u32[]{:S(2)}, u32[]{:S(2)}) async-start(bf16[64,48,128]{2,1,0:T(8,128)(2,1)} %shard_map.150), calls=%async_computation.3 | async-start | bytes 1572864 | tf_op jit(solution)/shard_map/all_to_all | solution.py:277
  120.4 1.3 copy-start.1
  141.5 0.9 copy-start.6
  142.5 6.9 %collective-permute-start = (bf16[528,256]{1,0:T(8,128)(2,1)S(1)}, bf16[528,256]{1,0:T(8,128)(2,1)S(1)}, u32[]{:S(2)}, u32[]{:S(2)}) collective-permute-start(bf16[528,256]{1,0:T(8,128)(2,1)S(1)} %shard_map.152.refs_0_), channel_id=1, source_target_pairs={{0,1},{1,0},{2,3},{3,2},{4,5},{5,4},{6,7},{7,6},{8,9},{9,8},{10,11... | collective-permute-start | bytes 811016 | tf_op jit(solution)/shard_map/ppermute | solution.py:280
Sparse Core Ops, SparseCore 0:
  10.2 43.3 all-gather.5
  73.8 35.3 all-gather.7

commit v4 on v3

--- a/solution.py
+++ b/solution.py
@@ -35,9 +35,11 @@
     return jnp.where(cond, 1.0, 0.0).astype(BF)
 
 
-def call(body, out_shapes, *args, scratch=(), smem=(), after=()):
+def call(body, out_shapes, *args, scratch=(), smem=(), far=(), vmem=48, after=()):
     specs = [
-        pl.BlockSpec(memory_space=pltpu.SMEM if at in smem else pltpu.VMEM)
+        pl.BlockSpec(
+            memory_space=pltpu.SMEM if at in smem else pl.ANY if at in far else pltpu.VMEM
+        )
         for at in range(len(args))
     ]
     specs += [pl.BlockSpec(memory_space=pl.ANY) for _ in after]
@@ -52,23 +54,27 @@
         in_specs=specs,
         out_specs=[pl.BlockSpec(memory_space=pltpu.VMEM) for _ in out_shapes],
         scratch_shapes=list(scratch),
-        compiler_params=pltpu.CompilerParams(vmem_limit_bytes=48 * 1024 * 1024),
+        compiler_params=pltpu.CompilerParams(vmem_limit_bytes=vmem * 1024 * 1024),
     )(*args, *after)
 
 
-def transpose_input(x_ref, xt_ref):
-    zeros = jnp.zeros((W - CS, BLK), F32)
-    xt = jnp.concatenate([x_ref[...].astype(F32), zeros], axis=0).T
-    xt_ref[...] = xt.reshape(NB, 8, W).astype(BF)
-
-
-def pack_cotangent(cot_ref, second_ref, out_ref, pad_ref):
-    out_ref[0:CS, :] = cot_ref[...]
+def begin(x_ref, cot_ref, second_ref, xt_ref, out_ref, x_in, cot_in, pad_ref, sems):
+    x_copy = pltpu.make_async_copy(x_ref, x_in, sems.at[0])
+    cot_copy = pltpu.make_async_copy(cot_ref, cot_in, sems.at[1])
+    x_copy.start()
+    cot_copy.start()
     pad_ref[...] = jnp.zeros(pad_ref.shape, F32)
-    pad_ref[0:KCH, 0:64] = second_ref[...].astype(F32)
+    eye = ones_where(iota((KCH, KCH), 0) == iota((KCH, KCH), 1))
+    pad_ref[0:KCH, 0:64] = dot(eye, second_ref[...], NT)
     more = jnp.concatenate([pltpu.roll(pad_ref[16:24, :], 64, 1), jnp.zeros((8, HALF), F32)], axis=0)
     tile = (pad_ref[0:16, :] + more).astype(BF)
     out_ref[CS:CS + 16, :] = jnp.concatenate([tile] * 4, axis=1)
+    x_copy.wait()
+    zeros = jnp.zeros((W - CS, BLK), F32)
+    xt = jnp.concatenate([x_in[...].astype(F32), zeros], axis=0).T
+    xt_ref[...] = xt.reshape(NB, 8, W).astype(BF)
+    cot_copy.wait()
+    out_ref[0:CS, :] = cot_in[...]
 
 
 def prepare(gain_ref, bias_ref, cross_ref, gain_out_ref, bias_out_ref, kron_ref, kront_ref, pad_ref):
@@ -90,7 +96,9 @@
 
 
 def channel(u_ref, block_ref, x_ref, gain_ref, bias_ref, weight_ref, cot_ref,
-            cots_ref, flag_ref, send_ref, act_ref, hidden_ref, rest_ref, factor_ref):
+            far_ref, flag_ref, send_ref, act_ref, hidden_ref, rest_ref, factor_ref, cots_ref, sem):
+    copy = pltpu.make_async_copy(far_ref, cots_ref, sem)
+    copy.start()
     cots = [cots_ref.at[g] for g in range(CB)]
     q = flag_ref[0]
     u = u_ref[...].astype(F32).reshape(BLK, W).astype(BF)
@@ -112,6 +120,7 @@
     slope = 0.5 * (1.0 + curve) + pre * (0.5 * (1.0 - curve * curve)) * (
         root * (1.0 + (3 * 0.044715) * square)
     )
+    copy.wait()
     tiles = jnp.concatenate([cot[CS:CS + 16, 0:HALF].astype(F32) for cot in cots], axis=0).astype(BF)
     k, m = iota((CS, HALF), 0), iota((CS, HALF), 1)
     start = KCH * (m // 16)
@@ -151,7 +160,8 @@
     send_ref[:, 16:48, :] = jnp.concatenate(parts, axis=1).astype(BF)
 
 
-def cross_backward(recv_ref, x_ref, kron_ref, send_ref, d_input_ref, misc_ref):
+def cross_backward(recv_ref, x_ref, kron_ref, act_ref, send_ref, d_input_ref, misc_ref, pass_ref):
+    pass_ref[...] = act_ref[...]
     head = recv_ref[:, 0:16, :].astype(F32)
     low = iota((NB, 8, HALF), 2) < 32
     left, right = head[:, 0:8, :], head[:, 8:16, :]
@@ -201,15 +211,10 @@
     out_ref[BLK:BLK + 16, :] = jnp.concatenate([cross, cross], axis=1).astype(BF)
 
 
-def finish_output(hidden_ref, factor_ref, acts_ref, out_ref):
-    factor = factor_ref[...]
-    branch = jnp.zeros((CS, BLK), F32)
-    for g in range(CB):
-        branch = branch + factor[:, g:g + 1] * acts_ref[g].astype(F32)
-    out_ref[...] = (hidden_ref[...].astype(F32) + branch.astype(BF).astype(F32)).astype(BF)
-
-
-def finish_input(recv_ref, rest_ref, flag_ref, grad_ref, first_ref, second_ref, gain_ref, bias_ref):
+def finish_input(recv_ref, rest_ref, hidden_ref, factor_ref, far_ref, flag_ref,
+                 grad_ref, first_ref, second_ref, gain_ref, bias_ref, out_ref, acts_ref, sem):
+    copy = pltpu.make_async_copy(far_ref, acts_ref, sem)
+    copy.start()
     head = recv_ref[:, 0:16, :].astype(F32)
     left, misc = head[:, 0:8, :], head[:, 8:16, :].reshape(BLK, HALF)
     low = iota((BLK, HALF), 1) < 32
@@ -221,9 +226,14 @@
     rows = misc[CS:CS + W].T
     gain_ref[...] = rows[96:97, 0:CS]
     bias_ref[...] = rows[97:98, 0:CS]
-    pick = ones_where(iota((KCH, CS), 1) == iota((KCH, CS), 0) + KCH * flag_ref[0])
-    second = dot(pick, misc[2 * CS:3 * CS].astype(BF))
-    second_ref[...] = pltpu.roll(second, 96, 1)[:, 0:64]
+    pick = ones_where(iota((CS, KCH), 0) == iota((CS, KCH), 1) + KCH * flag_ref[0])
+    second_ref[...] = dot(misc[2 * CS:3 * CS].astype(BF), pick, TN)[32:96]
+    copy.wait()
+    factor = factor_ref[...]
+    branch = jnp.zeros((CS, BLK), F32)
+    for g in range(CB):
+        branch = branch + factor[:, g:g + 1] * acts_ref[g].astype(F32)
+    out_ref[...] = (hidden_ref[...].astype(F32) + branch.astype(BF).astype(F32)).astype(BF)
 
 
 def finish_sums(own_ref, swap_ref, flag_ref, block_ref, cross_ref):
@@ -245,10 +255,12 @@
     ctx, ch = lax.axis_index("ctx"), lax.axis_index("ch")
     second_sum = (ctx >= 40) & (ctx < 60)
     flag = jnp.stack([ch, ch // 2, ch % 2, second_sum.astype(jnp.int32)]).astype(jnp.int32)
-    (xt,) = call(transpose_input, [((NB, 8, W), BF)], layer_input)
-    (packed,) = call(
-        pack_cotangent, [((CS + 16, BLK), BF)], cotangent, ch_second.reshape(KCH, CB * CB),
-        scratch=[pltpu.VMEM((24, HALF), F32)],
+    xt, packed = call(
+        begin, [((NB, 8, W), BF), ((CS + 16, BLK), BF)],
+        layer_input, cotangent, ch_second.transpose(1, 2, 0).reshape(CB * CB, KCH),
+        scratch=[pltpu.VMEM((CS, BLK), BF), pltpu.VMEM((CS, BLK), BF), pltpu.VMEM((24, HALF), F32),
+                 pltpu.SemaphoreType.DMA((2,))],
+        far=(0, 1), vmem=60,
     )
     x_cols = swap(xt, "ctx")
     cots = lax.all_gather(packed, "ch")
@@ -264,25 +276,29 @@
         channel,
         [((NB, 48, HALF), BF), ((CS, BLK), BF), ((CS, BLK), BF), ((CS, BLK), F32), ((CS, HALF), F32)],
         u, w_block, layer_input, gain, bias, ch_first, cotangent, cots, flag,
-        smem=(8,),
+        scratch=[pltpu.VMEM((CB, CS + 16, BLK), BF), pltpu.SemaphoreType.DMA], smem=(8,), far=(7,),
+        vmem=60,
     )
     recv = swap(send, "ctx")
+    send, d_input, misc, act = call(
+        cross_backward,
+        [((72, HALF), F32), ((BLK, W), BF), ((8, HALF), F32), ((CS, BLK), BF)],
+        recv, x_cols, kron, act,
+    )
     acts = lax.all_gather(act, "ch")
-    send, d_input, misc = call(
-        cross_backward, [((72, HALF), F32), ((BLK, W), BF), ((8, HALF), F32)], recv, x_cols, kron,
-    )
     (send,) = call(
         pack_last, [((NB, 48, HALF), BF)], lax.all_gather(send, "ch"), misc, d_input, flag, smem=(3,)
     )
     recv = swap(send, "ctx")
-    (output,) = call(finish_output, [((CS, BLK), BF)], hidden, factor, acts)
-    (half,) = call(split_last, [((BLK + 16, W), BF)], recv, after=[output])
+    (half,) = call(split_last, [((BLK + 16, W), BF)], recv)
     swapped = lax.ppermute(half, "ch", PAIR)
-    grad_input, grad_first, grad_second, grad_gain, grad_bias = call(
+    grad_input, grad_first, grad_second, grad_gain, grad_bias, output = call(
         finish_input,
-        [((CS, BLK), BF), ((1, CS, CS), F32), ((KCH, CB * CB), F32), ((1, CS), F32), ((1, CS), F32)],
-        recv, rest, flag,
-        smem=(2,),
+        [((CS, BLK), BF), ((1, CS, CS), F32), ((CB * CB, KCH), F32), ((1, CS), F32), ((1, CS), F32),
+         ((CS, BLK), BF)],
+        recv, rest, hidden, factor, acts, flag,
+        scratch=[pltpu.VMEM((CB, CS, BLK), BF), pltpu.SemaphoreType.DMA], smem=(5,), far=(4,),
+        vmem=60, after=[half],
     )
     grad_block, grad_cross = call(
         finish_sums, [((BLK, BLK), F32), ((NB, NB), F32)], half, swapped, flag, smem=(2,)
@@ -293,7 +309,7 @@
         grad_block,
         grad_cross,
         grad_first,
-        grad_second.reshape(KCH, CB, CB),
+        grad_second.reshape(CB, CB, KCH).transpose(2, 0, 1),
         grad_gain.reshape(CS),
         grad_bias.reshape(CS),
     )

time: 159 us -> 156 us (0.981)
  blocking collectives: 18.8 us -> 76.8 us
  waiting for transfers between devices: 60.9 us -> 19.4 us
  starting transfers between devices: 43.6 us -> 24 us
  local copies, waits for them, and re-layouts: 6.99 us -> 3.35 us
  Pallas kernels: 13.3 us -> 16.8 us
    all_to_all x0 -> x2, blocking collectives: none -> 59.3 us  [on_device(): recv = swap(send, 'ctx')]
    all_to_all x2 -> x0, waiting for transfers between devices: 39.1 us -> none  [on_device(): recv = swap(send, 'ctx')]
    all_to_all x2 -> x0, starting transfers between devices: 19.7 us -> none  [on_device(): recv = swap(send, 'ctx')]
    pallas_call x11 -> x9, Pallas kernels: 13.3 us -> 16.8 us  [call(): pl.pallas_call(run, out_shape=[jax.ShapeDtypeStruct(s, d) for s, d in out...]
    all_to_all x1, waiting for transfers between devices: 10.4 us -> 7.13 us  [on_device(): x_cols = swap(xt, 'ctx')]
    unnamed x24 -> x20, local copies, waits for them, and re-layouts: 5.49 us -> 3.35 us
  transfers between devices with their start and end apart: 7 -> 5, of which waited for: 5 -> 4; matrix products, arithmetic and copies ran while one was open for 0% -> 0% of each run, Pallas kernels for 5% -> 3%
where the time goes in v4:
time: 156 us; the launch traced here: 155 us
  blocking collectives  76.8 us (49%)
  starting transfers between devices  24 us (15%)
  waiting for transfers between devices  19.4 us (12%)
  Pallas kernels  16.8 us (11%)
  between operations  14.2 us (9%)
  local copies, waits for them, and re-layouts  3.35 us (2%)
    all_to_all x2, blocking collectives, on_device(): recv = swap(send, 'ctx')  59.3 us
    all_gather x1, blocking collectives, on_device(): lax.all_gather(send, 'ch')  17.5 us
    pallas_call x9, Pallas kernels, call(): pl.pallas_call(run, out_shape=[jax.ShapeDtypeStruct(s, d) for s, d in out...  16.8 us
    all_to_all x1, starting transfers between devices, on_device(): x_cols = swap(xt, 'ctx')  13 us
    all_to_all x1, waiting for transfers between devices, on_device(): u = swap(u_cols, 'ctx')  9.86 us
    all_to_all x1, waiting for transfers between devices, on_device(): x_cols = swap(xt, 'ctx')  7.13 us
    all_to_all x1, starting transfers between devices, on_device(): u = swap(u_cols, 'ctx')  6.17 us
    ppermute x1, starting transfers between devices, on_device(): swapped = lax.ppermute(half, 'ch', PAIR)  4.79 us
  transfers between devices with their start and end apart: 5, of which 4 were waited for; matrix products, arithmetic and copies ran while one was open for 0% of the time, Pallas kernels for 3%

profile of v4, /device:TPU:1, one launch (start us, length us, event | category | flops | bytes accessed | tf_op | source)
XLA Modules:
  0.0 155.0 jit_solution(16423148191363615717)
XLA Ops:
  7.2 0.0 all-gather.6.cloned.1.call-start
  7.2 2.6 %shard_map.144 = (bf16[64,8,256]{2,1,0:T(8,128)(2,1)}, bf16[176,512]{1,0:T(8,128)(2,1)}) custom-call(bf16[160,512]{1,0:T(8,128)(2,1)} %refs_2_.3, bf16[160,512]{1,0:T(8,128)(2,1)} %refs_6_.1, bf16[64,20]{1,0:T(8,128)(2,1)} %bitcast.22), custom_call_target="tpu_custom_call" | custom-call | tf_op jit(solution)/shard_map/pallas_call | solution.py:51
  9.8 0.0 all-gather.6.cloned.1.call-update
  9.8 13.0 %all-to-all-start = ((bf16[64,8,256]{2,1,0:T(8,128)(2,1)}), bf16[64,8,256]{2,1,0:T(8,128)(2,1)S(1)}, u32[]{:S(2)}, u32[]{:S(2)}) async-start(bf16[64,8,256]{2,1,0:T(8,128)(2,1)} %get-tuple-element.32), calls=%async_computation | async-start | bytes 524288 | tf_op jit(solution)/shard_map/all_to_all | solution.py:265
  22.8 0.0 copy-start.5
  22.8 0.7 copy-done.5
  23.5 0.7 copy-done.7
  24.2 0.7 copy-done.8
  24.9 0.7 shard_map.143
  25.5 0.0 copy-start.3
  25.5 0.6 copy-done.3
  26.2 0.6 copy-done.4
  26.8 7.1 %all-to-all-done.refs_1_ = bf16[64,8,256]{2,1,0:T(8,128)(2,1)S(1)} async-done(((bf16[64,8,256]{2,1,0:T(8,128)(2,1)}), bf16[64,8,256]{2,1,0:T(8,128)(2,1)S(1)}, u32[]{:S(2)}, u32[]{:S(2)}) %all-to-all-start) | async-done | bytes 262176 | tf_op jit(solution)/shard_map/all_to_all | solution.py:265
  33.9 1.0 shard_map.145
  34.9 6.2 %all-to-all-start.1 = ((bf16[64,8,256]{2,1,0:T(8,128)(2,1)}), bf16[64,8,256]{2,1,0:T(8,128)(2,1)S(1)}, u32[]{:S(2)}, u32[]{:S(2)}) async-start(bf16[64,8,256]{2,1,0:T(8,128)(2,1)} %shard_map.145), calls=%async_computation.1 | async-start | bytes 524288 | tf_op jit(solution)/shard_map/all_to_all | solution.py:274
  41.1 0.0 all-gather.8.cloned.1.call-start
  41.2 0.6 pad_add_fusion.refs_8_.refs_3_.refs_5_.refs_2_
  41.8 9.9 %all-to-all-done.1.refs_0_ = bf16[64,8,256]{2,1,0:T(8,128)(2,1)S(1)} async-done(((bf16[64,8,256]{2,1,0:T(8,128)(2,1)}), bf16[64,8,256]{2,1,0:T(8,128)(2,1)S(1)}, u32[]{:S(2)}, u32[]{:S(2)}) %all-to-all-start.1) | async-done | bytes 262176 | tf_op jit(solution)/shard_map/all_to_all | solution.py:274
  51.7 1.2 all-gather.6.cloned.1.call-done
  52.9 4.9 %shard_map.146 = (bf16[64,48,128]{2,1,0:T(8,128)(2,1)}, bf16[160,512]{1,0:T(8,128)(2,1)}, bf16[160,512]{1,0:T(8,128)(2,1)}, f32[160,512]{1,0:T(8,128)}, f32[160,128]{1,0:T(8,128)}) custom-call(bf16[64,8,256]{2,1,0:T(8,128)(2,1)} %copy-done.9, bf16[512,512]{1,0:T(8,128)(2,1)} %refs_1_.3, bf16[160,512]{1,0:T(8,128)(2,1)} %refs_2_.3, f32[160,128]{1,0:T(8,128)} %copy-done.3, ...), custom_call_target="tpu_custom_call" | custom-call | tf_op jit(solution)/shard_map/pallas_call | solution.py:51
  57.8 0.0 copy-start.2
  57.8 32.5 %all_to_all.20.refs_0_ = bf16[64,48,128]{2,1,0:T(8,128)(2,1)S(1)} all-to-all(bf16[64,48,128]{2,1,0:T(8,128)(2,1)} %get-tuple-element.36), channel_id=1, replica_groups=mesh['ctx'=64,'ch'=8] {'ctx'}, dimensions={0} | all-to-all | bytes 1572864 | tf_op jit(solution)/shard_map/all_to_all | solution.py:282
  90.4 1.6 %shard_map.147 = (f32[72,128]{1,0:T(8,128)S(1)}, bf16[512,256]{1,0:T(8,128)(2,1)S(1)}, f32[8,128]{1,0:T(8,128)S(1)}, bf16[160,512]{1,0:T(8,128)(2,1)}) custom-call(bf16[64,48,128]{2,1,0:T(8,128)(2,1)S(1)} %all_to_all.20.refs_0_, bf16[64,8,256]{2,1,0:T(8,128)(2,1)S(1)} %all-to-all-done.refs_1_, bf16[512,512]{1,0:T(8,128)(2,1)S(1)} %get-tuple-element.37.refs_2_, ...), custom_call_target="tpu_custom_call" | custom-call | tf_op jit(solution)/shard_map/pallas_call | solution.py:51
  92.0 0.0 all-gather.8.cloned.1.call-update
  92.0 17.5 %all-gather.1 = f32[576,128]{1,0:T(8,128)S(1)} all-gather(f32[72,128]{1,0:T(8,128)S(1)} %get-tuple-element.39), channel_id=3, replica_groups=mesh['ctx'=64,'ch'=8] {'ch'}, dimensions={0}, use_global_device_ids=true | all-gather | bytes 331776 | tf_op jit(solution)/shard_map/all_gather | solution.py:290
  109.4 0.6 shard_map.148
  110.1 26.7 %all_to_all.21.refs_0_ = bf16[64,48,128]{2,1,0:T(8,128)(2,1)S(1)} all-to-all(bf16[64,48,128]{2,1,0:T(8,128)(2,1)S(1)} %shard_map.148), channel_id=1, replica_groups=mesh['ctx'=64,'ch'=8] {'ctx'}, dimensions={0} | all-to-all | bytes 1572864 | tf_op jit(solution)/shard_map/all_to_all | solution.py:292
  136.8 0.1 shard_map.149.refs_6_.refs_0_
  136.9 4.8 %collective-permute-start = (bf16[528,256]{1,0:T(8,128)(2,1)S(1)}, bf16[528,256]{1,0:T(8,128)(2,1)S(1)}, u32[]{:S(2)}, u32[]{:S(2)}) collective-permute-start(bf16[528,256]{1,0:T(8,128)(2,1)S(1)} %shard_map.149.refs_6_.refs_0_), channel_id=1, source_target_pairs={{0,1},{1,0},{2,3},{3,2},{4,5},{5,4},{6,7},{7,6},{8,9},{9,8},{10,11... | collective-permute-start | bytes 811016 | tf_op jit(solution)/shard_map/ppermute | solution.py:294
  141.7 1.2 collective-permute-done.refs_1_
  142.9 1.6 %shard_map.151 = (f32[512,512]{1,0:T(8,128)}, f32[64,64]{1,0:T(8,128)}) custom-call(bf16[528,256]{1,0:T(8,128)(2,1)S(1)} %shard_map.149.refs_6_.refs_0_, bf16[528,256]{1,0:T(8,128)(2,1)S(1)} %collective-permute-done.refs_1_, s32[4]{0:T(128)S(1)} %copy-done.6), custom_call_target="tpu_custom_call" | custom-call | tf_op jit(solution)/shard_map/pallas_call | solution.py:51
  144.5 3.7 %shard_map.150 = (bf16[160,512]{1,0:T(8,128)(2,1)}, f32[1,160,160]{2,1,0:T(8,128)}, f32[64,20]{1,0:T(8,128)}, f32[1,160]{1,0:T(1,128)}, f32[1,160]{1,0:T(1,128)}, /*index=5*/bf16[160,512]{1,0:T(8,128)(2,1)}) custom-call(bf16[64,48,128]{2,1,0:T(8,128)(2,1)} %copy-done, f32[160,512]{1,0:T(8,128)} %get-tuple-element.42.refs_1_, ...), custom_call_target="tpu_custom_call" | custom-call | tf_op jit(solution)/shard_map/pallas_call | solution.py:51
  (13 shorter events, 0.0 us)
Async XLA Ops:
  7.2 45.7 %all-gather.6.cloned.1.call-start = ((), (), s32[]{:S(2)}) async-start(), calls=%async_computation.4 | async-start | bytes 1622016 | tf_op jit(solution)/shard_map/all_gather | solution.py:266
  9.8 24.1 %all-to-all-start = ((bf16[64,8,256]{2,1,0:T(8,128)(2,1)}), bf16[64,8,256]{2,1,0:T(8,128)(2,1)S(1)}, u32[]{:S(2)}, u32[]{:S(2)}) async-start(bf16[64,8,256]{2,1,0:T(8,128)(2,1)} %get-tuple-element.32), calls=%async_computation | async-start | bytes 524288 | tf_op jit(solution)/shard_map/all_to_all | solution.py:265
  22.8 0.7 copy-start.5
  23.5 0.7 copy-start.7
  24.2 0.7 copy-start.8
  25.5 0.6 copy-start.3
  26.2 0.6 copy-start.4
  34.9 16.8 %all-to-all-start.1 = ((bf16[64,8,256]{2,1,0:T(8,128)(2,1)}), bf16[64,8,256]{2,1,0:T(8,128)(2,1)S(1)}, u32[]{:S(2)}, u32[]{:S(2)}) async-start(bf16[64,8,256]{2,1,0:T(8,128)(2,1)} %shard_map.145), calls=%async_computation.1 | async-start | bytes 524288 | tf_op jit(solution)/shard_map/all_to_all | solution.py:274
  41.1 103.4 %all-gather.8.cloned.1.call-start = ((), (), s32[]{:S(2)}) async-start(), calls=%async_computation.5 | async-start | bytes 1474560 | tf_op jit(solution)/shard_map/all_gather | solution.py:288
  51.7 1.2 copy-start.9
  57.8 32.6 %copy-start.2 = (bf16[160,512]{1,0:T(8,128)(2,1)S(1)}, bf16[160,512]{1,0:T(8,128)(2,1)}, u32[]{:S(2)}) copy-start(bf16[160,512]{1,0:T(8,128)(2,1)} %get-tuple-element.38.refs_3_) | copy-start | bytes 491524
  90.4 19.1 %copy-start.6 = (s32[4]{0:T(128)S(1)}, s32[4]{0:T(128)}, u32[]{:S(2)}) copy-start(s32[4]{0:T(128)} %pad_add_fusion.refs_8_.refs_3_.refs_5_.refs_2_) | copy-start | bytes 52
  136.8 7.7 %copy-start = (bf16[64,48,128]{2,1,0:T(8,128)(2,1)}, bf16[64,48,128]{2,1,0:T(8,128)(2,1)S(1)}, u32[]{:S(2)}) copy-start(bf16[64,48,128]{2,1,0:T(8,128)(2,1)S(1)} %all_to_all.21.refs_0_) | copy-start | bytes 2359300
  136.9 7.6 %copy-start.1 = (bf16[528,256]{1,0:T(8,128)(2,1)}, bf16[528,256]{1,0:T(8,128)(2,1)S(1)}, u32[]{:S(2)}) copy-start(bf16[528,256]{1,0:T(8,128)(2,1)S(1)} %shard_map.149.refs_6_.refs_0_) | copy-start | bytes 811012
  136.9 5.9 %collective-permute-start = (bf16[528,256]{1,0:T(8,128)(2,1)S(1)}, bf16[528,256]{1,0:T(8,128)(2,1)S(1)}, u32[]{:S(2)}, u32[]{:S(2)}) collective-permute-start(bf16[528,256]{1,0:T(8,128)(2,1)S(1)} %shard_map.149.refs_6_.refs_0_), channel_id=1, source_target_pairs={{0,1},{1,0},{2,3},{3,2},{4,5},{5,4},{6,7},{7,6},{8,9},{9,8},{10,11... | collective-permute-start | bytes 811016 | tf_op jit(solution)/shard_map/ppermute | solution.py:294
Sparse Core Ops, SparseCore 0:
  10.1 42.7 all-gather.5
  92.1 32.2 all-gather.7

commit v5 on v4

--- a/solution.py
+++ b/solution.py
@@ -95,33 +95,33 @@
     out_ref[...] = dot(kront_ref[...], cols).reshape(NB, 8, W).astype(BF)
 
 
-def channel(u_ref, block_ref, x_ref, gain_ref, bias_ref, weight_ref, cot_ref,
-            far_ref, flag_ref, send_ref, act_ref, hidden_ref, rest_ref, factor_ref, cots_ref, sem):
-    copy = pltpu.make_async_copy(far_ref, cots_ref, sem)
-    copy.start()
-    cots = [cots_ref.at[g] for g in range(CB)]
-    q = flag_ref[0]
+def forward(u_ref, block_ref, x_ref, gain_ref, bias_ref, weight_ref,
+            mixed_ref, gate_ref, hidden_ref, act_ref, slope_ref):
     u = u_ref[...].astype(F32).reshape(BLK, W).astype(BF)
-    mixed = dot(u, block_ref[...], TN)[:CS].astype(BF).astype(F32)
+    mixed = dot(u, block_ref[...], TN)[:CS].astype(BF)
+    mixed_ref[...] = mixed
     x = x_ref[...].astype(F32)
     gain = jnp.concatenate([gain_ref[...]] * 4, axis=1)
     bias = jnp.concatenate([bias_ref[...]] * 4, axis=1)
     gate = jax.nn.sigmoid(x * gain + bias)
-    hidden = (x + gate * mixed).astype(BF)
+    gate_ref[...] = gate
+    hidden = (x + gate * mixed.astype(F32)).astype(BF)
     hidden_ref[...] = hidden
-    weight = weight_ref[0]
-    pre = dot(weight, hidden)
+    pre = dot(weight_ref[0], hidden)
     root = 0.7978845608028654
     square = pre * pre
     curve = jnp.tanh(root * (pre + 0.044715 * (square * pre)))
-    act = (pre * (0.5 * (1.0 + curve))).astype(BF)
-    act_ref[...] = act
-    act = act.astype(F32)
-    slope = 0.5 * (1.0 + curve) + pre * (0.5 * (1.0 - curve * curve)) * (
+    act_ref[...] = (pre * (0.5 * (1.0 + curve))).astype(BF)
+    slope_ref[...] = 0.5 * (1.0 + curve) + pre * (0.5 * (1.0 - curve * curve)) * (
         root * (1.0 + (3 * 0.044715) * square)
     )
-    copy.wait()
-    tiles = jnp.concatenate([cot[CS:CS + 16, 0:HALF].astype(F32) for cot in cots], axis=0).astype(BF)
+
+
+def channel(u_ref, block_ref, x_ref, gain_ref, weight_ref, mixed_ref, gate_ref, hidden_ref, act_ref,
+            slope_ref, cot_ref, cots_ref, flag_ref, send_ref, rest_ref, factor_ref):
+    q = flag_ref[0]
+    act = act_ref[...].astype(F32)
+    tiles = jnp.concatenate([cots_ref[g, CS:CS + 16, 0:HALF].astype(F32) for g in range(CB)], axis=0).astype(BF)
     k, m = iota((CS, HALF), 0), iota((CS, HALF), 1)
     start = KCH * (m // 16)
     low = dot(ones_where(k == start + m % 16), tiles)
@@ -133,19 +133,21 @@
     d_act = jnp.zeros((CS, BLK), F32)
     grad_second = jnp.zeros((CS, HALF), F32)
     for g in range(CB):
-        cot = cots[g][0:CS, :].astype(F32)
+        cot = cots_ref[g, 0:CS, :].astype(F32)
         d_act = d_act + back[:, g:g + 1] * cot
         column = jnp.sum(cot * act, axis=1, keepdims=True)
         grad_second = jnp.where(m == 32 + CB * g + q, column, grad_second)
-    d_pre = (d_act.astype(BF).astype(F32) * slope).astype(BF)
+    d_pre = (d_act.astype(BF).astype(F32) * slope_ref[...]).astype(BF)
     zeros = jnp.zeros((W - CS, BLK), F32)
-    tall = jnp.concatenate([hidden.astype(F32), zeros], axis=0).astype(BF)
+    tall = jnp.concatenate([hidden_ref[...].astype(F32), zeros], axis=0).astype(BF)
     grad_first = dot(d_pre, tall, NT)
-    d_hidden = cot_ref[...].astype(F32) + dot(weight, d_pre, TN)
+    d_hidden = cot_ref[...].astype(F32) + dot(weight_ref[0], d_pre, TN)
+    gate = gate_ref[...]
     d_mixed = jnp.concatenate([d_hidden * gate, zeros], axis=0).astype(BF)
-    d_gate = d_hidden * mixed * gate * (1.0 - gate)
-    grad_gain = jnp.sum(d_gate * x, axis=1, keepdims=True)
+    d_gate = d_hidden * mixed_ref[...].astype(F32) * gate * (1.0 - gate)
+    grad_gain = jnp.sum(d_gate * x_ref[...].astype(F32), axis=1, keepdims=True)
     grad_bias = jnp.sum(d_gate, axis=1, keepdims=True)
+    gain = jnp.concatenate([gain_ref[...]] * 4, axis=1)
     rest_ref[...] = d_hidden + d_gate * gain
     v = dot(block_ref[...], d_mixed, NT)
     left, right = grad_first[:, :HALF], grad_first[:, HALF:]
@@ -155,6 +157,7 @@
     right = jnp.where(iota((BLK, HALF), 1) < 32, v[:, HALF:], misc).reshape(NB, 8, HALF)
     left = v[:, :HALF].reshape(NB, 8, HALF)
     send_ref[:, 0:16, :] = jnp.concatenate([left, right], axis=1).astype(BF)
+    u = u_ref[...].astype(F32).reshape(BLK, W).astype(BF)
     d_block = dot(u, d_mixed, NN)
     parts = [d_block[:, HALF * s:HALF * (s + 1)].reshape(NB, 8, HALF) for s in range(4)]
     send_ref[:, 16:48, :] = jnp.concatenate(parts, axis=1).astype(BF)
@@ -211,10 +214,15 @@
     out_ref[BLK:BLK + 16, :] = jnp.concatenate([cross, cross], axis=1).astype(BF)
 
 
-def finish_input(recv_ref, rest_ref, hidden_ref, factor_ref, far_ref, flag_ref,
-                 grad_ref, first_ref, second_ref, gain_ref, bias_ref, out_ref, acts_ref, sem):
-    copy = pltpu.make_async_copy(far_ref, acts_ref, sem)
-    copy.start()
+def finish_output(hidden_ref, factor_ref, acts_ref, out_ref):
+    factor = factor_ref[...]
+    branch = jnp.zeros((CS, BLK), F32)
+    for g in range(CB):
+        branch = branch + factor[:, g:g + 1] * acts_ref[g].astype(F32)
+    out_ref[...] = (hidden_ref[...].astype(F32) + branch.astype(BF).astype(F32)).astype(BF)
+
+
+def finish_input(recv_ref, rest_ref, flag_ref, grad_ref, first_ref, second_ref, gain_ref, bias_ref):
     head = recv_ref[:, 0:16, :].astype(F32)
     left, misc = head[:, 0:8, :], head[:, 8:16, :].reshape(BLK, HALF)
     low = iota((BLK, HALF), 1) < 32
@@ -228,12 +236,6 @@
     bias_ref[...] = rows[97:98, 0:CS]
     pick = ones_where(iota((CS, KCH), 0) == iota((CS, KCH), 1) + KCH * flag_ref[0])
     second_ref[...] = dot(misc[2 * CS:3 * CS].astype(BF), pick, TN)[32:96]
-    copy.wait()
-    factor = factor_ref[...]
-    branch = jnp.zeros((CS, BLK), F32)
-    for g in range(CB):
-        branch = branch + factor[:, g:g + 1] * acts_ref[g].astype(F32)
-    out_ref[...] = (hidden_ref[...].astype(F32) + branch.astype(BF).astype(F32)).astype(BF)
 
 
 def finish_sums(own_ref, swap_ref, flag_ref, block_ref, cross_ref):
@@ -272,12 +274,15 @@
     )
     (u_cols,) = call(cross_forward, [((NB, 8, W), BF)], kront, x_cols)
     u = swap(u_cols, "ctx")
-    send, act, hidden, rest, factor = call(
-        channel,
-        [((NB, 48, HALF), BF), ((CS, BLK), BF), ((CS, BLK), BF), ((CS, BLK), F32), ((CS, HALF), F32)],
-        u, w_block, layer_input, gain, bias, ch_first, cotangent, cots, flag,
-        scratch=[pltpu.VMEM((CB, CS + 16, BLK), BF), pltpu.SemaphoreType.DMA], smem=(8,), far=(7,),
-        vmem=60,
+    wide = (CS, BLK)
+    mixed, gate, hidden, act, slope = call(
+        forward, [(wide, BF), (wide, F32), (wide, BF), (wide, BF), (wide, F32)],
+        u, w_block, layer_input, gain, bias, ch_first,
+    )
+    send, rest, factor = call(
+        channel, [((NB, 48, HALF), BF), (wide, F32), ((CS, HALF), F32)],
+        u, w_block, layer_input, gain, ch_first, mixed, gate, hidden, act, slope, cotangent, cots, flag,
+        smem=(12,),
     )
     recv = swap(send, "ctx")
     send, d_input, misc, act = call(
@@ -292,14 +297,13 @@
     recv = swap(send, "ctx")
     (half,) = call(split_last, [((BLK + 16, W), BF)], recv)
     swapped = lax.ppermute(half, "ch", PAIR)
-    grad_input, grad_first, grad_second, grad_gain, grad_bias, output = call(
+    grad_input, grad_first, grad_second, grad_gain, grad_bias = call(
         finish_input,
-        [((CS, BLK), BF), ((1, CS, CS), F32), ((CB * CB, KCH), F32), ((1, CS), F32), ((1, CS), F32),
-         ((CS, BLK), BF)],
-        recv, rest, hidden, factor, acts, flag,
-        scratch=[pltpu.VMEM((CB, CS, BLK), BF), pltpu.SemaphoreType.DMA], smem=(5,), far=(4,),
-        vmem=60, after=[half],
-    )
+        [((CS, BLK), BF), ((1, CS, CS), F32), ((CB * CB, KCH), F32), ((1, CS), F32), ((1, CS), F32)],
+        recv, rest, flag,
+        smem=(2,),
+    )
+    (output,) = call(finish_output, [((CS, BLK), BF)], hidden, factor, acts, after=[half])
     grad_block, grad_cross = call(
         finish_sums, [((BLK, BLK), F32), ((NB, NB), F32)], half, swapped, flag, smem=(2,)
     )

time: 156 us -> 153 us (0.981)
  Pallas kernels: 16.8 us -> 13.3 us
  blocking collectives: 76.8 us -> 75.2 us
    pallas_call x9 -> x11, Pallas kernels: 16.8 us -> 13.3 us  [call(): pl.pallas_call(run, out_shape=[jax.ShapeDtypeStruct(s, d) for s, d in out...]
    unnamed x20 -> x22, local copies, waits for them, and re-layouts: 3.35 us -> 4.81 us
  transfers between devices with their start and end apart: 5 -> 5, of which waited for: 4 -> 3; matrix products, arithmetic and copies ran while one was open for 0% -> 0% of each run, Pallas kernels for 3% -> 4%
where the time goes in v5:
time: 153 us; the launch traced here: 152 us
  blocking collectives  75.2 us (49%)
  starting transfers between devices  24 us (16%)
  waiting for transfers between devices  20.5 us (13%)
  between operations  14.2 us (9%)
  Pallas kernels  13.3 us (9%)
  local copies, waits for them, and re-layouts  4.81 us (3%)
    all_to_all x2, blocking collectives, on_device(): recv = swap(send, 'ctx')  57.7 us
    all_gather x1, blocking collectives, on_device(): lax.all_gather(send, 'ch')  17.5 us
    pallas_call x11, Pallas kernels, call(): pl.pallas_call(run, out_shape=[jax.ShapeDtypeStruct(s, d) for s, d in out...  13.3 us
    all_to_all x1, starting transfers between devices, on_device(): x_cols = swap(xt, 'ctx')  12.9 us
    all_to_all x1, waiting for transfers between devices, on_device(): u = swap(u_cols, 'ctx')  10.4 us
    all_to_all x1, waiting for transfers between devices, on_device(): x_cols = swap(xt, 'ctx')  8.33 us
    all_to_all x1, starting transfers between devices, on_device(): u = swap(u_cols, 'ctx')  6.19 us
    unnamed x22, local copies, waits for them, and re-layouts  4.81 us
  transfers between devices with their start and end apart: 5, of which 3 were waited for; matrix products, arithmetic and copies ran while one was open for 0% of the time, Pallas kernels for 4%

profile of v5, /device:TPU:1, one launch (start us, length us, event | category | flops | bytes accessed | tf_op | source)
XLA Modules:
  0.0 152.1 jit_solution(5041253668807268129)
XLA Ops:
  7.2 0.0 all-gather.6.cloned.1.call-start
  7.2 2.6 %shard_map.144 = (bf16[64,8,256]{2,1,0:T(8,128)(2,1)}, bf16[176,512]{1,0:T(8,128)(2,1)}) custom-call(bf16[160,512]{1,0:T(8,128)(2,1)} %refs_2_.5, bf16[160,512]{1,0:T(8,128)(2,1)} %refs_10_.1, bf16[64,20]{1,0:T(8,128)(2,1)} %bitcast.22), custom_call_target="tpu_custom_call" | custom-call | tf_op jit(solution)/shard_map/pallas_call | solution.py:51
  9.9 0.0 all-gather.6.cloned.1.call-update
  9.9 12.9 %all-to-all-start = ((bf16[64,8,256]{2,1,0:T(8,128)(2,1)}), bf16[64,8,256]{2,1,0:T(8,128)(2,1)S(1)}, u32[]{:S(2)}, u32[]{:S(2)}) async-start(bf16[64,8,256]{2,1,0:T(8,128)(2,1)} %get-tuple-element.34), calls=%async_computation | async-start | bytes 524288 | tf_op jit(solution)/shard_map/all_to_all | solution.py:267
  22.9 0.0 copy-start.4
  22.9 0.0 copy-start.8
  22.9 0.7 copy-done.8
  23.6 0.7 copy-done.9
  24.3 0.7 copy-done.10
  25.0 0.7 shard_map.143
  25.7 8.3 %all-to-all-done.refs_1_ = bf16[64,8,256]{2,1,0:T(8,128)(2,1)S(1)} async-done(((bf16[64,8,256]{2,1,0:T(8,128)(2,1)}), bf16[64,8,256]{2,1,0:T(8,128)(2,1)S(1)}, u32[]{:S(2)}, u32[]{:S(2)}) %all-to-all-start) | async-done | bytes 262176 | tf_op jit(solution)/shard_map/all_to_all | solution.py:267
  34.0 1.0 shard_map.145
  35.0 6.2 %all-to-all-start.1 = ((bf16[64,8,256]{2,1,0:T(8,128)(2,1)}), bf16[64,8,256]{2,1,0:T(8,128)(2,1)S(1)}, u32[]{:S(2)}, u32[]{:S(2)}) async-start(bf16[64,8,256]{2,1,0:T(8,128)(2,1)} %shard_map.145), calls=%async_computation.1 | async-start | bytes 524288 | tf_op jit(solution)/shard_map/all_to_all | solution.py:276
  41.2 0.0 all-gather.8.cloned.1.call-start
  41.3 0.1 pad_add_fusion.refs_12_.refs_3_.refs_2_
  41.4 10.4 %all-to-all-done.1.refs_0_ = bf16[64,8,256]{2,1,0:T(8,128)(2,1)S(1)} async-done(((bf16[64,8,256]{2,1,0:T(8,128)(2,1)}), bf16[64,8,256]{2,1,0:T(8,128)(2,1)S(1)}, u32[]{:S(2)}, u32[]{:S(2)}) %all-to-all-start.1) | async-done | bytes 262176 | tf_op jit(solution)/shard_map/all_to_all | solution.py:276
  51.8 0.7 shard_map.146
  52.5 1.7 %all-gather.6.cloned.1.call-done = bf16[1408,512]{1,0:T(8,128)(2,1)} async-done(((bf16[176,512]{1,0:T(8,128)(2,1)}), bf16[1408,512]{1,0:T(8,128)(2,1)}) %all-gather.6.cloned.1.call-update) | async-done | bytes 1441808 | tf_op jit(solution)/shard_map/all_gather | solution.py:268
  54.1 1.4 copy-done.2
  55.5 2.0 %shard_map.147 = (bf16[64,48,128]{2,1,0:T(8,128)(2,1)S(1)}, f32[160,512]{1,0:T(8,128)S(1)}, f32[160,128]{1,0:T(8,128)S(1)}) custom-call(bf16[64,8,256]{2,1,0:T(8,128)(2,1)S(1)} %all-to-all-done.1.refs_0_, bf16[512,512]{1,0:T(8,128)(2,1)S(1)} %copy-done, bf16[160,512]{1,0:T(8,128)(2,1)S(1)} %copy-done.1, f32[160,128]{1,0:T(8,128)S(1)} %get-tuple-element.35.refs_3_, ...), custom_call_target="tpu_custom_call" | custom-call | tf_op jit(solution)/shard_map/pallas_call | solution.py:51
  57.5 31.0 %all_to_all.20.refs_0_ = bf16[64,48,128]{2,1,0:T(8,128)(2,1)S(1)} all-to-all(bf16[64,48,128]{2,1,0:T(8,128)(2,1)S(1)} %get-tuple-element.44), channel_id=1, replica_groups=mesh['ctx'=64,'ch'=8] {'ctx'}, dimensions={0} | all-to-all | bytes 1572864 | tf_op jit(solution)/shard_map/all_to_all | solution.py:287
  88.5 1.6 %shard_map.148 = (f32[72,128]{1,0:T(8,128)S(1)}, bf16[512,256]{1,0:T(8,128)(2,1)S(1)}, f32[8,128]{1,0:T(8,128)S(1)}, bf16[160,512]{1,0:T(8,128)(2,1)}) custom-call(bf16[64,48,128]{2,1,0:T(8,128)(2,1)S(1)} %all_to_all.20.refs_0_, bf16[64,8,256]{2,1,0:T(8,128)(2,1)S(1)} %all-to-all-done.refs_1_, bf16[512,512]{1,0:T(8,128)(2,1)S(1)} %get-tuple-element.45.refs_2_, ...), custom_call_target="tpu_custom_call" | custom-call | tf_op jit(solution)/shard_map/pallas_call | solution.py:51
  90.0 0.0 all-gather.8.cloned.1.call-update
  90.0 17.5 %all-gather.2 = f32[576,128]{1,0:T(8,128)S(1)} all-gather(f32[72,128]{1,0:T(8,128)S(1)} %get-tuple-element.47), channel_id=4, replica_groups=mesh['ctx'=64,'ch'=8] {'ch'}, dimensions={0}, use_global_device_ids=true | all-gather | bytes 331776 | tf_op jit(solution)/shard_map/all_gather | solution.py:295
  107.5 0.6 shard_map.149
  108.1 26.8 %all_to_all.21.refs_0_ = bf16[64,48,128]{2,1,0:T(8,128)(2,1)S(1)} all-to-all(bf16[64,48,128]{2,1,0:T(8,128)(2,1)S(1)} %shard_map.149), channel_id=1, replica_groups=mesh['ctx'=64,'ch'=8] {'ctx'}, dimensions={0} | all-to-all | bytes 1572864 | tf_op jit(solution)/shard_map/all_to_all | solution.py:297
  134.9 0.1 shard_map.150.refs_3_.refs_0_
  135.0 4.8 %collective-permute-start = (bf16[528,256]{1,0:T(8,128)(2,1)S(1)}, bf16[528,256]{1,0:T(8,128)(2,1)S(1)}, u32[]{:S(2)}, u32[]{:S(2)}) collective-permute-start(bf16[528,256]{1,0:T(8,128)(2,1)S(1)} %shard_map.150.refs_3_.refs_0_), channel_id=1, source_target_pairs={{0,1},{1,0},{2,3},{3,2},{4,5},{5,4},{6,7},{7,6},{8,9},{9,8},{10,11... | collective-permute-start | bytes 811016 | tf_op jit(solution)/shard_map/ppermute | solution.py:299
  139.8 1.4 shard_map.152
  141.2 1.6 %shard_map.153 = (f32[512,512]{1,0:T(8,128)}, f32[64,64]{1,0:T(8,128)}) custom-call(bf16[528,256]{1,0:T(8,128)(2,1)S(1)} %shard_map.150.refs_3_.refs_0_, bf16[528,256]{1,0:T(8,128)(2,1)S(1)} %collective-permute-done.refs_1_, s32[4]{0:T(128)S(1)} %pad_add_fusion.refs_12_.refs_3_.refs_2_), custom_call_target="tpu_custom_call" | custom-call | tf_op jit(solution)/shard_map/pallas_call | solution.py:51
  142.9 1.3 copy-done.3
  144.2 1.0 shard_map.151
  (17 shorter events, 0.0 us)
Async XLA Ops:
  7.2 44.6 %copy-start.1 = (bf16[160,512]{1,0:T(8,128)(2,1)S(1)}, bf16[160,512]{1,0:T(8,128)(2,1)}, u32[]{:S(2)}) copy-start(bf16[160,512]{1,0:T(8,128)(2,1)} %refs_2_.5) | copy-start | bytes 491524
  7.2 44.6 %copy-start.5 = (bf16[1,160,160]{2,1,0:T(8,128)(2,1)S(1)}, bf16[1,160,160]{2,1,0:T(8,128)(2,1)}, u32[]{:S(2)}) copy-start(bf16[1,160,160]{2,1,0:T(8,128)(2,1)} %refs_4_.1) | copy-start | bytes 153604
  7.2 44.6 %copy-start = (bf16[512,512]{1,0:T(8,128)(2,1)S(1)}, bf16[512,512]{1,0:T(8,128)(2,1)}, u32[]{:S(2)}) copy-start(bf16[512,512]{1,0:T(8,128)(2,1)} %refs_1_.5) | copy-start | bytes 1572868
  7.2 46.9 %all-gather.6.cloned.1.call-start = ((), (), s32[]{:S(2)}) async-start(), calls=%async_computation.4 | async-start | bytes 1622016 | tf_op jit(solution)/shard_map/all_gather | solution.py:268
  9.9 24.1 %all-to-all-start = ((bf16[64,8,256]{2,1,0:T(8,128)(2,1)}), bf16[64,8,256]{2,1,0:T(8,128)(2,1)S(1)}, u32[]{:S(2)}, u32[]{:S(2)}) async-start(bf16[64,8,256]{2,1,0:T(8,128)(2,1)} %get-tuple-element.34), calls=%async_computation | async-start | bytes 524288 | tf_op jit(solution)/shard_map/all_to_all | solution.py:267
  22.9 31.3 %copy-start.4 = (bf16[160,512]{1,0:T(8,128)(2,1)S(1)}, bf16[160,512]{1,0:T(8,128)(2,1)}, u32[]{:S(2)}) copy-start(bf16[160,512]{1,0:T(8,128)(2,1)} %refs_10_.1) | copy-start | bytes 491524
  22.9 0.8 copy-start.8
  23.6 0.7 copy-start.9
  24.3 0.7 copy-start.10
  35.0 16.8 %all-to-all-start.1 = ((bf16[64,8,256]{2,1,0:T(8,128)(2,1)}), bf16[64,8,256]{2,1,0:T(8,128)(2,1)S(1)}, u32[]{:S(2)}, u32[]{:S(2)}) async-start(bf16[64,8,256]{2,1,0:T(8,128)(2,1)} %shard_map.145), calls=%async_computation.1 | async-start | bytes 524288 | tf_op jit(solution)/shard_map/all_to_all | solution.py:276
  41.2 101.7 %all-gather.8.cloned.1.call-start = ((), (), s32[]{:S(2)}) async-start(), calls=%async_computation.5 | async-start | bytes 1474560 | tf_op jit(solution)/shard_map/all_gather | solution.py:293
  54.1 1.4 copy-start.2
  57.5 32.5 %copy-start.6 = (f32[160,128]{1,0:T(8,128)}, f32[160,128]{1,0:T(8,128)S(1)}, u32[]{:S(2)}) copy-start(f32[160,128]{1,0:T(8,128)S(1)} %get-tuple-element.43.refs_1_) | copy-start | bytes 245764
  134.9 8.0 %copy-start.7 = (f32[160,128]{1,0:T(8,128)S(1)}, f32[160,128]{1,0:T(8,128)}, u32[]{:S(2)}) copy-start(f32[160,128]{1,0:T(8,128)} %copy-done.6) | copy-start | bytes 245764
  135.0 6.2 %collective-permute-start = (bf16[528,256]{1,0:T(8,128)(2,1)S(1)}, bf16[528,256]{1,0:T(8,128)(2,1)S(1)}, u32[]{:S(2)}, u32[]{:S(2)}) collective-permute-start(bf16[528,256]{1,0:T(8,128)(2,1)S(1)} %shard_map.150.refs_3_.refs_0_), channel_id=1, source_target_pairs={{0,1},{1,0},{2,3},{3,2},{4,5},{5,4},{6,7},{7,6},{8,9},{9,8},{10,11... | collective-permute-start | bytes 811016 | tf_op jit(solution)/shard_map/ppermute | solution.py:299
  142.9 1.3 copy-start.3
Sparse Core Ops, SparseCore 0:
  10.2 43.9 all-gather.5
  90.2 31.9 all-gather.7

commit v6 on v5

--- a/solution.py
+++ b/solution.py
@@ -58,23 +58,26 @@
     )(*args, *after)
 
 
-def begin(x_ref, cot_ref, second_ref, xt_ref, out_ref, x_in, cot_in, pad_ref, sems):
-    x_copy = pltpu.make_async_copy(x_ref, x_in, sems.at[0])
-    cot_copy = pltpu.make_async_copy(cot_ref, cot_in, sems.at[1])
-    x_copy.start()
-    cot_copy.start()
+def pack_cotangent(cot_ref, second_ref, out_ref, cot_in, pad_ref, sem):
+    copy = pltpu.make_async_copy(cot_ref, cot_in, sem)
+    copy.start()
     pad_ref[...] = jnp.zeros(pad_ref.shape, F32)
     eye = ones_where(iota((KCH, KCH), 0) == iota((KCH, KCH), 1))
     pad_ref[0:KCH, 0:64] = dot(eye, second_ref[...], NT)
     more = jnp.concatenate([pltpu.roll(pad_ref[16:24, :], 64, 1), jnp.zeros((8, HALF), F32)], axis=0)
     tile = (pad_ref[0:16, :] + more).astype(BF)
     out_ref[CS:CS + 16, :] = jnp.concatenate([tile] * 4, axis=1)
-    x_copy.wait()
+    copy.wait()
+    out_ref[0:CS, :] = cot_in[...]
+
+
+def transpose_input(x_ref, xt_ref, x_in, sem):
+    copy = pltpu.make_async_copy(x_ref, x_in, sem)
+    copy.start()
+    copy.wait()
     zeros = jnp.zeros((W - CS, BLK), F32)
     xt = jnp.concatenate([x_in[...].astype(F32), zeros], axis=0).T
     xt_ref[...] = xt.reshape(NB, 8, W).astype(BF)
-    cot_copy.wait()
-    out_ref[0:CS, :] = cot_in[...]
 
 
 def prepare(gain_ref, bias_ref, cross_ref, gain_out_ref, bias_out_ref, kron_ref, kront_ref, pad_ref):
@@ -257,12 +260,16 @@
     ctx, ch = lax.axis_index("ctx"), lax.axis_index("ch")
     second_sum = (ctx >= 40) & (ctx < 60)
     flag = jnp.stack([ch, ch // 2, ch % 2, second_sum.astype(jnp.int32)]).astype(jnp.int32)
-    xt, packed = call(
-        begin, [((NB, 8, W), BF), ((CS + 16, BLK), BF)],
-        layer_input, cotangent, ch_second.transpose(1, 2, 0).reshape(CB * CB, KCH),
-        scratch=[pltpu.VMEM((CS, BLK), BF), pltpu.VMEM((CS, BLK), BF), pltpu.VMEM((24, HALF), F32),
-                 pltpu.SemaphoreType.DMA((2,))],
-        far=(0, 1), vmem=60,
+    (packed,) = call(
+        pack_cotangent, [((CS + 16, BLK), BF)],
+        cotangent, ch_second.transpose(1, 2, 0).reshape(CB * CB, KCH),
+        scratch=[pltpu.VMEM((CS, BLK), BF), pltpu.VMEM((24, HALF), F32), pltpu.SemaphoreType.DMA],
+        far=(0,), vmem=60,
+    )
+    (xt,) = call(
+        transpose_input, [((NB, 8, W), BF)], layer_input,
+        scratch=[pltpu.VMEM((CS, BLK), BF), pltpu.SemaphoreType.DMA],
+        far=(0,), vmem=60, after=[packed],
     )
     x_cols = swap(xt, "ctx")
     cots = lax.all_gather(packed, "ch")

time: 153 us -> 155 us (1.013)
  blocking collectives: 75.2 us -> 77.3 us
  local copies, waits for them, and re-layouts: 4.81 us -> 2.72 us
  Pallas kernels: 13.3 us -> 14.9 us
    unnamed x22, local copies, waits for them, and re-layouts: 4.81 us -> 2.72 us
    all_to_all x1, waiting for transfers between devices: 8.33 us -> 10.4 us  [on_device(): x_cols = swap(xt, 'ctx')]
    all_gather x1, waiting for transfers between devices: 1.69 us -> 0.02 us  [on_device(): cots = lax.all_gather(packed, 'ch')]
    all_to_all x2, blocking collectives: 57.7 us -> 59.4 us  [on_device(): recv = swap(send, 'ctx')]
    pallas_call x11 -> x12, Pallas kernels: 13.3 us -> 14.9 us  [call(): pl.pallas_call(run, out_shape=[jax.ShapeDtypeStruct(s, d) for s, d in out...]
  transfers between devices with their start and end apart: 5 -> 5, of which waited for: 3 -> 2; matrix products, arithmetic and copies ran while one was open for 0% -> 0% of each run, Pallas kernels for 4% -> 5%
where the time goes in v6:
time: 155 us; the launch traced here: 154 us
  blocking collectives  77.3 us (50%)
  starting transfers between devices  24 us (15%)
  waiting for transfers between devices  20.9 us (13%)
  Pallas kernels  14.9 us (10%)
  between operations  14.3 us (9%)
  local copies, waits for them, and re-layouts  2.72 us (2%)
    all_to_all x2, blocking collectives, on_device(): recv = swap(send, 'ctx')  59.4 us
    all_gather x1, blocking collectives, on_device(): lax.all_gather(send, 'ch')  17.9 us
    pallas_call x12, Pallas kernels, call(): pl.pallas_call(run, out_shape=[jax.ShapeDtypeStruct(s, d) for s, d in out...  14.9 us
    all_to_all x1, starting transfers between devices, on_device(): x_cols = swap(xt, 'ctx')  12.9 us
    all_to_all x1, waiting for transfers between devices, on_device(): u = swap(u_cols, 'ctx')  10.4 us
    all_to_all x1, waiting for transfers between devices, on_device(): x_cols = swap(xt, 'ctx')  10.4 us
    all_to_all x1, starting transfers between devices, on_device(): u = swap(u_cols, 'ctx')  6.19 us
    ppermute x1, starting transfers between devices, on_device(): swapped = lax.ppermute(half, 'ch', PAIR)  4.78 us
  transfers between devices with their start and end apart: 5, of which 2 were waited for; matrix products, arithmetic and copies ran while one was open for 0% of the time, Pallas kernels for 5%

profile of v6, /device:TPU:1, one launch (start us, length us, event | category | flops | bytes accessed | tf_op | source)
XLA Modules:
  0.0 154.1 jit_solution(11481420821402826421)
XLA Ops:
  7.2 0.0 all-gather.6.cloned.1.call-start
  7.2 2.3 %shard_map.144.refs_1_ = bf16[176,512]{1,0:T(8,128)(2,1)} custom-call(bf16[160,512]{1,0:T(8,128)(2,1)} %refs_10_.1, bf16[64,20]{1,0:T(8,128)(2,1)} %bitcast.22), custom_call_target="tpu_custom_call" | custom-call | tf_op jit(solution)/shard_map/pallas_call | solution.py:51
  9.6 0.0 all-gather.6.cloned.1.call-update
  9.6 0.0 copy-start
  9.6 0.0 copy-start.1
  9.6 0.0 copy-start.5
  9.7 1.8 %shard_map.145 = bf16[64,8,256]{2,1,0:T(8,128)(2,1)} custom-call(bf16[160,512]{1,0:T(8,128)(2,1)} %refs_2_.5, bf16[176,512]{1,0:T(8,128)(2,1)} %shard_map.144.refs_1_), custom_call_target="tpu_custom_call" | custom-call | tf_op jit(solution)/shard_map/pallas_call | solution.py:51
  11.5 12.9 %all-to-all-start = ((bf16[64,8,256]{2,1,0:T(8,128)(2,1)}), bf16[64,8,256]{2,1,0:T(8,128)(2,1)S(1)}, u32[]{:S(2)}, u32[]{:S(2)}) async-start(bf16[64,8,256]{2,1,0:T(8,128)(2,1)} %shard_map.145), calls=%async_computation | async-start | bytes 524288 | tf_op jit(solution)/shard_map/all_to_all | solution.py:274
  24.4 0.0 copy-start.4
  24.5 0.7 shard_map.143
  25.2 10.4 %all-to-all-done.refs_1_ = bf16[64,8,256]{2,1,0:T(8,128)(2,1)S(1)} async-done(((bf16[64,8,256]{2,1,0:T(8,128)(2,1)}), bf16[64,8,256]{2,1,0:T(8,128)(2,1)S(1)}, u32[]{:S(2)}, u32[]{:S(2)}) %all-to-all-start) | async-done | bytes 262176 | tf_op jit(solution)/shard_map/all_to_all | solution.py:274
  35.6 1.0 shard_map.146
  36.6 6.2 %all-to-all-start.1 = ((bf16[64,8,256]{2,1,0:T(8,128)(2,1)}), bf16[64,8,256]{2,1,0:T(8,128)(2,1)S(1)}, u32[]{:S(2)}, u32[]{:S(2)}) async-start(bf16[64,8,256]{2,1,0:T(8,128)(2,1)} %shard_map.146), calls=%async_computation.1 | async-start | bytes 524288 | tf_op jit(solution)/shard_map/all_to_all | solution.py:283
  42.8 0.0 all-gather.8.cloned.1.call-start
  42.9 0.1 pad_add_fusion.refs_12_.refs_3_.refs_2_
  42.9 10.4 %all-to-all-done.1.refs_0_ = bf16[64,8,256]{2,1,0:T(8,128)(2,1)S(1)} async-done(((bf16[64,8,256]{2,1,0:T(8,128)(2,1)}), bf16[64,8,256]{2,1,0:T(8,128)(2,1)S(1)}, u32[]{:S(2)}, u32[]{:S(2)}) %all-to-all-start.1) | async-done | bytes 262176 | tf_op jit(solution)/shard_map/all_to_all | solution.py:283
  53.4 0.7 shard_map.147
  54.0 0.0 all-gather.6.cloned.1.call-done
  54.1 1.4 copy-done.2
  55.4 2.0 %shard_map.148 = (bf16[64,48,128]{2,1,0:T(8,128)(2,1)S(1)}, f32[160,512]{1,0:T(8,128)S(1)}, f32[160,128]{1,0:T(8,128)S(1)}) custom-call(bf16[64,8,256]{2,1,0:T(8,128)(2,1)S(1)} %all-to-all-done.1.refs_0_, bf16[512,512]{1,0:T(8,128)(2,1)S(1)} %copy-done, bf16[160,512]{1,0:T(8,128)(2,1)S(1)} %copy-done.1, f32[160,128]{1,0:T(8,128)S(1)} %get-tuple-element.32.refs_3_, ...), custom_call_target="tpu_custom_call" | custom-call | tf_op jit(solution)/shard_map/pallas_call | solution.py:51
  57.4 32.5 %all_to_all.20.refs_0_ = bf16[64,48,128]{2,1,0:T(8,128)(2,1)S(1)} all-to-all(bf16[64,48,128]{2,1,0:T(8,128)(2,1)S(1)} %get-tuple-element.40), channel_id=1, replica_groups=mesh['ctx'=64,'ch'=8] {'ctx'}, dimensions={0} | all-to-all | bytes 1572864 | tf_op jit(solution)/shard_map/all_to_all | solution.py:294
  89.9 1.6 %shard_map.149 = (f32[72,128]{1,0:T(8,128)S(1)}, bf16[512,256]{1,0:T(8,128)(2,1)S(1)}, f32[8,128]{1,0:T(8,128)S(1)}, bf16[160,512]{1,0:T(8,128)(2,1)}) custom-call(bf16[64,48,128]{2,1,0:T(8,128)(2,1)S(1)} %all_to_all.20.refs_0_, bf16[64,8,256]{2,1,0:T(8,128)(2,1)S(1)} %all-to-all-done.refs_1_, bf16[512,512]{1,0:T(8,128)(2,1)S(1)} %get-tuple-element.41.refs_2_, ...), custom_call_target="tpu_custom_call" | custom-call | tf_op jit(solution)/shard_map/pallas_call | solution.py:51
  91.5 0.0 all-gather.8.cloned.1.call-update
  91.5 17.9 %all-gather.2 = f32[576,128]{1,0:T(8,128)S(1)} all-gather(f32[72,128]{1,0:T(8,128)S(1)} %get-tuple-element.43), channel_id=4, replica_groups=mesh['ctx'=64,'ch'=8] {'ch'}, dimensions={0}, use_global_device_ids=true | all-gather | bytes 331776 | tf_op jit(solution)/shard_map/all_gather | solution.py:302
  109.4 0.6 shard_map.150
  110.1 26.9 %all_to_all.21.refs_0_ = bf16[64,48,128]{2,1,0:T(8,128)(2,1)S(1)} all-to-all(bf16[64,48,128]{2,1,0:T(8,128)(2,1)S(1)} %shard_map.150), channel_id=1, replica_groups=mesh['ctx'=64,'ch'=8] {'ctx'}, dimensions={0} | all-to-all | bytes 1572864 | tf_op jit(solution)/shard_map/all_to_all | solution.py:304
  136.9 0.1 shard_map.151.refs_3_.refs_0_
  137.0 4.8 %collective-permute-start = (bf16[528,256]{1,0:T(8,128)(2,1)S(1)}, bf16[528,256]{1,0:T(8,128)(2,1)S(1)}, u32[]{:S(2)}, u32[]{:S(2)}) collective-permute-start(bf16[528,256]{1,0:T(8,128)(2,1)S(1)} %shard_map.151.refs_3_.refs_0_), channel_id=1, source_target_pairs={{0,1},{1,0},{2,3},{3,2},{4,5},{5,4},{6,7},{7,6},{8,9},{9,8},{10,11... | collective-permute-start | bytes 811016 | tf_op jit(solution)/shard_map/ppermute | solution.py:306
  141.8 1.4 shard_map.153
  143.3 1.6 %shard_map.154 = (f32[512,512]{1,0:T(8,128)}, f32[64,64]{1,0:T(8,128)}) custom-call(bf16[528,256]{1,0:T(8,128)(2,1)S(1)} %shard_map.151.refs_3_.refs_0_, bf16[528,256]{1,0:T(8,128)(2,1)S(1)} %collective-permute-done.refs_1_, s32[4]{0:T(128)S(1)} %pad_add_fusion.refs_12_.refs_3_.refs_2_), custom_call_target="tpu_custom_call" | custom-call | tf_op jit(solution)/shard_map/pallas_call | solution.py:51
  144.9 1.3 copy-done.3
  146.2 1.0 shard_map.152
  (18 shorter events, 0.0 us)
Async XLA Ops:
  7.2 17.3 %copy-start.10 = (f32[160]{0:T(256)S(1)}, f32[160]{0:T(256)}, u32[]{:S(2)}) copy-start(f32[160]{0:T(256)} %param.14) | copy-start | bytes 1924
  7.2 17.3 %copy-start.9 = (f32[160]{0:T(256)S(1)}, f32[160]{0:T(256)}, u32[]{:S(2)}) copy-start(f32[160]{0:T(256)} %param.13) | copy-start | bytes 1924
  7.2 17.3 %copy-start.8 = (bf16[64,64]{1,0:T(8,128)(2,1)S(1)}, bf16[64,64]{1,0:T(8,128)(2,1)}, u32[]{:S(2)}) copy-start(bf16[64,64]{1,0:T(8,128)(2,1)} %refs_2_.3) | copy-start | bytes 24580
  7.2 46.9 %all-gather.6.cloned.1.call-start = ((), (), s32[]{:S(2)}) async-start(), calls=%async_computation.4 | async-start | bytes 1622016 | tf_op jit(solution)/shard_map/all_gather | solution.py:275
  9.6 43.8 %copy-start = (bf16[512,512]{1,0:T(8,128)(2,1)S(1)}, bf16[512,512]{1,0:T(8,128)(2,1)}, u32[]{:S(2)}) copy-start(bf16[512,512]{1,0:T(8,128)(2,1)} %refs_1_.3) | copy-start | bytes 1572868
  9.6 43.7 %copy-start.1 = (bf16[160,512]{1,0:T(8,128)(2,1)S(1)}, bf16[160,512]{1,0:T(8,128)(2,1)}, u32[]{:S(2)}) copy-start(bf16[160,512]{1,0:T(8,128)(2,1)} %refs_2_.5) | copy-start | bytes 491524
  9.6 43.7 %copy-start.5 = (bf16[1,160,160]{2,1,0:T(8,128)(2,1)S(1)}, bf16[1,160,160]{2,1,0:T(8,128)(2,1)}, u32[]{:S(2)}) copy-start(bf16[1,160,160]{2,1,0:T(8,128)(2,1)} %refs_4_.1) | copy-start | bytes 153604
  11.5 24.1 %all-to-all-start = ((bf16[64,8,256]{2,1,0:T(8,128)(2,1)}), bf16[64,8,256]{2,1,0:T(8,128)(2,1)S(1)}, u32[]{:S(2)}, u32[]{:S(2)}) async-start(bf16[64,8,256]{2,1,0:T(8,128)(2,1)} %shard_map.145), calls=%async_computation | async-start | bytes 524288 | tf_op jit(solution)/shard_map/all_to_all | solution.py:274
  24.4 29.6 %copy-start.4 = (bf16[160,512]{1,0:T(8,128)(2,1)S(1)}, bf16[160,512]{1,0:T(8,128)(2,1)}, u32[]{:S(2)}) copy-start(bf16[160,512]{1,0:T(8,128)(2,1)} %refs_10_.1) | copy-start | bytes 491524
  36.6 16.8 %all-to-all-start.1 = ((bf16[64,8,256]{2,1,0:T(8,128)(2,1)}), bf16[64,8,256]{2,1,0:T(8,128)(2,1)S(1)}, u32[]{:S(2)}, u32[]{:S(2)}) async-start(bf16[64,8,256]{2,1,0:T(8,128)(2,1)} %shard_map.146), calls=%async_computation.1 | async-start | bytes 524288 | tf_op jit(solution)/shard_map/all_to_all | solution.py:283
  42.8 102.1 %all-gather.8.cloned.1.call-start = ((), (), s32[]{:S(2)}) async-start(), calls=%async_computation.5 | async-start | bytes 1474560 | tf_op jit(solution)/shard_map/all_gather | solution.py:300
  54.1 1.4 copy-start.2
  57.4 34.1 %copy-start.6 = (f32[160,128]{1,0:T(8,128)}, f32[160,128]{1,0:T(8,128)S(1)}, u32[]{:S(2)}) copy-start(f32[160,128]{1,0:T(8,128)S(1)} %get-tuple-element.39.refs_1_) | copy-start | bytes 245764
  136.9 8.0 %copy-start.7 = (f32[160,128]{1,0:T(8,128)S(1)}, f32[160,128]{1,0:T(8,128)}, u32[]{:S(2)}) copy-start(f32[160,128]{1,0:T(8,128)} %copy-done.6) | copy-start | bytes 245764
  137.0 6.2 %collective-permute-start = (bf16[528,256]{1,0:T(8,128)(2,1)S(1)}, bf16[528,256]{1,0:T(8,128)(2,1)S(1)}, u32[]{:S(2)}, u32[]{:S(2)}) collective-permute-start(bf16[528,256]{1,0:T(8,128)(2,1)S(1)} %shard_map.151.refs_3_.refs_0_), channel_id=1, source_target_pairs={{0,1},{1,0},{2,3},{3,2},{4,5},{5,4},{6,7},{7,6},{8,9},{9,8},{10,11... | collective-permute-start | bytes 811016 | tf_op jit(solution)/shard_map/ppermute | solution.py:306
  144.9 1.3 copy-start.3
Sparse Core Ops, SparseCore 0:
  10.2 43.2 all-gather.5
  91.7 33.9 all-gather.7

commit v7 on v5

--- a/solution.py
+++ b/solution.py
@@ -214,10 +214,14 @@
     out_ref[BLK:BLK + 16, :] = jnp.concatenate([cross, cross], axis=1).astype(BF)
 
 
-def finish_output(hidden_ref, factor_ref, acts_ref, out_ref):
+def finish_output(hidden_ref, factor_ref, far_ref, out_ref, acts_ref, sems):
+    copies = [pltpu.make_async_copy(far_ref.at[g], acts_ref.at[g], sems.at[g]) for g in range(CB)]
+    for copy in copies:
+        copy.start()
     factor = factor_ref[...]
     branch = jnp.zeros((CS, BLK), F32)
     for g in range(CB):
+        copies[g].wait()
         branch = branch + factor[:, g:g + 1] * acts_ref[g].astype(F32)
     out_ref[...] = (hidden_ref[...].astype(F32) + branch.astype(BF).astype(F32)).astype(BF)
 
@@ -303,7 +307,11 @@
         recv, rest, flag,
         smem=(2,),
     )
-    (output,) = call(finish_output, [((CS, BLK), BF)], hidden, factor, acts, after=[half])
+    (output,) = call(
+        finish_output, [((CS, BLK), BF)], hidden, factor, acts,
+        scratch=[pltpu.VMEM((CB, CS, BLK), BF), pltpu.SemaphoreType.DMA((CB,))],
+        far=(2,), vmem=60, after=[half],
+    )
     grad_block, grad_cross = call(
         finish_sums, [((BLK, BLK), F32), ((NB, NB), F32)], half, swapped, flag, smem=(2,)
     )

time: 153 us -> 154 us (level)
  Pallas kernels: 13.3 us -> 15.8 us
  waiting for transfers between devices: 20.5 us -> 22.3 us
  blocking collectives: 75.2 us -> 73.4 us
    pallas_call x11, Pallas kernels: 13.3 us -> 15.8 us  [call(): pl.pallas_call(run, out_shape=[jax.ShapeDtypeStruct(s, d) for s, d in out...]
    all_gather x1, waiting for transfers between devices: 1.69 us -> 3.53 us  [on_device(): cots = lax.all_gather(packed, 'ch')]
    all_to_all x2, blocking collectives: 57.7 us -> 55.9 us  [on_device(): recv = swap(send, 'ctx')]
where the time goes in v7:
time: 154 us; the launch traced here: 153 us
  blocking collectives  73.4 us (48%)
  starting transfers between devices  24 us (16%)
  waiting for transfers between devices  22.3 us (14%)
  Pallas kernels  15.8 us (10%)
  between operations  14.2 us (9%)
  local copies, waits for them, and re-layouts  3.5 us (2%)
    all_to_all x2, blocking collectives, on_device(): recv = swap(send, 'ctx')  55.9 us
    all_gather x1, blocking collectives, on_device(): lax.all_gather(send, 'ch')  17.5 us
    pallas_call x11, Pallas kernels, call(): pl.pallas_call(run, out_shape=[jax.ShapeDtypeStruct(s, d) for s, d in out...  15.8 us
    all_to_all x1, starting transfers between devices, on_device(): x_cols = swap(xt, 'ctx')  12.9 us
    all_to_all x1, waiting for transfers between devices, on_device(): u = swap(u_cols, 'ctx')  10.4 us
    all_to_all x1, waiting for transfers between devices, on_device(): x_cols = swap(xt, 'ctx')  8.33 us
    all_to_all x1, starting transfers between devices, on_device(): u = swap(u_cols, 'ctx')  6.19 us
    ppermute x1, starting transfers between devices, on_device(): swapped = lax.ppermute(half, 'ch', PAIR)  4.79 us
  transfers between devices with their start and end apart: 5, of which 3 were waited for; matrix products, arithmetic and copies ran while one was open for 0% of the time, Pallas kernels for 4%

profile of v7, /device:TPU:1, one launch (start us, length us, event | category | flops | bytes accessed | tf_op | source)
XLA Modules:
  0.0 153.2 jit_solution(11628332371462943830)
XLA Ops:
  7.2 0.0 all-gather.6.cloned.1.call-start
  7.2 2.6 %shard_map.144 = (bf16[64,8,256]{2,1,0:T(8,128)(2,1)}, bf16[176,512]{1,0:T(8,128)(2,1)}) custom-call(bf16[160,512]{1,0:T(8,128)(2,1)} %refs_2_.5, bf16[160,512]{1,0:T(8,128)(2,1)} %refs_10_.1, bf16[64,20]{1,0:T(8,128)(2,1)} %bitcast.22), custom_call_target="tpu_custom_call" | custom-call | tf_op jit(solution)/shard_map/pallas_call | solution.py:51
  9.9 0.0 all-gather.6.cloned.1.call-update
  9.9 12.9 %all-to-all-start = ((bf16[64,8,256]{2,1,0:T(8,128)(2,1)}), bf16[64,8,256]{2,1,0:T(8,128)(2,1)S(1)}, u32[]{:S(2)}, u32[]{:S(2)}) async-start(bf16[64,8,256]{2,1,0:T(8,128)(2,1)} %get-tuple-element.34), calls=%async_computation | async-start | bytes 524288 | tf_op jit(solution)/shard_map/all_to_all | solution.py:271
  22.9 0.0 copy-start.4
  22.9 0.0 copy-start.8
  22.9 0.7 copy-done.8
  23.6 0.7 copy-done.9
  24.3 0.7 copy-done.10
  25.0 0.7 shard_map.143
  25.7 8.3 %all-to-all-done.refs_1_ = bf16[64,8,256]{2,1,0:T(8,128)(2,1)S(1)} async-done(((bf16[64,8,256]{2,1,0:T(8,128)(2,1)}), bf16[64,8,256]{2,1,0:T(8,128)(2,1)S(1)}, u32[]{:S(2)}, u32[]{:S(2)}) %all-to-all-start) | async-done | bytes 262176 | tf_op jit(solution)/shard_map/all_to_all | solution.py:271
  34.0 1.0 shard_map.145
  35.0 6.2 %all-to-all-start.1 = ((bf16[64,8,256]{2,1,0:T(8,128)(2,1)}), bf16[64,8,256]{2,1,0:T(8,128)(2,1)S(1)}, u32[]{:S(2)}, u32[]{:S(2)}) async-start(bf16[64,8,256]{2,1,0:T(8,128)(2,1)} %shard_map.145), calls=%async_computation.1 | async-start | bytes 524288 | tf_op jit(solution)/shard_map/all_to_all | solution.py:280
  41.2 0.0 all-gather.8.cloned.1.call-start
  41.3 0.1 pad_add_fusion.refs_12_.refs_3_.refs_2_
  41.4 10.4 %all-to-all-done.1.refs_0_ = bf16[64,8,256]{2,1,0:T(8,128)(2,1)S(1)} async-done(((bf16[64,8,256]{2,1,0:T(8,128)(2,1)}), bf16[64,8,256]{2,1,0:T(8,128)(2,1)S(1)}, u32[]{:S(2)}, u32[]{:S(2)}) %all-to-all-start.1) | async-done | bytes 262176 | tf_op jit(solution)/shard_map/all_to_all | solution.py:280
  51.8 0.7 shard_map.146
  52.5 3.5 %all-gather.6.cloned.1.call-done = bf16[1408,512]{1,0:T(8,128)(2,1)} async-done(((bf16[176,512]{1,0:T(8,128)(2,1)}), bf16[1408,512]{1,0:T(8,128)(2,1)}) %all-gather.6.cloned.1.call-update) | async-done | bytes 1441808 | tf_op jit(solution)/shard_map/all_gather | solution.py:272
  56.0 1.4 copy-done.3
  57.4 2.0 %shard_map.147 = (bf16[64,48,128]{2,1,0:T(8,128)(2,1)S(1)}, f32[160,512]{1,0:T(8,128)S(1)}, f32[160,128]{1,0:T(8,128)S(1)}) custom-call(bf16[64,8,256]{2,1,0:T(8,128)(2,1)S(1)} %all-to-all-done.1.refs_0_, bf16[512,512]{1,0:T(8,128)(2,1)S(1)} %copy-done.1, bf16[160,512]{1,0:T(8,128)(2,1)S(1)} %copy-done.2, f32[160,128]{1,0:T(8,128)S(1)} %get-tuple-element.35.refs_3_, ...), custom_call_target="tpu_custom_call" | custom-call | tf_op jit(solution)/shard_map/pallas_call | solution.py:51
  59.4 29.1 %all_to_all.20.refs_0_ = bf16[64,48,128]{2,1,0:T(8,128)(2,1)S(1)} all-to-all(bf16[64,48,128]{2,1,0:T(8,128)(2,1)S(1)} %get-tuple-element.44), channel_id=1, replica_groups=mesh['ctx'=64,'ch'=8] {'ctx'}, dimensions={0} | all-to-all | bytes 1572864 | tf_op jit(solution)/shard_map/all_to_all | solution.py:291
  88.5 1.6 %shard_map.148 = (f32[72,128]{1,0:T(8,128)S(1)}, bf16[512,256]{1,0:T(8,128)(2,1)S(1)}, f32[8,128]{1,0:T(8,128)S(1)}, bf16[160,512]{1,0:T(8,128)(2,1)}) custom-call(bf16[64,48,128]{2,1,0:T(8,128)(2,1)S(1)} %all_to_all.20.refs_0_, bf16[64,8,256]{2,1,0:T(8,128)(2,1)S(1)} %all-to-all-done.refs_1_, bf16[512,512]{1,0:T(8,128)(2,1)S(1)} %get-tuple-element.45.refs_2_, ...), custom_call_target="tpu_custom_call" | custom-call | tf_op jit(solution)/shard_map/pallas_call | solution.py:51
  90.0 0.0 all-gather.8.cloned.1.call-update
  90.1 17.5 %all-gather.2 = f32[576,128]{1,0:T(8,128)S(1)} all-gather(f32[72,128]{1,0:T(8,128)S(1)} %get-tuple-element.47), channel_id=4, replica_groups=mesh['ctx'=64,'ch'=8] {'ch'}, dimensions={0}, use_global_device_ids=true | all-gather | bytes 331776 | tf_op jit(solution)/shard_map/all_gather | solution.py:299
  107.5 0.6 shard_map.149
  108.1 26.8 %all_to_all.21.refs_0_ = bf16[64,48,128]{2,1,0:T(8,128)(2,1)S(1)} all-to-all(bf16[64,48,128]{2,1,0:T(8,128)(2,1)S(1)} %shard_map.149), channel_id=1, replica_groups=mesh['ctx'=64,'ch'=8] {'ctx'}, dimensions={0} | all-to-all | bytes 1572864 | tf_op jit(solution)/shard_map/all_to_all | solution.py:301
  135.0 0.1 shard_map.150.refs_3_.refs_0_
  135.1 4.8 %collective-permute-start = (bf16[528,256]{1,0:T(8,128)(2,1)S(1)}, bf16[528,256]{1,0:T(8,128)(2,1)S(1)}, u32[]{:S(2)}, u32[]{:S(2)}) collective-permute-start(bf16[528,256]{1,0:T(8,128)(2,1)S(1)} %shard_map.150.refs_3_.refs_0_), channel_id=1, source_target_pairs={{0,1},{1,0},{2,3},{3,2},{4,5},{5,4},{6,7},{7,6},{8,9},{9,8},{10,11... | collective-permute-start | bytes 811016 | tf_op jit(solution)/shard_map/ppermute | solution.py:303
  139.9 1.4 shard_map.152
  141.3 0.0 collective-permute-done.refs_1_
  141.3 1.6 %shard_map.153 = (f32[512,512]{1,0:T(8,128)}, f32[64,64]{1,0:T(8,128)}) custom-call(bf16[528,256]{1,0:T(8,128)(2,1)S(1)} %shard_map.150.refs_3_.refs_0_, bf16[528,256]{1,0:T(8,128)(2,1)S(1)} %collective-permute-done.refs_1_, s32[4]{0:T(128)S(1)} %pad_add_fusion.refs_12_.refs_3_.refs_2_), custom_call_target="tpu_custom_call" | custom-call | tf_op jit(solution)/shard_map/pallas_call | solution.py:51
  143.0 3.4 %shard_map.151 = bf16[160,512]{1,0:T(8,128)(2,1)} custom-call(bf16[160,512]{1,0:T(8,128)(2,1)} %copy-done.5, f32[160,128]{1,0:T(8,128)} %copy-done.7, bf16[8,160,512]{2,1,0:T(8,128)(2,1)} %bitcast.21, bf16[528,256]{1,0:T(8,128)(2,1)} %copy-done), custom_call_target="tpu_custom_call" | custom-call | tf_op jit(solution)/shard_map/pallas_call | solution.py:51
  (17 shorter events, 0.0 us)
Async XLA Ops:
  7.2 44.6 %copy-start.2 = (bf16[160,512]{1,0:T(8,128)(2,1)S(1)}, bf16[160,512]{1,0:T(8,128)(2,1)}, u32[]{:S(2)}) copy-start(bf16[160,512]{1,0:T(8,128)(2,1)} %refs_2_.5) | copy-start | bytes 491524
  7.2 44.6 %copy-start.6 = (bf16[1,160,160]{2,1,0:T(8,128)(2,1)S(1)}, bf16[1,160,160]{2,1,0:T(8,128)(2,1)}, u32[]{:S(2)}) copy-start(bf16[1,160,160]{2,1,0:T(8,128)(2,1)} %refs_4_.1) | copy-start | bytes 153604
  7.2 44.6 %copy-start.1 = (bf16[512,512]{1,0:T(8,128)(2,1)S(1)}, bf16[512,512]{1,0:T(8,128)(2,1)}, u32[]{:S(2)}) copy-start(bf16[512,512]{1,0:T(8,128)(2,1)} %refs_1_.5) | copy-start | bytes 1572868
  7.2 48.8 %all-gather.6.cloned.1.call-start = ((), (), s32[]{:S(2)}) async-start(), calls=%async_computation.4 | async-start | bytes 1622016 | tf_op jit(solution)/shard_map/all_gather | solution.py:272
  9.9 24.1 %all-to-all-start = ((bf16[64,8,256]{2,1,0:T(8,128)(2,1)}), bf16[64,8,256]{2,1,0:T(8,128)(2,1)S(1)}, u32[]{:S(2)}, u32[]{:S(2)}) async-start(bf16[64,8,256]{2,1,0:T(8,128)(2,1)} %get-tuple-element.34), calls=%async_computation | async-start | bytes 524288 | tf_op jit(solution)/shard_map/all_to_all | solution.py:271
  22.9 33.1 %copy-start.4 = (bf16[160,512]{1,0:T(8,128)(2,1)S(1)}, bf16[160,512]{1,0:T(8,128)(2,1)}, u32[]{:S(2)}) copy-start(bf16[160,512]{1,0:T(8,128)(2,1)} %refs_10_.1) | copy-start | bytes 491524
  22.9 0.8 copy-start.8
  23.6 0.7 copy-start.9
  24.3 0.7 copy-start.10
  35.0 16.8 %all-to-all-start.1 = ((bf16[64,8,256]{2,1,0:T(8,128)(2,1)}), bf16[64,8,256]{2,1,0:T(8,128)(2,1)S(1)}, u32[]{:S(2)}, u32[]{:S(2)}) async-start(bf16[64,8,256]{2,1,0:T(8,128)(2,1)} %shard_map.145), calls=%async_computation.1 | async-start | bytes 524288 | tf_op jit(solution)/shard_map/all_to_all | solution.py:280
  41.2 101.7 %all-gather.8.cloned.1.call-start = ((), (), s32[]{:S(2)}) async-start(), calls=%async_computation.5 | async-start | bytes 1474560 | tf_op jit(solution)/shard_map/all_gather | solution.py:297
  52.5 6.9 %copy-start.5 = (bf16[160,512]{1,0:T(8,128)(2,1)}, bf16[160,512]{1,0:T(8,128)(2,1)S(1)}, u32[]{:S(2)}) copy-start(bf16[160,512]{1,0:T(8,128)(2,1)S(1)} %get-tuple-element.37.refs_7_.refs_0_) | copy-start | bytes 491524
  56.0 1.4 copy-start.3
  59.4 30.7 %copy-start.7 = (f32[160,128]{1,0:T(8,128)}, f32[160,128]{1,0:T(8,128)S(1)}, u32[]{:S(2)}) copy-start(f32[160,128]{1,0:T(8,128)S(1)} %get-tuple-element.43.refs_1_) | copy-start | bytes 245764
  135.1 7.9 %copy-start = (bf16[528,256]{1,0:T(8,128)(2,1)}, bf16[528,256]{1,0:T(8,128)(2,1)S(1)}, u32[]{:S(2)}) copy-start(bf16[528,256]{1,0:T(8,128)(2,1)S(1)} %shard_map.150.refs_3_.refs_0_) | copy-start | bytes 811012
  135.1 6.2 %collective-permute-start = (bf16[528,256]{1,0:T(8,128)(2,1)S(1)}, bf16[528,256]{1,0:T(8,128)(2,1)S(1)}, u32[]{:S(2)}, u32[]{:S(2)}) collective-permute-start(bf16[528,256]{1,0:T(8,128)(2,1)S(1)} %shard_map.150.refs_3_.refs_0_), channel_id=1, source_target_pairs={{0,1},{1,0},{2,3},{3,2},{4,5},{5,4},{6,7},{7,6},{8,9},{9,8},{10,11... | collective-permute-start | bytes 811016 | tf_op jit(solution)/shard_map/ppermute | solution.py:303
Sparse Core Ops, SparseCore 0:
  10.2 45.7 all-gather.5
  90.2 32.0 all-gather.7
